TPU v7x, 128 devices: a whole 4x4x4 slice. The times are simulated.
128 devices in a mesh: gx: 4 (over z), gy: 32 (over x, y, core).
Axes of the slice: x: 4, y: 4, z: 4, core: 2. Of those that a mesh axis runs over, the one named last changes fastest.
Arguments:
- solid_temp: float32 [128, 1024, 1024], P('gx', 'gy'), may hold values from -6 to 6
- conduct: float32 [128, 1024, 1024], P('gx', 'gy'), may hold values from 0.5 to 4
- power: float32 [128, 1024, 1024], P('gx', 'gy'), may hold values from -6 to 6
- channel_owner: int32 [16384], replicated, may hold values from 0 to 127, as said below
- wall_rows: int32 [524288], P(('gx', 'gy')), may hold values from 0 to 8191, as said below
- span_prop: float32 [2048, 128, 128], P(('gx', 'gy')), as said below
- span_carry: float32 [2048, 128], P(('gx', 'gy')), may hold values from 0.8 to 1
- channel_coef: float32 [32768], P(('gx', 'gy')), may hold values from 0.2 to 2
- channel_inlet: float32 [32768], P(('gx', 'gy')), may hold values from -1 to 1
Outputs:
- solid_out: float32 [128, 1024, 1024], P('gx', 'gy')
- fluid_temp: float32 [32768, 2048], P(('gx', 'gy'))
Inputs may be any that keep to these rules, and one draw needn't show every extreme that they name: `channel_owner`: some device owns exactly 256 channels and none more. `wall_rows`: the 4096 entries of one device are distinct rows of that device. `span_prop`: entries [i, j] with i > j are zero.
All inputs are finite; a program needn't handle non-finite values.
Results may differ from a plain program's by a relative error of at most 0.0003.
Values sent between devices are 32-bit elements; how exact they have to be, the bound alone decides.
No kernel may reach another device: no remote copies, remote signals or barrier semaphores. Data moves between devices by JAX's collectives and lax.ppermute only.
A program may use at most 128 MiB of HBM per device.

v0:
```python
import jax
import jax.numpy as jnp
from jax import lax
from jax.sharding import PartitionSpec as P

SWEEPS = 2


def padded(cells, sides, width):
    for axis, dim in sides:
        count = lax.axis_size(axis)
        ends = count - 1
        head = lax.slice_in_dim(cells, 0, width, axis=dim)
        tail = lax.slice_in_dim(cells, cells.shape[dim] - width, cells.shape[dim], axis=dim)
        cells = jnp.concatenate(
            [
                lax.ppermute(tail, axis, [(i, (i + 1) % count) for i in range(ends)]),
                cells,
                lax.ppermute(head, axis, [((i + 1) % count, i) for i in range(ends)]),
            ],
            axis=dim,
        )
    return cells


def relax(temp_pad, cond_pad, heat):
    centre = cond_pad[1:-1, 1:-1]
    inner = temp_pad[1:-1, 1:-1]
    numer = heat
    denom = jnp.zeros_like(heat)
    sides = (
        (cond_pad[2:, 1:-1], temp_pad[2:, 1:-1]),
        (cond_pad[:-2, 1:-1], temp_pad[:-2, 1:-1]),
        (cond_pad[1:-1, 2:], temp_pad[1:-1, 2:]),
        (cond_pad[1:-1, :-2], temp_pad[1:-1, :-2]),
    )
    cond_z = jnp.pad(centre, ((0, 0), (0, 0), (1, 1)))
    temp_z = jnp.pad(inner, ((0, 0), (0, 0), (1, 1)))
    sides = sides + ((cond_z[:, :, 2:], temp_z[:, :, 2:]), (cond_z[:, :, :-2], temp_z[:, :, :-2]))
    for cond_side, temp_side in sides:
        face = 0.5 * (centre + cond_side)
        numer = numer + face * temp_side
        denom = denom + face
    denom = denom + jnp.where(centre > 0.0, 0.0, 1.0)
    return jnp.where(centre > 0.0, numer / denom, 0.0)


def local(
    solid_temp,
    conduct,
    power,
    channel_owner,
    wall_rows,
    span_prop,
    span_carry,
    channel_coef,
    channel_inlet,
):
    devices = lax.axis_size(("gx", "gy"))
    me = lax.axis_index(("gx", "gy"))
    size_x, size_y, size_z = solid_temp.shape
    spans, block = span_carry.shape
    slots = channel_coef.shape[0]
    capacity = wall_rows.shape[0] // devices
    walls = solid_temp.reshape(-1, block)
    sent = jnp.take(walls, wall_rows, axis=0).reshape(devices, capacity, block)
    arrived = lax.all_to_all(sent, ("gx", "gy"), split_axis=0, concat_axis=0, tiled=True)
    cond_pad = padded(conduct, (("gx", 0), ("gy", 1)), 1)
    swept = solid_temp
    for sweep in range(SWEEPS):
        temp_pad = padded(swept, (("gx", 0), ("gy", 1)), 1)
        swept = relax(temp_pad, cond_pad, power)
    owned = jnp.sum((channel_owner == me).astype(jnp.int32))
    ticket = jnp.arange(slots * spans, dtype=jnp.int32)
    place = (me + ticket) % devices * capacity + ticket // devices
    channel_wall = jnp.take(arrived.reshape(-1, block), place, axis=0).reshape(slots, spans, block)
    live = (jnp.arange(slots, dtype=jnp.int32) < owned)[:, None, None]
    coef = channel_coef[:, None]

    def advance(prev, pieces):
        wall_block, prop, carry = pieces
        fresh = jnp.dot(
            coef * wall_block,
            prop,
            precision=lax.Precision.HIGHEST,
            preferred_element_type=jnp.float32,
        )
        fresh = fresh + carry[None, :] * prev[:, None]
        return (fresh[:, -1], fresh)

    last, fluid = lax.scan(
        advance, channel_inlet, (jnp.swapaxes(channel_wall, 0, 1), span_prop, span_carry)
    )
    fluid = jnp.where(live, jnp.swapaxes(fluid, 0, 1), 0.0)
    flux = jnp.where(live, coef[:, :, None] * (channel_wall - fluid), 0.0)
    anchor = jnp.arange(devices, dtype=jnp.int32)[:, None]
    position = jnp.arange(capacity, dtype=jnp.int32)[None, :]
    back_ticket = position * devices + (anchor - me) % devices
    outgoing = jnp.take(flux.reshape(-1, block), back_ticket.reshape(-1), axis=0).reshape(
        devices, capacity, block
    )
    returned = lax.all_to_all(outgoing, ("gx", "gy"), split_axis=0, concat_axis=0, tiled=True)
    sink = jnp.zeros_like(walls).at[wall_rows].add(returned.reshape(-1, block))
    solid_out = swept - sink.reshape(size_x, size_y, size_z)
    fluid_temp = fluid.reshape(slots, spans * block)
    return (solid_out, fluid_temp)


def solution(mesh):
    placed = (
        P("gx", "gy", None),
        P("gx", "gy", None),
        P("gx", "gy", None),
        P(),
        P(("gx", "gy")),
        P(("gx", "gy"), None, None),
        P(("gx", "gy"), None),
        P(("gx", "gy")),
        P(("gx", "gy")),
    )
    return jax.shard_map(
        local,
        mesh=mesh,
        in_specs=placed,
        out_specs=(P("gx", "gy", None), P(("gx", "gy"), None)),
        check_vma=False,
    )
```

profile of v0, /device:TPU:102, one launch (start us, length us, event | category | flops | bytes accessed | tf_op | source)
XLA Modules:
  0.0 282.0 jit_solution(13313984660321261877)
XLA Ops:
  1.6 1.3 collective-permute-start.2
  2.9 4.6 %collective-permute-start = (f32[1,32,1024]{2,1,0:T(8,128)S(1)}, f32[1,32,1024]{2,1,0:T(8,128)S(1)}, u32[]{:S(2)}, u32[]{:S(2)}) collective-permute-start(f32[1,32,1024]{2,1,0:T(8,128)S(1)} %get-tuple-element.68), channel_id=1, source_target_pairs={{32,0},{64,32},{96,64},{33,1},{65,33},{97,65},{34,2},{66,34},{98,6... | collective-permute-start | bytes 393224 | tf_op jit(solution)/shard_map/ppermute | solution.py:19
  7.5 1.7 fusion.68
  9.2 1.3 collective-permute-start.3
  10.5 4.6 %collective-permute-start.1 = (f32[1,32,1024]{2,1,0:T(8,128)}, f32[1,32,1024]{2,1,0:T(8,128)S(1)}, u32[]{:S(2)}, u32[]{:S(2)}) collective-permute-start(f32[1,32,1024]{2,1,0:T(8,128)} %get-tuple-element.69), channel_id=1, source_target_pairs={{32,0},{64,32},{96,64},{33,1},{65,33},{97,65},{34,2},{66,34},{98,6... | collective-permute-start | bytes 393224 | tf_op jit(solution)/shard_map/ppermute | solution.py:19
  15.1 4.9 %reshape.90 = f32[8192,128]{1,0:T(8,128)} reshape(f32[32,32,1024]{2,1,0:T(8,128)} %param.13) | data formatting | bytes 8388608 | tf_op jit(solution)/shard_map/reshape | solution.py:65
  20.8 13.0 %gather_fusion = f32[4096,128]{1,0:T(8,128)S(1)} fusion(f32[8192,128]{1,0:T(8,128)} %reshape.90, s32[4096]{0:T(1024)S(1)} %get-tuple-element.71), kind=kCustom, calls=%fused_computation.2 | custom fusion | bytes 4210688 | tf_op jit(solution)/shard_map/jit(_take)/gather | solution.py:66
  33.8 2.4 broadcast_select_fusion.3
  36.2 9.8 %all-to-all-start = ((f32[128,32,128]{2,1,0:T(8,128)}), f32[128,32,128]{2,1,0:T(8,128)S(1)}, u32[]{:S(2)}, u32[]{:S(2)}) async-start(f32[128,32,128]{2,1,0:T(8,128)} %broadcast_select_fusion.3), calls=%async_computation | async-start | bytes 4194304 | tf_op jit(solution)/shard_map/all_to_all | solution.py:67
  46.8 2.7 constant_dynamic-update-slice_fusion.1
  49.8 4.8 %collective-permute-start.4 = (f32[34,1,1024]{2,0,1:T(8,128)S(1)}, f32[34,1,1024]{2,0,1:T(8,128)S(1)}, u32[]{:S(2)}, u32[]{:S(2)}) collective-permute-start(f32[34,1,1024]{2,0,1:T(8,128)S(1)} %copy.45), channel_id=1, source_target_pairs={{1,0},{2,1},{3,2},{4,3},{5,4},{6,5},{7,6},{8,7},{9,8},{10,9},{11,1... | collective-permute-start | bytes 417800 | tf_op jit(solution)/shard_map/ppermute | solution.py:19
  54.6 1.9 collective-permute-start.6
  57.2 2.1 copy-done.5
  60.2 5.7 %collective-permute-start.5 = (f32[34,1,1024]{2,0,1:T(8,128)}, f32[34,1,1024]{2,0,1:T(8,128)}, u32[]{:S(2)}, u32[]{:S(2)}) collective-permute-start(f32[34,1,1024]{2,0,1:T(8,128)} %copy.47), channel_id=1, source_target_pairs={{1,0},{2,1},{3,2},{4,3},{5,4},{6,5},{7,6},{8,7},{9,8},{10,9},{11,1... | collective-permute-start | bytes 417800 | tf_op jit(solution)/shard_map/ppermute | solution.py:19
  66.7 1.9 collective-permute-start.7
  70.4 3.8 %collective-permute-done.6 = f32[34,1,1024]{2,0,1:T(8,128)} collective-permute-done((f32[34,1,1024]{2,0,1:T(8,128)S(1)}, f32[34,1,1024]{2,0,1:T(8,128)}, u32[]{:S(2)}, u32[]{:S(2)}) %collective-permute-start.6) | collective-permute-done | bytes 139296 | tf_op jit(solution)/shard_map/ppermute | solution.py:17
  77.4 14.2 %gather_fusion.1 = f32[4096,128]{1,0:T(8,128)} fusion(f32[4096,128]{1,0:T(8,128)S(1)} %bitcast.46, s32[4096]{0:T(1024)S(1)} %broadcast_clamp_fusion), kind=kCustom, calls=%fused_computation.clone | custom fusion | bytes 4210688 | tf_op jit(solution)/shard_map/jit(_take)/gather | solution.py:76
  91.6 3.6 %broadcast_select_fusion.1 = f32[4096,128]{1,0:T(8,128)S(1)} fusion(f32[4096,128]{1,0:T(8,128)} %gather_fusion.1, pred[4096]{0:T(1024)(128)(4,1)S(1)} %compare_and_fusion.1), kind=kLoop, calls=%fused_computation.87 | loop fusion | flops 524288 | bytes 4198400 | tf_op jit(solution)/shard_map/jit(_take)/select_n | solution.py:76
  95.2 2.0 copy.63
  97.2 1.8 copy.58
  99.2 31.8 %while.12 = (s32[]{:T(128)}, f32[256]{0:T(256)S(1)}, f32[16,256,128]{1,2,0:T(8,128)S(1)}, f32[256,1]{0,1:T(1,128)S(1)}, f32[16,256,128]{2,1,0:T(8,128)}, /*index...) while((s32[]{:T(128)}, f32[256]{0:T(256)S(1)}, f32[16,256,128]{1,2,0:T(8,128)S(1)}, ...), condition=%wide.region_2.4_spmd, body=%wide.region_1.3_spmd.sunk | while | flops 50429952 | bytes 466009 | solution.py:91
  99.9 1.3 bitcast_dynamic-update-slice_fusion.2
  101.9 1.3 bitcast_dynamic-update-slice_fusion.2
  103.9 1.3 bitcast_dynamic-update-slice_fusion.2
  107.9 1.3 bitcast_dynamic-update-slice_fusion.2
  109.9 1.3 bitcast_dynamic-update-slice_fusion.2
  111.9 1.3 bitcast_dynamic-update-slice_fusion.2
  113.9 1.3 bitcast_dynamic-update-slice_fusion.2
  115.8 1.3 bitcast_dynamic-update-slice_fusion.2
  121.8 1.3 bitcast_dynamic-update-slice_fusion.2
  131.1 1.4 copy-done.3
  132.5 3.2 %fusion.50 = f32[256,16,128]{0,2,1:T(8,128)} fusion(f32[256,16,128]{0,2,1:T(8,128)} %copy.58, f32[256]{0:T(256)S(1)} %bitcast.55, pred[256]{0:T(512)(128)(4,1)S(1)} %iota_compare_fusion, f32[16,256,128]{1,2,0:T(8,128)S(1)} %get-tuple-element.40), kind=kLoop, calls=%fused_computation.81 | loop fusion | flops 2097152 | bytes 6292736 | tf_op jit(solution)/shard_map/jit(_where)/select_n | solution.py:95
  135.7 2.2 copy.59
  137.9 14.2 %gather_fusion.2 = f32[4096,128]{1,0:T(8,128)} fusion(f32[4096,128]{1,0:T(8,128)S(1)} %bitcast.47, s32[4096]{0:T(1024)S(1)} %get-tuple-element.73), kind=kCustom, calls=%fused_computation.1.clone | custom fusion | bytes 4210688 | tf_op jit(solution)/shard_map/jit(_take)/gather | solution.py:99
  152.1 4.7 %broadcast_select_fusion = f32[4096,128]{1,0:T(8,128)} fusion(f32[4096,128]{1,0:T(8,128)} %gather_fusion.2, pred[4096]{0:T(1024)(128)(4,1)S(1)} %compare_and_fusion), kind=kLoop, calls=%fused_computation.86 | loop fusion | flops 524288 | bytes 4198400 | tf_op jit(solution)/shard_map/jit(_take)/select_n | solution.py:99
  156.8 8.1 %all-to-all-start.1 = ((f32[128,32,128]{2,1,0:T(8,128)}), f32[128,32,128]{2,1,0:T(8,128)}, u32[]{:S(2)}, u32[]{:S(2)}) async-start(f32[128,32,128]{2,1,0:T(8,128)} %bitcast.13), calls=%async_computation.1 | async-start | bytes 4194304 | tf_op jit(solution)/shard_map/all_to_all | solution.py:102
  164.9 28.5 %fusion.16 = f32[32,32,1024]{2,1,0:T(8,128)S(1)} fusion(f32[32,32,1024]{2,1,0:T(8,128)} %param.13, f32[34,32,1024]{2,1,0:T(8,128)} %copy-done.5, f32[34,1,1024]{2,1,0:T(1,128)S(1)} %copy.52, f32[34,1,1024]{2,1,0:T(1,128)S(1)} %copy.48, f32[1,32,1024]{2,1,0:T(8,128)S(1)} %collective-permute-done.3, f32[32,32,1024]{2,1,0:T(8,128)} %param.15, ...), kind=kLoop, calls=%fused_computation.29 | loop fusion | flops 44040192 | bytes 26771456 | tf_op jit(solution)/shard_map/jit(_where)/select_n | solution.py:45
  193.5 2.8 collective-permute-start.8
  196.3 1.3 collective-permute-start.9
  197.6 1.9 collective-permute-done.8
  199.4 4.1 %collective-permute-done.9 = f32[1,32,1024]{2,1,0:T(8,128)S(1)} collective-permute-done((f32[1,32,1024]{2,1,0:T(8,128)S(1)}, f32[1,32,1024]{2,1,0:T(8,128)S(1)}, u32[]{:S(2)}, u32[]{:S(2)}) %collective-permute-start.9) | collective-permute-done | bytes 131104 | tf_op jit(solution)/shard_map/ppermute | solution.py:17
  203.8 3.8 %collective-permute-start.10 = (f32[34,1,1024]{2,0,1:T(8,128)S(1)}, f32[34,1,1024]{2,0,1:T(8,128)S(1)}, u32[]{:S(2)}, u32[]{:S(2)}) collective-permute-start(f32[34,1,1024]{2,0,1:T(8,128)S(1)} %copy.53), channel_id=1, source_target_pairs={{1,0},{2,1},{3,2},{4,3},{5,4},{6,5},{7,6},{8,7},{9,8},{10,9},{11,1... | collective-permute-start | bytes 417800 | tf_op jit(solution)/shard_map/ppermute | solution.py:19
  207.7 1.9 collective-permute-start.11
  210.6 5.8 %collective-permute-done.11 = f32[34,1,1024]{2,0,1:T(8,128)S(1)} collective-permute-done((f32[34,1,1024]{2,0,1:T(8,128)S(1)}, f32[34,1,1024]{2,0,1:T(8,128)S(1)}, u32[]{:S(2)}, u32[]{:S(2)}) %collective-permute-start.11) | collective-permute-done | bytes 139296 | tf_op jit(solution)/shard_map/ppermute | solution.py:17
  216.8 1.8 copy.61
  218.6 24.9 %scatter_custom_fusion = f32[8192,128]{1,0:T(8,128)} fusion(s32[4096]{0:T(1024)} %get-tuple-element.72, f32[4096,128]{1,0:T(8,128)} %bitcast.14, f32[]{:T(128)} %constant.86.clone.1), kind=kCustom, calls=%fused_computation.83 | custom fusion | flops 524288 | bytes 4194816 | tf_op jit(solution)/shard_map/scatter-add | solution.py:103
  243.5 5.0 %reshape.96 = f32[32,32,1024]{2,1,0:T(8,128)} reshape(f32[8192,128]{1,0:T(8,128)} %scatter_custom_fusion) | data formatting | bytes 8388608 | tf_op jit(solution)/shard_map/reshape | solution.py:104
  248.4 33.3 %fusion.23 = f32[32,32,1024]{2,1,0:T(8,128)} fusion(f32[32,32,1024]{2,1,0:T(8,128)} %reshape.96, f32[32,32,1024]{2,1,0:T(8,128)} %copy-done, f32[34,1,1024]{2,1,0:T(1,128)S(1)} %copy.56, f32[1,32,1024]{2,1,0:T(8,128)S(1)} %collective-permute-done.8, f32[1,32,1024]{2,1,0:T(8,128)S(1)} %collective-permute-done.9, f32[34,1,1024]{2,1,0:T(1,128)S(1)} %copy.54, ...), kind=kLoop, calls=%fused_computation.36 | loop fusion | flops 49283072 | bytes 26509312 | tf_op jit(solution)/shard_map/sub | solution.py:104
  (103 shorter events, 31.9 us)
Async XLA Ops:
  1.6 45.1 %collective-permute-start.2 = (f32[1,32,1024]{2,1,0:T(8,128)S(1)}, f32[1,32,1024]{2,1,0:T(8,128)S(1)}, u32[]{:S(2)}, u32[]{:S(2)}) collective-permute-start(f32[1,32,1024]{2,1,0:T(8,128)S(1)} %get-tuple-element.67), channel_id=1, source_target_pairs={{0,32},{32,64},{64,96},{1,33},{33,65},{65,97},{2,34},{34,66},{66,9... | collective-permute-start | bytes 393224 | tf_op jit(solution)/shard_map/ppermute | solution.py:17
  2.9 46.5 %collective-permute-start = (f32[1,32,1024]{2,1,0:T(8,128)S(1)}, f32[1,32,1024]{2,1,0:T(8,128)S(1)}, u32[]{:S(2)}, u32[]{:S(2)}) collective-permute-start(f32[1,32,1024]{2,1,0:T(8,128)S(1)} %get-tuple-element.68), channel_id=1, source_target_pairs={{32,0},{64,32},{96,64},{33,1},{65,33},{97,65},{34,2},{66,34},{98,6... | collective-permute-start | bytes 393224 | tf_op jit(solution)/shard_map/ppermute | solution.py:19
  9.2 47.4 %collective-permute-start.3 = (f32[1,32,1024]{2,1,0:T(8,128)}, f32[1,32,1024]{2,1,0:T(8,128)S(1)}, u32[]{:S(2)}, u32[]{:S(2)}) collective-permute-start(f32[1,32,1024]{2,1,0:T(8,128)} %get-tuple-element.70), channel_id=1, source_target_pairs={{0,32},{32,64},{64,96},{1,33},{33,65},{65,97},{2,34},{34,66},{66,9... | collective-permute-start | bytes 393224 | tf_op jit(solution)/shard_map/ppermute | solution.py:17
  10.5 46.7 %collective-permute-start.1 = (f32[1,32,1024]{2,1,0:T(8,128)}, f32[1,32,1024]{2,1,0:T(8,128)S(1)}, u32[]{:S(2)}, u32[]{:S(2)}) collective-permute-start(f32[1,32,1024]{2,1,0:T(8,128)} %get-tuple-element.69), channel_id=1, source_target_pairs={{32,0},{64,32},{96,64},{33,1},{65,33},{97,65},{34,2},{66,34},{98,6... | collective-permute-start | bytes 393224 | tf_op jit(solution)/shard_map/ppermute | solution.py:19
  15.0 5.1 %copy-start.6 = (s32[4096]{0:T(1024)S(1)}, s32[4096]{0:T(1024)}, u32[]{:S(2)}) copy-start(s32[4096]{0:T(1024)} %param.17) | copy-start | bytes 49156
  33.8 12.3 %copy-start.7 = (s32[16384]{0:T(1024)S(1)}, s32[16384]{0:T(1024)}, u32[]{:S(2)}) copy-start(s32[16384]{0:T(1024)} %param.16) | copy-start | bytes 196612
  36.2 41.2 %all-to-all-start = ((f32[128,32,128]{2,1,0:T(8,128)}), f32[128,32,128]{2,1,0:T(8,128)S(1)}, u32[]{:S(2)}, u32[]{:S(2)}) async-start(f32[128,32,128]{2,1,0:T(8,128)} %broadcast_select_fusion.3), calls=%async_computation | async-start | bytes 4194304 | tf_op jit(solution)/shard_map/all_to_all | solution.py:67
  46.8 9.8 %copy-start.1 = (f32[32,32,1024]{2,1,0:T(8,128)S(1)}, f32[32,32,1024]{2,1,0:T(8,128)}, u32[]{:S(2)}) copy-start(f32[32,32,1024]{2,1,0:T(8,128)} %param.13) | copy-start | bytes 12582916
  49.5 7.7 %copy-start.2 = (f32[34,32,1024]{2,1,0:T(8,128)}, f32[34,32,1024]{2,1,0:T(8,128)S(1)}, u32[]{:S(2)}) copy-start(f32[34,32,1024]{2,1,0:T(8,128)S(1)} %constant_dynamic-update-slice_fusion) | copy-start | bytes 13369348
  49.8 20.5 %collective-permute-start.4 = (f32[34,1,1024]{2,0,1:T(8,128)S(1)}, f32[34,1,1024]{2,0,1:T(8,128)S(1)}, u32[]{:S(2)}, u32[]{:S(2)}) collective-permute-start(f32[34,1,1024]{2,0,1:T(8,128)S(1)} %copy.45), channel_id=1, source_target_pairs={{1,0},{2,1},{3,2},{4,3},{5,4},{6,5},{7,6},{8,7},{9,8},{10,9},{11,1... | collective-permute-start | bytes 417800 | tf_op jit(solution)/shard_map/ppermute | solution.py:19
  54.6 19.6 %collective-permute-start.6 = (f32[34,1,1024]{2,0,1:T(8,128)S(1)}, f32[34,1,1024]{2,0,1:T(8,128)}, u32[]{:S(2)}, u32[]{:S(2)}) collective-permute-start(f32[34,1,1024]{2,0,1:T(8,128)S(1)} %copy.49), channel_id=1, source_target_pairs={{0,1},{1,2},{2,3},{3,4},{4,5},{5,6},{6,7},{7,8},{8,9},{9,10},{10,1... | collective-permute-start | bytes 417800 | tf_op jit(solution)/shard_map/ppermute | solution.py:17
  57.2 2.1 copy-start.5
  60.2 15.0 %collective-permute-start.5 = (f32[34,1,1024]{2,0,1:T(8,128)}, f32[34,1,1024]{2,0,1:T(8,128)}, u32[]{:S(2)}, u32[]{:S(2)}) collective-permute-start(f32[34,1,1024]{2,0,1:T(8,128)} %copy.47), channel_id=1, source_target_pairs={{1,0},{2,1},{3,2},{4,3},{5,4},{6,5},{7,6},{8,7},{9,8},{10,9},{11,1... | collective-permute-start | bytes 417800 | tf_op jit(solution)/shard_map/ppermute | solution.py:19
  66.7 9.7 %collective-permute-start.7 = (f32[34,1,1024]{2,0,1:T(8,128)}, f32[34,1,1024]{2,0,1:T(8,128)}, u32[]{:S(2)}, u32[]{:S(2)}) collective-permute-start(f32[34,1,1024]{2,0,1:T(8,128)} %copy.51), channel_id=1, source_target_pairs={{0,1},{1,2},{2,3},{3,4},{4,5},{5,6},{6,7},{7,8},{8,9},{9,10},{10,1... | collective-permute-start | bytes 417800 | tf_op jit(solution)/shard_map/ppermute | solution.py:17
  97.2 2.0 copy-start.8
  97.2 2.0 copy-start.9
  131.0 1.4 copy-start.3
  156.8 61.8 %all-to-all-start.1 = ((f32[128,32,128]{2,1,0:T(8,128)}), f32[128,32,128]{2,1,0:T(8,128)}, u32[]{:S(2)}, u32[]{:S(2)}) async-start(f32[128,32,128]{2,1,0:T(8,128)} %bitcast.13), calls=%async_computation.1 | async-start | bytes 4194304 | tf_op jit(solution)/shard_map/all_to_all | solution.py:102
  193.4 23.3 %copy-start = (f32[32,32,1024]{2,1,0:T(8,128)}, f32[32,32,1024]{2,1,0:T(8,128)S(1)}, u32[]{:S(2)}) copy-start(f32[32,32,1024]{2,1,0:T(8,128)S(1)} %fusion.16) | copy-start | bytes 12582916
  193.5 23.1 %copy-start.4 = (f32[16,256,128]{1,2,0:T(8,128)S(1)}, f32[16,256,128]{1,2,0:T(8,128)}, u32[]{:S(2)}) copy-start(f32[16,256,128]{1,2,0:T(8,128)} %copy-done.3) | copy-start | bytes 6291460
  193.5 5.9 %collective-permute-start.8 = (f32[1,32,1024]{2,1,0:T(8,128)S(1)}, f32[1,32,1024]{2,1,0:T(8,128)S(1)}, u32[]{:S(2)}, u32[]{:S(2)}) collective-permute-start(f32[1,32,1024]{2,1,0:T(8,128)S(1)} %get-tuple-element.66), channel_id=1, source_target_pairs={{32,0},{64,32},{96,64},{33,1},{65,33},{97,65},{34,2},{66,34},{98,6... | collective-permute-start | bytes 393224 | tf_op jit(solution)/shard_map/ppermute | solution.py:19
  196.3 7.3 %collective-permute-start.9 = (f32[1,32,1024]{2,1,0:T(8,128)S(1)}, f32[1,32,1024]{2,1,0:T(8,128)S(1)}, u32[]{:S(2)}, u32[]{:S(2)}) collective-permute-start(f32[1,32,1024]{2,1,0:T(8,128)S(1)} %get-tuple-element.65), channel_id=1, source_target_pairs={{0,32},{32,64},{64,96},{1,33},{33,65},{65,97},{2,34},{34,66},{66,9... | collective-permute-start | bytes 393224 | tf_op jit(solution)/shard_map/ppermute | solution.py:17
  203.8 6.6 %collective-permute-start.10 = (f32[34,1,1024]{2,0,1:T(8,128)S(1)}, f32[34,1,1024]{2,0,1:T(8,128)S(1)}, u32[]{:S(2)}, u32[]{:S(2)}) collective-permute-start(f32[34,1,1024]{2,0,1:T(8,128)S(1)} %copy.53), channel_id=1, source_target_pairs={{1,0},{2,1},{3,2},{4,3},{5,4},{6,5},{7,6},{8,7},{9,8},{10,9},{11,1... | collective-permute-start | bytes 417800 | tf_op jit(solution)/shard_map/ppermute | solution.py:19
  207.7 8.7 %collective-permute-start.11 = (f32[34,1,1024]{2,0,1:T(8,128)S(1)}, f32[34,1,1024]{2,0,1:T(8,128)S(1)}, u32[]{:S(2)}, u32[]{:S(2)}) collective-permute-start(f32[34,1,1024]{2,0,1:T(8,128)S(1)} %copy.55), channel_id=1, source_target_pairs={{0,1},{1,2},{2,3},{3,4},{4,5},{5,6},{6,7},{7,8},{8,9},{9,10},{10,1... | collective-permute-start | bytes 417800 | tf_op jit(solution)/shard_map/ppermute | solution.py:17
where the time goes:
time: 284 us; the launch traced here: 282 us
  other arithmetic  103 us (36%)
  local copies, waits for them, and re-layouts  85.7 us (30%)
  starting transfers between devices  53.7 us (19%)
  matrix products  20.1 us (7%)
  waiting for transfers between devices  17.5 us (6%)
    sub x1, other arithmetic, local(): solid_out = swept - sink.reshape(size_x, size_y, size_z)  33.3 us
    select_n x1, other arithmetic, relax(): return jnp.where(centre > 0.0, numer / denom, 0.0)  28.5 us
    ppermute x6, starting transfers between devices, padded(): lax.ppermute(head, axis, [((i + 1) % count, i) for i in range(ends)])  26.2 us
    scatter-add x1, other arithmetic, local(): sink = jnp.zeros_like(walls).at[wall_rows].add(returned.reshape(-1, block))  24.9 us
    dot_general x16, matrix products, advance(): jnp.dot(coef * wall_block, prop, precision=lax.Precision.HIGHEST, preferr...  20.1 us
    gather x1, local copies, waits for them, and re-layouts, local(): jnp.take(arrived.reshape(-1, block), place, axis=0)  14.2 us
    gather x1, local copies, waits for them, and re-layouts, local(): jnp.take(flux.reshape(-1, block), back_ticket.reshape(-1), axis=0)  14.2 us
    ppermute x6, waiting for transfers between devices, padded(): lax.ppermute(tail, axis, [(i, (i + 1) % count) for i in range(ends)])  13.7 us
  transfers between devices with their start and end apart: 14, of which 6 were waited for; matrix products, arithmetic and copies ran while one was open for 23% of the time, Pallas kernels for 0%

commit v1 on v0

v1 whole, which is shorter than its diff:
```python
import functools
import jax
import jax.numpy as jnp
from jax import lax
from jax.experimental import pallas as pl
from jax.experimental.pallas import tpu as pltpu
from jax.sharding import PartitionSpec as P

VM = pl.BlockSpec(memory_space=pltpu.VMEM)
SM = pl.BlockSpec(memory_space=pltpu.SMEM)
LIMIT = 56 * 2**20


def tiles(a):
    x, y, z = a.shape
    return a.reshape(x, y // 8, 8, z // 128, 128).transpose(0, 1, 3, 2, 4).reshape(-1, 128)


def untiles(a, x, y, z):
    return a.reshape(x, y // 8, z // 128, 8, 128).transpose(0, 1, 3, 2, 4).reshape(x, y, z)


def gather_kernel(idx, src, out, *, unroll):
    def body(i, _):
        base = pl.multiple_of(i * unroll, unroll)
        at = [idx[base + n] for n in range(unroll)]
        rows = [src[pl.ds(t, 1), :] for t in at]
        for n in range(unroll):
            out[pl.ds(base + n, 1), :] = rows[n]
        return 0
    lax.fori_loop(0, out.shape[0] // unroll, body, 0)


def gather(idx, src, unroll=16):
    return pl.pallas_call(
        functools.partial(gather_kernel, unroll=unroll),
        out_shape=jax.ShapeDtypeStruct((idx.shape[0], 128), jnp.float32),
        in_specs=[SM, VM], out_specs=VM,
        compiler_params=pltpu.CompilerParams(vmem_limit_bytes=LIMIT), name="gather_rows",
    )(idx, src)


def scatter_kernel(idx, rows, src, out, *, unroll):
    out[...] = src[...]
    def body(i, _):
        base = pl.multiple_of(i * unroll, unroll)
        at = [idx[base + n] for n in range(unroll)]
        new = [out[pl.ds(t, 1), :] - rows[pl.ds(base + n, 1), :] for n, t in enumerate(at)]
        for t, v in zip(at, new):
            out[pl.ds(t, 1), :] = v
        return 0
    lax.fori_loop(0, rows.shape[0] // unroll, body, 0)


def scatter(idx, rows, src, unroll=16):
    return pl.pallas_call(
        functools.partial(scatter_kernel, unroll=unroll),
        out_shape=jax.ShapeDtypeStruct(src.shape, jnp.float32),
        in_specs=[SM, VM, VM], out_specs=VM,
        compiler_params=pltpu.CompilerParams(vmem_limit_bytes=LIMIT), name="scatter_rows",
    )(idx, rows, src)


def step_up(a, edge, corner, fill):
    rolled = pltpu.roll(a, 127, 1)
    carried = pltpu.roll(rolled, 7, 0)
    return jnp.where(edge, jnp.where(corner, fill, carried), rolled)


def step_down(a, edge, corner, fill):
    rolled = pltpu.roll(a, 1, 1)
    carried = pltpu.roll(rolled, 1, 0)
    return jnp.where(edge, jnp.where(corner, fill, carried), rolled)


def relax_loop(xs, ys, load_u, load_c, load_p, side_u, side_c, store):
    lane = lax.broadcasted_iota(jnp.int32, (8, 128), 1)
    sub = lax.broadcasted_iota(jnp.int32, (8, 128), 0)
    top, bottom = lane == 127, lane == 0
    last, first = sub == 7, sub == 0

    def body(x, _):
        line = lambda f, side, y: f(x, y) if 0 <= y < ys else side(x, 0 if y < 0 else 1)
        u_old, c_old = line(load_u, side_u, -1), line(load_c, side_c, -1)
        u, c = line(load_u, side_u, 0), line(load_c, side_c, 0)
        w_old, w = u_old * c_old, u * c
        for y in range(ys):
            u_new, c_new = line(load_u, side_u, y + 1), line(load_c, side_c, y + 1)
            w_new = u_new * c_new
            ul, uh = load_u(x - 1, y), load_u(x + 1, y)
            cl, ch = load_c(x - 1, y), load_c(x + 1, y)
            face = c + step_up(c, top, last, 0.0)
            flow = face * step_up(u, top, last, 0.0)
            back = step_down(face * u, bottom, first, 0.0)
            below = step_down(face, bottom, first, c)
            numer = c * ((u_old + u_new) + (ul + uh)) + ((w_old + w_new) + (cl * ul + ch * uh))
            numer = numer + (flow + back) + 2.0 * load_p(x, y)
            denom = 4.0 * c + ((c_old + c_new) + (cl + ch)) + (face + below)
            store(x, y, numer / denom)
            u_old, c_old, w_old = u, c, w
            u, c, w = u_new, c_new, w_new
        return 0

    lax.fori_loop(0, xs, body, 0)


def tile_line(ref, x, y, shift=0):
    return ref[pl.ds(pl.multiple_of((x + shift) * 256, 256) + (y // 8) * 64 + y % 8, 8, stride=8), :]


def sweep1_kernel(u, c, p, xlo, xhi, ylo, yhi, out, fx0, fx1, fy0, fy1, us, cs, ps, sems):
    rows = us.shape[0] - 512
    jobs = [(u, us.at[pl.ds(256, rows)]), (c, cs.at[pl.ds(256, rows)]), (p, ps),
            (xlo.at[pl.ds(0, 256)], us.at[pl.ds(0, 256)]), (xlo.at[pl.ds(256, 256)], cs.at[pl.ds(0, 256)]),
            (xhi.at[pl.ds(0, 256)], us.at[pl.ds(256 + rows, 256)]),
            (xhi.at[pl.ds(256, 256)], cs.at[pl.ds(256 + rows, 256)])]
    copies = [pltpu.make_async_copy(a, b, sems.at[n]) for n, (a, b) in enumerate(jobs)]
    for copy in copies:
        copy.start()
    for copy in copies:
        copy.wait()

    def side(lo, hi, start):
        return lambda x, top: (hi if top else lo)[pl.ds(pl.multiple_of(x * 8 + start, 8), 8), :]

    def store(x, y, v):
        out[pl.ds(pl.multiple_of(x * 256 + y * 8, 8), 8), :] = v
        if y == 0:
            fy0[pl.ds(pl.multiple_of(x * 8, 8), 8), :] = v
        if y == 31:
            fy1[pl.ds(pl.multiple_of(x * 8, 8), 8), :] = v

    relax_loop(32, 32,
               lambda x, y: tile_line(us, x, y, 1), lambda x, y: tile_line(cs, x, y, 1),
               lambda x, y: tile_line(ps, x, y),
               side(ylo, yhi, 0), side(ylo, yhi, 256), store)
    fx0[...] = out[pl.ds(0, 256), :]
    fx1[...] = out[pl.ds(rows - 256, 256), :]


ANY = pl.BlockSpec(memory_space=pl.ANY)


def sweep1(u, c, p, xlo, xhi, ylo, yhi):
    f = jnp.float32
    S = lambda n: jax.ShapeDtypeStruct((n, 128), f)
    return pl.pallas_call(
        sweep1_kernel,
        out_shape=(S(8192), S(256), S(256), S(256), S(256)),
        in_specs=[ANY] * 5 + [VM] * 2, out_specs=(VM,) * 5,
        scratch_shapes=[pltpu.VMEM((8192 + 512, 128), f), pltpu.VMEM((8192 + 512, 128), f),
                        pltpu.VMEM((8192, 128), f), pltpu.SemaphoreType.DMA((7,))],
        compiler_params=pltpu.CompilerParams(vmem_limit_bytes=LIMIT), name="sweep_first",
    )(u, c, p, xlo, xhi, ylo, yhi)


def sweep2_kernel(u, c, p, u_xlo, u_xhi, xlo, xhi, u_ylo, u_yhi, ylo, yhi, out, us, cs, ps, sems):
    rows = us.shape[0] - 512
    jobs = [(u, us.at[pl.ds(256, rows)]), (c, cs.at[pl.ds(256, rows)]), (p, ps),
            (u_xlo, us.at[pl.ds(0, 256)]), (xlo.at[pl.ds(256, 256)], cs.at[pl.ds(0, 256)]),
            (u_xhi, us.at[pl.ds(256 + rows, 256)]),
            (xhi.at[pl.ds(256, 256)], cs.at[pl.ds(256 + rows, 256)])]
    copies = [pltpu.make_async_copy(a, b, sems.at[n]) for n, (a, b) in enumerate(jobs)]
    for copy in copies:
        copy.start()
    for copy in copies:
        copy.wait()

    def side(lo, hi, start):
        return lambda x, top: (hi if top else lo)[pl.ds(pl.multiple_of(x * 8 + start, 8), 8), :]

    def store(x, y, v):
        out[pl.ds(pl.multiple_of(x * 256, 256) + (y // 8) * 64 + y % 8, 8, stride=8), :] = v

    relax_loop(32, 32,
               lambda x, y: us[pl.ds(pl.multiple_of((x + 1) * 256 + y * 8, 8), 8), :],
               lambda x, y: tile_line(cs, x, y, 1), lambda x, y: tile_line(ps, x, y),
               side(u_ylo, u_yhi, 0), side(ylo, yhi, 256), store)


def sweep2(u, c, p, u_xlo, u_xhi, u_ylo, u_yhi, xlo, xhi, ylo, yhi):
    f = jnp.float32
    return pl.pallas_call(
        sweep2_kernel,
        out_shape=jax.ShapeDtypeStruct((8192, 128), f),
        in_specs=[ANY] * 7 + [VM] * 4, out_specs=VM,
        scratch_shapes=[pltpu.VMEM((8192 + 512, 128), f), pltpu.VMEM((8192 + 512, 128), f),
                        pltpu.VMEM((8192, 128), f), pltpu.SemaphoreType.DMA((7,))],
        compiler_params=pltpu.CompilerParams(vmem_limit_bytes=LIMIT), name="sweep_second",
    )(u, c, p, u_xlo, u_xhi, xlo, xhi, u_ylo, u_yhi, ylo, yhi)


def channel_kernel(me, arrived, props, carry, coef, inlet, live, fluid_out, flux_out, prev):
    spans = props.shape[0]
    here = me[0]
    prev[...] = inlet[...]
    bf = jnp.bfloat16
    f = jnp.float32
    keep = live[...] > 0.0

    for s in range(spans):
        starts = [pl.multiple_of(lax.rem(here + (q * 16 + s), 128) * 32, 32) for q in range(8)]
        wall = jnp.concatenate([arrived[pl.ds(b, 32), :] for b in starts], axis=0)
        scale = coef[...]
        x = scale * wall
        hi = x.astype(bf)
        lo = (x - hi.astype(f)).astype(bf)
        p = props[s]
        ph = p.astype(bf)
        pt = (p - ph.astype(f)).astype(bf)
        dot = functools.partial(jnp.dot, preferred_element_type=f)
        fresh = (dot(lo, ph) + dot(hi, pt)) + dot(hi, ph)
        row = carry[pl.ds(s, 1), :]
        before = prev[...]
        fluid = fresh + row * before
        if s + 1 < spans:
            prev[...] = jnp.broadcast_to(fluid[:, 127:128], fluid.shape)
        flux = jnp.where(keep, scale * (wall - fluid), 0.0)
        fluid = jnp.where(keep, fluid, 0.0)
        for q in range(8):
            flux_out[pl.ds(starts[q], 32), :] = flux[q * 32:(q + 1) * 32]
            fluid_out[pl.ds(s * 8 + q, 32, stride=spans * 8), :] = fluid[q * 32:(q + 1) * 32]


def channel(me, arrived, props, carry, coef, inlet, live):
    f = jnp.float32
    return pl.pallas_call(
        channel_kernel,
        out_shape=(jax.ShapeDtypeStruct((4096, 128), f), jax.ShapeDtypeStruct((4096, 128), f)),
        in_specs=[SM] + [VM] * 6, out_specs=(VM, VM),
        scratch_shapes=[pltpu.VMEM((256, 128), f)],
        compiler_params=pltpu.CompilerParams(vmem_limit_bytes=LIMIT), name="channel_march",
    )(me, arrived, props, carry, coef, inlet, live)


def up(a, axis):
    n = lax.axis_size(axis)
    return lax.ppermute(a, axis, [(i, i + 1) for i in range(n - 1)])


def down(a, axis):
    n = lax.axis_size(axis)
    return lax.ppermute(a, axis, [(i + 1, i) for i in range(n - 1)])


def local(solid_temp, conduct, power, channel_owner, wall_rows, span_prop, span_carry,
          channel_coef, channel_inlet):
    both = ("gx", "gy")
    devices = lax.axis_size(both)
    me = lax.axis_index(both)
    nx, ny, nz = solid_temp.shape
    slots = channel_coef.shape[0]
    u, c, p = tiles(solid_temp), tiles(conduct), tiles(power)

    at = (wall_rows & ~63) | ((wall_rows & 7) << 3) | ((wall_rows >> 3) & 7)
    sent = gather(at, u, 32)
    arrived = lax.all_to_all(sent.reshape(devices, -1, 128), both, 0, 0, tiled=True)

    xface = lambda i: jnp.concatenate([u[i * 256:(i + 1) * 256], c[i * 256:(i + 1) * 256]])
    yface = lambda j: jnp.concatenate([a[:, j].reshape(nx * nz // 128, 128) for a in (solid_temp, conduct)])
    xlo, xhi = up(xface(nx - 1), "gx"), down(xface(0), "gx")
    ylo, yhi = up(yface(ny - 1), "gy"), down(yface(0), "gy")
    once, fx0, fx1, fy0, fy1 = sweep1(u, c, p, xlo, xhi, ylo, yhi)
    twice = sweep2(once, c, p, up(fx1, "gx"), down(fx0, "gx"), up(fy1, "gy"), down(fy0, "gy"),
                   xlo, xhi, ylo, yhi)

    owned = jnp.sum((channel_owner == me).astype(jnp.int32))
    turned = lambda v: jnp.broadcast_to(v.reshape(-1, 8).T.reshape(slots, 1), (slots, 128))
    live = turned((jnp.arange(slots, dtype=jnp.int32) < owned).astype(jnp.float32))
    fluid, flux = channel(me.astype(jnp.int32).reshape(1), arrived.reshape(-1, 128), span_prop, span_carry,
                          turned(channel_coef), turned(channel_inlet), live)
    returned = lax.all_to_all(flux.reshape(devices, -1, 128), both, 0, 0, tiled=True)
    solid_out = untiles(scatter(at, returned.reshape(-1, 128), twice, 16), nx, ny, nz)
    return solid_out, untiles(fluid, 1, slots, span_carry.shape[0] * 128)[0]


def solution(mesh):
    both = ("gx", "gy")
    placed = (P("gx", "gy", None),) * 3 + (P(),) + (P(both),) + (
        P(both, None, None), P(both, None), P(both), P(both))
    return jax.shard_map(local, mesh=mesh, in_specs=placed,
                         out_specs=(P("gx", "gy", None), P(both, None)), check_vma=False)
```

time: 284 us -> 163 us (0.57)
  the two profiles are of different devices: /device:TPU:102 before, /device:TPU:1 now
where the time goes in v1:
time: 163 us; the launch traced here: 160 us
  Pallas kernels  60.5 us (37%)
  waiting for transfers between devices  47.7 us (29%)
  starting transfers between devices  36.8 us (23%)
  local copies, waits for them, and re-layouts  11.3 us (7%)
  other arithmetic  2.7 us (2%)
    all_to_all x1, waiting for transfers between devices, local(): lax.all_to_all(sent.reshape(devices, -1, 128), both, 0, 0, tiled=True)  28.6 us
    pallas_call x1, Pallas kernels, sweep1(): pl.pallas_call(sweep1_kernel, out_shape=(S(8192), S(256), S(256), S(256),...  17.4 us
    pallas_call x1, Pallas kernels, sweep2(): pl.pallas_call(sweep2_kernel, out_shape=jax.ShapeDtypeStruct((8192, 128),...  17 us
    ppermute x4, starting transfers between devices, up(): return lax.ppermute(a, axis, [(i, i + 1) for i in range(n - 1)])  14.5 us
    ppermute x4, waiting for transfers between devices, up(): return lax.ppermute(a, axis, [(i, i + 1) for i in range(n - 1)])  13.2 us
    pallas_call x1, Pallas kernels, scatter(): pl.pallas_call(functools.partial(scatter_kernel, unroll=unroll), out_shap...  11.7 us
    all_to_all x1, starting transfers between devices, local(): lax.all_to_all(sent.reshape(devices, -1, 128), both, 0, 0, tiled=True)  11.5 us
    pallas_call x1, Pallas kernels, gather(): pl.pallas_call(functools.partial(gather_kernel, unroll=unroll), out_shape...  7.39 us
  transfers between devices with their start and end apart: 10, of which 5 were waited for; matrix products, arithmetic and copies ran while one was open for 5% of the time, Pallas kernels for 21%

profile of v1, /device:TPU:1, one launch (start us, length us, event | category | flops | bytes accessed | tf_op | source)
XLA Modules:
  0.0 159.8 jit_solution(11782136691158215456)
XLA Ops:
  0.6 1.3 and_or_fusion.idx
  2.0 7.4 %gather_rows.1 = f32[4096,128]{1,0:T(8,128)} custom-call(s32[4096]{0:T(1024)} %and_or_fusion.idx, f32[8192,128]{1,0:T(8,128)} %bitcast.40), custom_call_target="tpu_custom_call" | custom-call | tf_op jit(solution)/shard_map/gather_rows/pallas_call | solution.py:35
  9.3 11.5 %all-to-all-start = ((f32[128,32,128]{2,1,0:T(8,128)}), f32[128,32,128]{2,1,0:T(8,128)S(1)}, u32[]{:S(2)}, u32[]{:S(2)}) async-start(f32[128,32,128]{2,1,0:T(8,128)} %bitcast.49), calls=%async_computation | async-start | bytes 4194304 | tf_op jit(solution)/shard_map/all_to_all | solution.py:257
  20.9 0.6 convert_reduce_fusion
  21.5 0.7 fusion
  22.2 0.1 reshape.89
  22.2 0.0 copy-done.11
  22.3 0.1 reshape.78
  22.3 0.1 copy.11
  22.4 0.1 broadcast_in_dim.19
  22.5 0.1 reshape.79
  22.6 0.1 copy.12
  22.6 0.1 broadcast_in_dim.21
  22.7 28.6 %all-to-all-done = f32[128,32,128]{2,1,0:T(8,128)S(1)} async-done(((f32[128,32,128]{2,1,0:T(8,128)}), f32[128,32,128]{2,1,0:T(8,128)S(1)}, u32[]{:S(2)}, u32[]{:S(2)}) %all-to-all-start) | async-done | bytes 2097184 | tf_op jit(solution)/shard_map/all_to_all | solution.py:257
  51.4 0.9 broadcast_in_dim.23.live
  52.2 0.8 broadcast_in_dim.20.coef
  53.0 0.7 broadcast_in_dim.22.inlet
  53.8 7.0 %channel_march.1 = (f32[4096,128]{1,0:T(8,128)}, f32[4096,128]{1,0:T(8,128)}) custom-call(s32[1]{0:T(128)} %bitcast.me, f32[4096,128]{1,0:T(8,128)} %bitcast.50, f32[16,128,128]{2,1,0:T(8,128)} %props.1, f32[16,128]{1,0:T(8,128)} %carry.1, f32[256,128]{1,0:T(8,128)} %broadcast_in_dim.20.coef, f32[256,128]{1,0:T(8,128)} %broadcast_in_dim.22.inlet, ...), custom_call_target="tpu_custom_call" | custom-call | tf_op jit(solution)/shard_map/channel_march/pallas_call | solution.py:227
  60.8 4.3 %all-to-all-start.1 = ((f32[128,32,128]{2,1,0:T(8,128)}), f32[128,32,128]{2,1,0:T(8,128)S(1)}, u32[]{:S(2)}, u32[]{:S(2)}) async-start(f32[128,32,128]{2,1,0:T(8,128)} %bitcast.52), calls=%async_computation.1 | async-start | bytes 4194304 | tf_op jit(solution)/shard_map/all_to_all | solution.py:272
  65.1 1.0 fusion.3
  66.1 1.0 fusion.4
  67.2 3.6 %collective-permute-start = (f32[512,128]{1,0:T(8,128)S(1)}, f32[512,128]{1,0:T(8,128)S(1)}, u32[]{:S(2)}, u32[]{:S(2)}) collective-permute-start(f32[512,128]{1,0:T(8,128)S(1)} %pad_maximum_fusion), channel_id=1, source_target_pairs={{0,32},{32,64},{64,96},{1,33},{33,65},{65,97},{2,34},{34,66},{66,9... | collective-permute-start | bytes 786440 | tf_op jit(solution)/shard_map/ppermute | solution.py:238
  70.8 1.3 collective-permute-start.1
  72.1 1.8 %fusion.1 = (f32[32,1,1024]{2,1,0:T(1,128)S(1)}, f32[32,1,1024]{2,1,0:T(1,128)S(1)}) fusion(f32[32,32,1024]{2,1,0:T(8,128)} %param.9), kind=kLoop, calls=%fused_computation.8 | loop fusion | bytes 524288 | tf_op jit(solution)/shard_map/slice | solution.py:260
  73.8 1.8 %fusion.2 = (f32[32,1,1024]{2,1,0:T(1,128)S(1)}, f32[32,1,1024]{2,1,0:T(1,128)S(1)}) fusion(f32[32,32,1024]{2,1,0:T(8,128)} %param.10), kind=kLoop, calls=%fused_computation.9 | loop fusion | bytes 524288 | tf_op jit(solution)/shard_map/slice | solution.py:260
  75.6 3.7 %collective-permute-start.2 = (f32[512,128]{1,0:T(8,128)S(1)}, f32[512,128]{1,0:T(8,128)S(1)}, u32[]{:S(2)}, u32[]{:S(2)}) collective-permute-start(f32[512,128]{1,0:T(8,128)S(1)} %pad_maximum_fusion.2), channel_id=1, source_target_pairs={{0,1},{1,2},{2,3},{3,4},{4,5},{5,6},{6,7},{7,8},{8,9},{9,10},{10,1... | collective-permute-start | bytes 786440 | tf_op jit(solution)/shard_map/ppermute | solution.py:238
  79.3 1.9 %collective-permute-start.3 = (f32[512,128]{1,0:T(8,128)S(1)}, f32[512,128]{1,0:T(8,128)S(1)}, u32[]{:S(2)}, u32[]{:S(2)}) collective-permute-start(f32[512,128]{1,0:T(8,128)S(1)} %pad_maximum_fusion.3), channel_id=1, source_target_pairs={{1,0},{2,1},{3,2},{4,3},{5,4},{6,5},{7,6},{8,7},{9,8},{10,9},{11,1... | collective-permute-start | bytes 786440 | tf_op jit(solution)/shard_map/ppermute | solution.py:243
  81.3 12.9 %collective-permute-done.xlo = f32[512,128]{1,0:T(8,128)S(1)} collective-permute-done((f32[512,128]{1,0:T(8,128)S(1)}, f32[512,128]{1,0:T(8,128)S(1)}, u32[]{:S(2)}, u32[]{:S(2)}) %collective-permute-start) | collective-permute-done | bytes 262176 | tf_op jit(solution)/shard_map/ppermute | solution.py:238
  94.2 1.6 collective-permute-done.1.xhi
  95.8 0.0 collective-permute-done.2.ylo
  95.8 0.0 collective-permute-done.3.yhi
  95.8 0.7 copy-done.3
  96.5 0.1 copy-done.4
  96.6 0.1 copy-done.5
  96.7 17.4 %sweep_first.1 = (f32[8192,128]{1,0:T(8,128)}, f32[256,128]{1,0:T(8,128)}, f32[256,128]{1,0:T(8,128)}, f32[256,128]{1,0:T(8,128)}, f32[256,128]{1,0:T(8,128)}) custom-call(f32[8192,128]{1,0:T(8,128)} %bitcast.42, f32[8192,128]{1,0:T(8,128)} %bitcast.44, f32[8192,128]{1,0:T(8,128)} %bitcast.46, f32[512,128]{1,0:T(8,128)} %copy-done.2, f32[512,128]{1,0:T(8,128)} %copy-done.3, ...), custom_call_target="tpu_custom_call" | custom-call | tf_op jit(solution)/shard_map/sweep_first/pallas_call | solution.py:147
  114.1 3.9 %collective-permute-start.4 = (f32[256,128]{1,0:T(8,128)}, f32[256,128]{1,0:T(8,128)S(1)}, u32[]{:S(2)}, u32[]{:S(2)}) collective-permute-start(f32[256,128]{1,0:T(8,128)} %get-tuple-element.11), channel_id=1, source_target_pairs={{0,32},{32,64},{64,96},{1,33},{33,65},{65,97},{2,34},{34,66},{66,9... | collective-permute-start | bytes 393224 | tf_op jit(solution)/shard_map/ppermute | solution.py:238
  117.9 1.3 collective-permute-start.5
  119.2 3.4 %collective-permute-start.6 = (f32[256,128]{1,0:T(8,128)}, f32[256,128]{1,0:T(8,128)S(1)}, u32[]{:S(2)}, u32[]{:S(2)}) collective-permute-start(f32[256,128]{1,0:T(8,128)} %get-tuple-element.13), channel_id=1, source_target_pairs={{0,1},{1,2},{2,3},{3,4},{4,5},{5,6},{6,7},{7,8},{8,9},{9,10},{10,1... | collective-permute-start | bytes 393224 | tf_op jit(solution)/shard_map/ppermute | solution.py:238
  122.6 1.9 %collective-permute-start.7 = (f32[256,128]{1,0:T(8,128)}, f32[256,128]{1,0:T(8,128)S(1)}, u32[]{:S(2)}, u32[]{:S(2)}) collective-permute-start(f32[256,128]{1,0:T(8,128)} %get-tuple-element.14), channel_id=1, source_target_pairs={{1,0},{2,1},{3,2},{4,3},{5,4},{6,5},{7,6},{8,7},{9,8},{10,9},{11,1... | collective-permute-start | bytes 393224 | tf_op jit(solution)/shard_map/ppermute | solution.py:243
  124.5 0.0 collective-permute-done.4.u_xlo
  124.6 0.0 collective-permute-done.5.u_xhi
  124.6 0.3 collective-permute-done.6.u_ylo
  124.9 4.3 %collective-permute-done.7.u_yhi = f32[256,128]{1,0:T(8,128)S(1)} collective-permute-done((f32[256,128]{1,0:T(8,128)}, f32[256,128]{1,0:T(8,128)S(1)}, u32[]{:S(2)}, u32[]{:S(2)}) %collective-permute-start.7) | collective-permute-done | bytes 131104 | tf_op jit(solution)/shard_map/ppermute | solution.py:243
  129.1 0.7 copy-done.9
  129.8 17.0 %sweep_second.1.src = f32[8192,128]{1,0:T(8,128)} custom-call(f32[8192,128]{1,0:T(8,128)} %get-tuple-element.10.u, f32[8192,128]{1,0:T(8,128)} %bitcast.45, f32[8192,128]{1,0:T(8,128)} %bitcast.47, f32[256,128]{1,0:T(8,128)} %copy-done.6, f32[256,128]{1,0:T(8,128)} %copy-done.7, f32[512,128]{1,0:T(8,128)} %copy-done.2, f32[512,128]{1,0:T(8,128)} %copy-done.3, ...), custom_call_target="tpu_custom_call" | custom-call | tf_op jit(solution)/shard_map/sweep_second/pallas_call | solution.py:183
  146.8 0.0 all-to-all-done.1
  146.8 1.3 copy-done
  148.1 11.7 %scatter_rows.1 = f32[8192,128]{1,0:T(8,128)} custom-call(s32[4096]{0:T(1024)} %and_or_fusion.idx, f32[4096,128]{1,0:T(8,128)} %bitcast.48, f32[8192,128]{1,0:T(8,128)} %sweep_second.1.src), custom_call_target="tpu_custom_call" | custom-call | tf_op jit(solution)/shard_map/scatter_rows/pallas_call | solution.py:56
  (24 shorter events, 0.1 us)
Async XLA Ops:
  2.0 18.9 %copy-start.10 = (s32[16384]{0:T(1024)S(1)}, s32[16384]{0:T(1024)}, u32[]{:S(2)}) copy-start(s32[16384]{0:T(1024)} %param.12) | copy-start | bytes 196612
  2.0 20.3 %copy-start.11 = (f32[256]{0:T(256)S(1)}, f32[256]{0:T(256)}, u32[]{:S(2)}) copy-start(f32[256]{0:T(256)} %param.16) | copy-start | bytes 3076
  2.0 20.5 %copy-start.12 = (f32[256]{0:T(256)S(1)}, f32[256]{0:T(256)}, u32[]{:S(2)}) copy-start(f32[256]{0:T(256)} %param.17) | copy-start | bytes 3076
  9.3 42.0 %all-to-all-start = ((f32[128,32,128]{2,1,0:T(8,128)}), f32[128,32,128]{2,1,0:T(8,128)S(1)}, u32[]{:S(2)}, u32[]{:S(2)}) async-start(f32[128,32,128]{2,1,0:T(8,128)} %bitcast.49), calls=%async_computation | async-start | bytes 4194304 | tf_op jit(solution)/shard_map/all_to_all | solution.py:257
  51.4 2.4 %copy-start.1 = (f32[128,32,128]{2,1,0:T(8,128)}, f32[128,32,128]{2,1,0:T(8,128)S(1)}, u32[]{:S(2)}) copy-start(f32[128,32,128]{2,1,0:T(8,128)S(1)} %all-to-all-done) | copy-start | bytes 6291460
  60.8 86.0 %all-to-all-start.1 = ((f32[128,32,128]{2,1,0:T(8,128)}), f32[128,32,128]{2,1,0:T(8,128)S(1)}, u32[]{:S(2)}, u32[]{:S(2)}) async-start(f32[128,32,128]{2,1,0:T(8,128)} %bitcast.52), calls=%async_computation.1 | async-start | bytes 4194304 | tf_op jit(solution)/shard_map/all_to_all | solution.py:272
  67.2 27.1 %collective-permute-start = (f32[512,128]{1,0:T(8,128)S(1)}, f32[512,128]{1,0:T(8,128)S(1)}, u32[]{:S(2)}, u32[]{:S(2)}) collective-permute-start(f32[512,128]{1,0:T(8,128)S(1)} %pad_maximum_fusion), channel_id=1, source_target_pairs={{0,32},{32,64},{64,96},{1,33},{33,65},{65,97},{2,34},{34,66},{66,9... | collective-permute-start | bytes 786440 | tf_op jit(solution)/shard_map/ppermute | solution.py:238
  70.8 25.0 %collective-permute-start.1 = (f32[512,128]{1,0:T(8,128)S(1)}, f32[512,128]{1,0:T(8,128)S(1)}, u32[]{:S(2)}, u32[]{:S(2)}) collective-permute-start(f32[512,128]{1,0:T(8,128)S(1)} %pad_maximum_fusion.1), channel_id=1, source_target_pairs={{32,0},{64,32},{96,64},{33,1},{65,33},{97,65},{34,2},{66,34},{98,6... | collective-permute-start | bytes 786440 | tf_op jit(solution)/shard_map/ppermute | solution.py:243
  75.6 20.2 %collective-permute-start.2 = (f32[512,128]{1,0:T(8,128)S(1)}, f32[512,128]{1,0:T(8,128)S(1)}, u32[]{:S(2)}, u32[]{:S(2)}) collective-permute-start(f32[512,128]{1,0:T(8,128)S(1)} %pad_maximum_fusion.2), channel_id=1, source_target_pairs={{0,1},{1,2},{2,3},{3,4},{4,5},{5,6},{6,7},{7,8},{8,9},{9,10},{10,1... | collective-permute-start | bytes 786440 | tf_op jit(solution)/shard_map/ppermute | solution.py:238
  79.3 16.5 %collective-permute-start.3 = (f32[512,128]{1,0:T(8,128)S(1)}, f32[512,128]{1,0:T(8,128)S(1)}, u32[]{:S(2)}, u32[]{:S(2)}) collective-permute-start(f32[512,128]{1,0:T(8,128)S(1)} %pad_maximum_fusion.3), channel_id=1, source_target_pairs={{1,0},{2,1},{3,2},{4,3},{5,4},{6,5},{7,6},{8,7},{9,8},{10,9},{11,1... | collective-permute-start | bytes 786440 | tf_op jit(solution)/shard_map/ppermute | solution.py:243
  94.2 1.6 %copy-start.2 = (f32[512,128]{1,0:T(8,128)}, f32[512,128]{1,0:T(8,128)S(1)}, u32[]{:S(2)}) copy-start(f32[512,128]{1,0:T(8,128)S(1)} %collective-permute-done.xlo) | copy-start | bytes 786436
  95.8 0.7 copy-start.3
  95.8 0.8 copy-start.4
  95.8 0.9 copy-start.5
  114.1 10.5 %collective-permute-start.4 = (f32[256,128]{1,0:T(8,128)}, f32[256,128]{1,0:T(8,128)S(1)}, u32[]{:S(2)}, u32[]{:S(2)}) collective-permute-start(f32[256,128]{1,0:T(8,128)} %get-tuple-element.11), channel_id=1, source_target_pairs={{0,32},{32,64},{64,96},{1,33},{33,65},{65,97},{2,34},{34,66},{66,9... | collective-permute-start | bytes 393224 | tf_op jit(solution)/shard_map/ppermute | solution.py:238
  117.9 6.6 %collective-permute-start.5 = (f32[256,128]{1,0:T(8,128)}, f32[256,128]{1,0:T(8,128)S(1)}, u32[]{:S(2)}, u32[]{:S(2)}) collective-permute-start(f32[256,128]{1,0:T(8,128)} %get-tuple-element.12), channel_id=1, source_target_pairs={{32,0},{64,32},{96,64},{33,1},{65,33},{97,65},{34,2},{66,34},{98,6... | collective-permute-start | bytes 393224 | tf_op jit(solution)/shard_map/ppermute | solution.py:243
  119.2 5.6 %collective-permute-start.6 = (f32[256,128]{1,0:T(8,128)}, f32[256,128]{1,0:T(8,128)S(1)}, u32[]{:S(2)}, u32[]{:S(2)}) collective-permute-start(f32[256,128]{1,0:T(8,128)} %get-tuple-element.13), channel_id=1, source_target_pairs={{0,1},{1,2},{2,3},{3,4},{4,5},{5,6},{6,7},{7,8},{8,9},{9,10},{10,1... | collective-permute-start | bytes 393224 | tf_op jit(solution)/shard_map/ppermute | solution.py:238
  122.6 6.5 %collective-permute-start.7 = (f32[256,128]{1,0:T(8,128)}, f32[256,128]{1,0:T(8,128)S(1)}, u32[]{:S(2)}, u32[]{:S(2)}) collective-permute-start(f32[256,128]{1,0:T(8,128)} %get-tuple-element.14), channel_id=1, source_target_pairs={{1,0},{2,1},{3,2},{4,3},{5,4},{6,5},{7,6},{8,7},{9,8},{10,9},{11,1... | collective-permute-start | bytes 393224 | tf_op jit(solution)/shard_map/ppermute | solution.py:243
  124.6 4.6 %copy-start.6 = (f32[256,128]{1,0:T(8,128)}, f32[256,128]{1,0:T(8,128)S(1)}, u32[]{:S(2)}) copy-start(f32[256,128]{1,0:T(8,128)S(1)} %collective-permute-done.4.u_xlo) | copy-start | bytes 393220
  124.6 4.5 %copy-start.7 = (f32[256,128]{1,0:T(8,128)}, f32[256,128]{1,0:T(8,128)S(1)}, u32[]{:S(2)}) copy-start(f32[256,128]{1,0:T(8,128)S(1)} %collective-permute-done.5.u_xhi) | copy-start | bytes 393220
  124.9 4.3 %copy-start.8 = (f32[256,128]{1,0:T(8,128)}, f32[256,128]{1,0:T(8,128)S(1)}, u32[]{:S(2)}) copy-start(f32[256,128]{1,0:T(8,128)S(1)} %collective-permute-done.6.u_ylo) | copy-start | bytes 393220
  129.1 0.7 copy-start.9
  146.8 1.4 copy-start

commit v2 on v1

v2 whole, which is shorter than its diff:
```python
import functools

import jax
import jax.numpy as jnp
from jax import lax
from jax.experimental import pallas as pl
from jax.experimental.pallas import tpu as pltpu
from jax.sharding import PartitionSpec as P

F32 = jnp.float32
VM = pl.BlockSpec(memory_space=pltpu.VMEM)
SM = pl.BlockSpec(memory_space=pltpu.SMEM)
ANY = pl.BlockSpec(memory_space=pl.ANY)
PARAMS = pltpu.CompilerParams(vmem_limit_bytes=56 * 2**20)
SMALL = pltpu.CompilerParams(vmem_limit_bytes=16 * 2**20)
LINES = 32
LINE = 8
PLANE = LINES * LINE
ROWS = LINES * PLANE
PARTS = 8
SPAN = ROWS // PARTS


def shape(rows):
    return pltpu.HBM((rows, 128), F32)


def in_hbm(*arrays):
    return [pltpu.with_memory_space_constraint(a, pltpu.HBM) for a in arrays]


def in_smem(*arrays):
    return [pltpu.with_memory_space_constraint(a, pltpu.SMEM) for a in arrays]


def tiles(a):
    x, y, z = a.shape
    return a.reshape(x, y // 8, 8, z // 128, 128).transpose(0, 1, 3, 2, 4).reshape(-1, 128)


def untiles(a, x, y, z):
    return a.reshape(x, y // 8, z // 128, 8, 128).transpose(0, 1, 3, 2, 4).reshape(x, y, z)


def aligned(i, n):
    return pl.multiple_of(i, n)


def tiled_line(x, y):
    return pl.ds(aligned(x * PLANE, PLANE) + (y // 8) * 64 + y % 8, LINE, stride=8)


def plain_line(x, y=0):
    return pl.ds(aligned(x * PLANE + y * LINE, LINE), LINE)


def place_in_tiles(r):
    return (r & ~63) | ((r & 7) << 3) | ((r >> 3) & 7)


def piece(ref, k, shift=0):
    return ref.at[pl.ds(aligned(k * SPAN + shift, 8), SPAN)]


def gather_kernel(rows, u, c, out, at, sx0, sx1, sy0, sy1, block, made, sides, at_v, sems, done, extra):
    loads = [pltpu.make_async_copy(piece(u, k), piece(block, k), sems.at[k]) for k in range(PARTS)]
    lines = [pltpu.make_async_copy(a, b, extra.at[n]) for n, (a, b) in enumerate((
        (c.at[:, pl.ds(0, 64)], sides.at[:, pl.ds(0, 64)]),
        (c.at[:, pl.ds(192, 64)], sides.at[:, pl.ds(192, 64)]),
        (c.at[0, pl.ds(64, 128)], sides.at[0, pl.ds(64, 128)]),
        (c.at[LINES - 1, pl.ds(64, 128)], sides.at[LINES - 1, pl.ds(64, 128)])))]
    for load in loads + lines:
        load.start()
    at_v[...] = place_in_tiles(rows[...])
    listed = pltpu.make_async_copy(at_v, at, sems.at[PARTS])
    listed.start()
    listed.wait()
    for load in loads:
        load.wait()
    groups = rows.shape[0]
    each = groups // PARTS

    def save(k):
        part = pl.ds(aligned(k * each * 128, 128), each * 128)
        return pltpu.make_async_copy(made.at[part], out.at[part], done.at[k])

    def step(k, _):
        def group(i, _):
            g = k * each + i
            base = aligned(g * 128, 128)
            for first in range(0, 128, 32):
                found = [block[pl.ds(at[g, first + n], 1), :] for n in range(32)]
                for n in range(32):
                    made[pl.ds(base + (first + n), 1), :] = found[n]
            return 0

        lax.fori_loop(0, each, group, 0)
        save(k).start()
        return 0

    lax.fori_loop(0, PARTS, step, 0)
    for load in lines:
        load.wait()
    for n in range(LINES):
        row = pl.ds(n * LINE, LINE)
        below = pl.ds(PLANE + n * LINE, LINE)
        for ref, x, y in ((sx0, 0, n), (sx1, LINES - 1, n), (sy0, n, 0), (sy1, n, LINES - 1)):
            ref[row, :] = block[tiled_line(x, y), :]
            ref[below, :] = sides[x, pl.ds((y // 8) * 64 + y % 8, LINE, stride=8), :]
    for k in range(PARTS):
        save(k).wait()


def gather(rows, u, c):
    n = rows.shape[0] * 128
    return pl.pallas_call(
        gather_kernel, out_shape=(shape(n), pltpu.SMEM(rows.shape, jnp.int32)) + (shape(2 * PLANE),) * 4,
        in_specs=[VM, ANY, ANY], out_specs=(ANY, SM) + (VM,) * 4,
        scratch_shapes=[pltpu.VMEM((ROWS, 128), F32), pltpu.VMEM((n, 128), F32), pltpu.VMEM((LINES, PLANE, 128), F32),
                        pltpu.VMEM(rows.shape, jnp.int32), pltpu.SemaphoreType.DMA((PARTS + 1,)),
                        pltpu.SemaphoreType.DMA((PARTS,)), pltpu.SemaphoreType.DMA((4,))],
        compiler_params=PARAMS, name="gather_rows",
    )(rows, *in_hbm(u, c.reshape(LINES, PLANE, 128)))


def finish_kernel(at, flux, src, kx0, kx1, ky0, ky1, xlo, xhi, ylo, yhi, out, block, sides, sems, beside):
    loads = [pltpu.make_async_copy(piece(src, k), piece(block, k), sems.at[k]) for k in range(PARTS)]
    extra = [pltpu.make_async_copy(a, sides.at[n], beside.at[n])
             for n, a in enumerate((kx0, kx1, ky0, ky1, xlo, xhi, ylo, yhi))]
    for load in loads + extra:
        load.start()
    for load in loads:
        load.wait()

    def group(g, _):
        base = aligned(g * 128, 128)
        for first in range(0, 128, 16):
            where = [at[g, first + n] for n in range(16)]
            new = [block[pl.ds(t, 1), :] - flux[pl.ds(base + (first + n), 1), :] for n, t in enumerate(where)]
            for t, v in zip(where, new):
                block[pl.ds(t, 1), :] = v
        return 0

    lax.fori_loop(0, at.shape[0], group, 0)
    for load in extra:
        load.wait()
    for n in range(LINES):
        line = plain_line(0, n)
        for side, place in enumerate((tiled_line(0, n), tiled_line(LINES - 1, n),
                                      tiled_line(n, 0), tiled_line(n, LINES - 1))):
            block[place, :] = block[place, :] + sides[side, line, :] * sides[side + 4, line, :]
    saves = [pltpu.make_async_copy(piece(block, k), piece(out, k), sems.at[k]) for k in range(PARTS)]
    for save in saves:
        save.start()
    for save in saves:
        save.wait()


def finish(at, flux, src, gains, halos):
    return pl.pallas_call(
        finish_kernel, out_shape=shape(ROWS), in_specs=[SM, VM] + [ANY] * 9, out_specs=ANY,
        scratch_shapes=[pltpu.VMEM((ROWS, 128), F32), pltpu.VMEM((8, PLANE, 128), F32),
                        pltpu.SemaphoreType.DMA((PARTS,)), pltpu.SemaphoreType.DMA((8,))],
        compiler_params=SMALL, name="subtract_rows",
    )(*in_smem(at), flux, *in_hbm(src, *gains, *halos))


def step_up(a, edge, corner, fill):
    rolled = pltpu.roll(a, 127, 1)
    carried = pltpu.roll(rolled, 7, 0)
    return jnp.where(edge, jnp.where(corner, fill, carried), rolled)


def step_down(a, edge, corner, fill):
    rolled = pltpu.roll(a, 1, 1)
    carried = pltpu.roll(rolled, 1, 0)
    return jnp.where(edge, jnp.where(corner, fill, carried), rolled)


def relax_plane(x, load_u, load_c, load_p, store, whole):
    lane = lax.broadcasted_iota(jnp.int32, (8, 128), 1)
    sub = lax.broadcasted_iota(jnp.int32, (8, 128), 0)
    top, bottom = lane == 127, lane == 0
    last, first = sub == 7, sub == 0
    zero = jnp.zeros((8, 128), F32)
    u_old, c_old, w_old = zero, zero, zero
    u, c = load_u(x, 0), load_c(x, 0)
    w = u * c
    for y in range(LINES):
        if y + 1 < LINES:
            u_new, c_new = load_u(x, y + 1), load_c(x, y + 1)
            w_new = u_new * c_new
        else:
            u_new, c_new, w_new = zero, zero, zero
        ul, uh = load_u(x - 1, y), load_u(x + 1, y)
        cl, ch = load_c(x - 1, y), load_c(x + 1, y)
        face = c + step_up(c, top, last, 0.0)
        flow = face * step_up(u, top, last, 0.0)
        back = step_down(face * u, bottom, first, 0.0)
        numer = c * ((u_old + u_new) + (ul + uh)) + ((w_old + w_new) + (cl * ul + ch * uh))
        numer = numer + (flow + back) + 2.0 * load_p(x, y)
        denom = None
        if whole:
            below = step_down(face, bottom, first, c)
            denom = 4.0 * c + ((c_old + c_new) + (cl + ch)) + (face + below)
        store(x, y, numer, denom, c)
        u_old, c_old, w_old = u, c, w
        u, c, w = u_new, c_new, w_new


def planes(ready, relax, save):
    each = LINES // PARTS
    ready(0)

    def step(k, _):
        @pl.when(k + 1 < PARTS)
        def _():
            ready(k + 1)

        lax.fori_loop(0, each, lambda i, _: (relax(k * each + i), 0)[1], 0)
        for copy in save(k):
            copy.start()
        return 0

    lax.fori_loop(0, PARTS, step, 0)


def both_sides(relax):
    lax.fori_loop(0, 2, lambda i, _: (relax(i * (LINES - 1)), 0)[1], 0)


def clear_beyond(*refs):
    for ref in refs:
        ref[pl.ds(0, PLANE), :] = jnp.zeros((PLANE, 128), F32)
        ref[pl.ds(PLANE + ROWS, PLANE), :] = jnp.zeros((PLANE, 128), F32)


def first_kernel(after, u, c, p, out, gain, nx0, nx1, ny0, ny1, us, cs, ps, vs, gs, nx, sems, done):
    del after

    def loads(k):
        return [pltpu.make_async_copy(piece(a, k), piece(b, k, shift), sems.at[n, k])
                for n, (a, b, shift) in enumerate(((u, us, PLANE), (c, cs, PLANE), (p, ps, 0)))]

    def save(k):
        return [pltpu.make_async_copy(piece(a, k), piece(b, k), done.at[n, k])
                for n, (a, b) in enumerate(((vs, out), (gs, gain)))]

    for k in range(PARTS):
        for load in loads(k):
            load.start()
    clear_beyond(us, cs)

    def ready(k):
        for load in loads(k):
            load.wait()

    load_u = lambda x, y: us[tiled_line(x + 1, y), :]
    load_c = lambda x, y: cs[tiled_line(x + 1, y), :]
    load_p = lambda x, y: ps[tiled_line(x, y), :]

    def put(sums, start, numer, denom):
        sums[pl.ds(aligned(start, 8), 8), :] = numer
        sums[pl.ds(aligned(start + PLANE, 8), 8), :] = denom

    def store(x, y, numer, denom, c):
        part = 1.0 / denom
        vs[plain_line(x, y), :] = numer * part
        gs[plain_line(x, y), :] = part
        if y == 0:
            put(ny0, x * LINE, numer, denom)
        if y == LINES - 1:
            put(ny1, x * LINE, numer, denom)

    planes(ready, lambda x: relax_plane(x, load_u, load_c, load_p, store, True), save)

    def store_x(x, y, numer, denom, c):
        put(nx, lax.div(x, LINES - 1) * (2 * PLANE) + y * LINE, numer, denom)

    both_sides(lambda x: relax_plane(x, load_u, load_c, load_p, store_x, True))
    nx0[...] = nx[pl.ds(0, 2 * PLANE), :]
    nx1[...] = nx[pl.ds(2 * PLANE, 2 * PLANE), :]
    for k in range(PARTS):
        for copy in save(k):
            copy.wait()


def sweep_first(after, u, c, p):
    return pl.pallas_call(
        first_kernel, out_shape=(shape(ROWS),) * 2 + (shape(2 * PLANE),) * 4,
        in_specs=[ANY] * 4, out_specs=(ANY,) * 2 + (VM,) * 4,
        scratch_shapes=[pltpu.VMEM((ROWS + 2 * PLANE, 128), F32), pltpu.VMEM((ROWS + 2 * PLANE, 128), F32),
                        pltpu.VMEM((ROWS, 128), F32), pltpu.VMEM((ROWS, 128), F32), pltpu.VMEM((ROWS, 128), F32),
                        pltpu.VMEM((4 * PLANE, 128), F32),
                        pltpu.SemaphoreType.DMA((3, PARTS)), pltpu.SemaphoreType.DMA((2, PARTS))],
        compiler_params=PARAMS, name="sweep_first",
    )(*in_hbm(after, u, c, p))


def sides_kernel(sx0, sx1, sy0, sy1, nx0, nx1, ny0, ny1, xlo, xhi, ylo, yhi, fx0, fx1, fy0, fy1):
    def part(ref, start=0):
        return ref[pl.ds(start, PLANE), :]

    def add(numer, denom, c, u_side, c_side):
        return numer + (c + c_side) * u_side, denom + c_side

    for ref, sent, sums, halo, ends in (
        (fx0, sx0, nx0, xlo, ((ylo, 0), (yhi, 0))),
        (fx1, sx1, nx1, xhi, ((ylo, PLANE - 8), (yhi, PLANE - 8))),
        (fy0, sy0, ny0, ylo, ((xlo, 0), (xhi, 0))),
        (fy1, sy1, ny1, yhi, ((xlo, PLANE - 8), (xhi, PLANE - 8))),
    ):
        c = part(sent, PLANE)
        numer, denom = add(part(sums), part(sums, PLANE), c, part(halo), part(halo, PLANE))
        ref[...] = numer / denom
        for rows, (other, line) in zip((0, PLANE - 8), ends):
            at = slice(rows, rows + 8)
            side = other[pl.ds(line, 8), :], other[pl.ds(PLANE + line, 8), :]
            n, d = add(numer[at], denom[at], c[at], *side)
            ref[pl.ds(rows, 8), :] = n / d


def fix_sides(parts, halos):
    return pl.pallas_call(
        sides_kernel, out_shape=(shape(PLANE),) * 4, in_specs=[VM] * 12, out_specs=(VM,) * 4,
        compiler_params=PARAMS, name="sweep_first_sides",
    )(*parts, *halos)


def second_kernel(after, u, c, p, gain, fx0, fx1, fy0, fy1, xlo, xhi, ylo, yhi, out, kx0, kx1, ky0, ky1,
                  us, cs, ps, gs, vs, kx, sems, done):
    del after

    def loads(k):
        return [pltpu.make_async_copy(piece(a, k), piece(b, k, shift), sems.at[n, k])
                for n, (a, b, shift) in enumerate(((u, us, PLANE), (c, cs, PLANE), (p, ps, 0), (gain, gs, 0)))]

    def save(k):
        return [pltpu.make_async_copy(piece(vs, k), piece(out, k), done.at[k])]

    for k in range(PARTS):
        for load in loads(k):
            load.start()
    clear_beyond(us, cs)

    def ready(k):
        for load in loads(k):
            load.wait()
        for i in range(LINES // PARTS):
            x = k * (LINES // PARTS) + i
            us[plain_line(x + 1, 0), :] = fy0[plain_line(0, x), :]
            us[plain_line(x + 1, LINES - 1), :] = fy1[plain_line(0, x), :]

        @pl.when(k == 0)
        def _():
            us[pl.ds(PLANE, PLANE), :] = fx0[...]

        @pl.when(k == PARTS - 1)
        def _():
            us[pl.ds(ROWS, PLANE), :] = fx1[...]

    load_u = lambda x, y: us[plain_line(x + 1, y), :]
    load_c = lambda x, y: cs[tiled_line(x + 1, y), :]
    load_p = lambda x, y: ps[tiled_line(x, y), :]
    y_sides = {0: (ylo, ky0), LINES - 1: (yhi, ky1)}

    def put(x, y, numer, part, c, beside):
        if y in y_sides or beside is not None:
            denom = 1.0 / part
            if beside is not None:
                denom = denom + beside
            if y in y_sides:
                halo, k_side = y_sides[y]
                outer = halo[pl.ds(aligned(PLANE + x * LINE, 8), 8), :]
                part = 1.0 / (denom + outer)
                k_side[plain_line(0, x), :] = (c + outer) * part
            else:
                part = 1.0 / denom
        vs[tiled_line(x, y), :] = numer * part
        return part

    def store(x, y, numer, _, c):
        put(x, y, numer, gs[plain_line(x, y), :], c, None)

    planes(ready, lambda x: relax_plane(x, load_u, load_c, load_p, store, False), lambda k: [])

    def store_x(x, y, numer, _, c):
        line = pl.ds(PLANE + y * LINE, LINE)
        beside = jnp.where(x == 0, xlo[line, :], xhi[line, :])
        part = put(x, y, numer, gs[plain_line(x, y), :], c, beside)
        kx[pl.ds(aligned(lax.div(x, LINES - 1) * PLANE + y * LINE, 8), 8), :] = (c + beside) * part

    both_sides(lambda x: relax_plane(x, load_u, load_c, load_p, store_x, False))
    for k in range(PARTS):
        for copy in save(k):
            copy.start()
    kx0[...] = kx[pl.ds(0, PLANE), :]
    kx1[...] = kx[pl.ds(PLANE, PLANE), :]
    for k in range(PARTS):
        for copy in save(k):
            copy.wait()


def sweep_second(after, u, c, p, gain, faces, halos):
    return pl.pallas_call(
        second_kernel, out_shape=(shape(ROWS),) + (shape(PLANE),) * 4,
        in_specs=[ANY] * 5 + [VM] * 8, out_specs=(ANY,) + (VM,) * 4,
        scratch_shapes=[pltpu.VMEM((ROWS + 2 * PLANE, 128), F32), pltpu.VMEM((ROWS + 2 * PLANE, 128), F32),
                        pltpu.VMEM((ROWS, 128), F32), pltpu.VMEM((ROWS, 128), F32), pltpu.VMEM((ROWS, 128), F32),
                        pltpu.VMEM((2 * PLANE, 128), F32),
                        pltpu.SemaphoreType.DMA((4, PARTS)), pltpu.SemaphoreType.DMA((PARTS,))],
        compiler_params=PARAMS, name="sweep_second",
    )(*in_hbm(after, u, c, p, gain), *faces, *halos)


def channel_kernel(*refs):
    (me, owners, arrived, props, carry, coef_at, inlet_at, fluid_out, flux_out,
     fluids, fluxes, weights, prev, coef, live, done_x, done_f, here_p) = refs[-18:]
    spans, groups = props.shape[0], arrived.shape[0]
    size = arrived.shape[1] // spans
    here = me[0]
    halves = [pltpu.make_async_copy(props.at[part], weights.at[part], here_p.at[n])
              for n, part in enumerate((pl.ds(0, spans // 2), pl.ds(spans // 2, spans // 2)))]
    for load in halves:
        load.start()
    owned = jnp.sum((owners[...] == here).astype(F32), axis=0, keepdims=True)
    owned = jnp.sum(owned, axis=1, keepdims=True)
    bf = jnp.bfloat16
    dot = functools.partial(jnp.dot, preferred_element_type=F32)

    def block(s):
        return pl.ds(aligned(lax.rem(here + s, spans) * size, size), size)

    def save_flux(s):
        return pltpu.make_async_copy(fluxes.at[:, block(s), :], flux_out.at[:, block(s), :], done_x.at[s])

    def save_fluid(n):
        part = pl.ds(n * 4 * groups, 4 * groups)
        return pltpu.make_async_copy(fluids.at[:, part, :], fluid_out.at[:, part, :], done_f.at[n])

    row = lax.broadcasted_iota(jnp.int32, (16, 128), 0)
    lane = lax.broadcasted_iota(jnp.int32, (16, 128), 1)
    for q in range(groups):
        mine = lane == row * groups + q
        for half in range(2):
            part = pl.ds(q * size + half * 16, 16)
            for ref, values in ((prev, inlet_at), (coef, coef_at)):
                column = jnp.sum(jnp.where(mine, values[pl.ds(half, 1), :], 0.0), axis=1, keepdims=True)
                ref[part, :] = jnp.broadcast_to(column, (16, 128))
            live[part, :] = jnp.where(((row + half * 16) * groups + q).astype(F32) < owned, 1.0, 0.0)
    keep = live[...] > 0.0

    for s in range(spans):
        if s % (spans // 2) == 0:
            halves[s // (spans // 2)].wait()
        turn = lax.div(here + s, spans)
        at = [(lax.rem(turn + q, groups), block(s)) for q in range(groups)]
        wall = jnp.concatenate([arrived[g, r, :] for g, r in at], axis=0)
        scale = coef[...]
        x = scale * wall
        hi = x.astype(bf)
        lo = (x - hi.astype(F32)).astype(bf)
        p = weights[s]
        p_hi = p.astype(bf)
        p_lo = (p - p_hi.astype(F32)).astype(bf)
        fresh = (dot(lo, p_hi) + dot(hi, p_lo)) + dot(hi, p_hi)
        fluid = fresh + carry[pl.ds(s, 1), :] * prev[...]
        if s + 1 < spans:
            prev[...] = jnp.broadcast_to(fluid[:, 127:128], fluid.shape)
        flux = jnp.where(keep, scale * (wall - fluid), 0.0)
        fluid = jnp.where(keep, fluid, 0.0)
        for q, (g, r) in enumerate(at):
            fluxes[g, r, :] = flux[q * size:(q + 1) * size]
            fluids[:, s * groups + q, :] = fluid[q * size:(q + 1) * size]
        save_flux(s).start()
        if s % 4 == 3:
            save_fluid(s // 4).start()
    for s in range(spans):
        save_flux(s).wait()
    for n in range(spans // 4):
        save_fluid(n).wait()


def channel(after, me, owners, arrived, props, carry, coef, inlet):
    spans = props.shape[0]
    groups = 8
    size = coef.shape[0] // groups
    rows = spans * size
    fluid, flux = pl.pallas_call(
        channel_kernel,
        out_shape=(jax.ShapeDtypeStruct((size, spans * groups, 128), F32),
                   pltpu.HBM((groups, rows, 128), F32)),
        in_specs=[ANY] * len(after) + [SM] + [VM] * 2 + [ANY] + [VM] * 3, out_specs=(ANY, ANY),
        scratch_shapes=[pltpu.VMEM((size, spans * groups, 128), F32), pltpu.VMEM((groups, rows, 128), F32),
                        pltpu.VMEM(props.shape, F32)]
        + [pltpu.VMEM((groups * size, 128), F32)] * 3
        + [pltpu.SemaphoreType.DMA((spans,)), pltpu.SemaphoreType.DMA((spans // 4,)),
           pltpu.SemaphoreType.DMA((2,))],
        compiler_params=SMALL, name="channel_march",
    )(*in_hbm(*after), me, owners, arrived.reshape(groups, rows, 128), *in_hbm(props), carry,
      coef.reshape(2, 128), inlet.reshape(2, 128))
    return fluid.reshape(-1, 128), flux


def up(a, axis):
    n = lax.axis_size(axis)
    return lax.ppermute(a, axis, [(i, i + 1) for i in range(n - 1)])


def down(a, axis):
    n = lax.axis_size(axis)
    return lax.ppermute(a, axis, [(i + 1, i) for i in range(n - 1)])


def local(solid_temp, conduct, power, channel_owner, wall_rows, span_prop, span_carry,
          channel_coef, channel_inlet):
    both = ("gx", "gy")
    devices = lax.axis_size(both)
    me = lax.axis_index(both).astype(jnp.int32).reshape(1)
    slots = channel_coef.shape[0]
    u, c, p = tiles(solid_temp), tiles(conduct), tiles(power)

    sent, at, *ends = gather(wall_rows.reshape(-1, 128), u, c)
    arrived = lax.all_to_all(sent.reshape(devices, -1, 128), both, 0, 0, tiled=True)

    halos = (up(ends[1], "gx"), down(ends[0], "gx"), up(ends[3], "gy"), down(ends[2], "gy"))
    once, gain, *sums = sweep_first(sent, u, c, p)
    faces = fix_sides((*ends, *sums), halos)

    fluid, flux = channel(faces, me, channel_owner.reshape(-1, 128), arrived, span_prop, span_carry,
                          channel_coef, channel_inlet)
    returned = lax.all_to_all(flux.reshape(devices, -1, 128), both, 0, 0, tiled=True)

    outer = (up(faces[1], "gx"), down(faces[0], "gx"), up(faces[3], "gy"), down(faces[2], "gy"))
    twice, *gains = sweep_second(flux, once, c, p, gain, faces, halos)
    solid_out = finish(at, returned.reshape(-1, 128), twice, gains, outer)
    return untiles(solid_out, *solid_temp.shape), untiles(fluid, 1, slots, span_carry.shape[0] * 128)[0]


def solution(mesh):
    both = ("gx", "gy")
    placed = (P("gx", "gy", None),) * 3 + (P(),) + (P(both),) + (
        P(both, None, None), P(both, None), P(both), P(both))
    return jax.shard_map(local, mesh=mesh, in_specs=placed,
                         out_specs=(P("gx", "gy", None), P(both, None)), check_vma=False)
```

time: 163 us -> 110 us (0.67); the launches traced: 160 us -> 110 us
  waiting for transfers between devices: 47.7 us -> 11.5 us
  local copies, waits for them, and re-layouts: 11.3 us -> 0.9 us
  Pallas kernels: 60.5 us -> 55.4 us
  starting transfers between devices: 36.8 us -> 41.1 us
  other arithmetic: 2.7 us -> 0 us
    all_to_all x1, waiting for transfers between devices: 28.6 us -> 0.01 us  [local(): lax.all_to_all(sent.reshape(devices, -1, 128), both, 0, 0, tiled=True)]
    ppermute x4, waiting for transfers between devices: 13.2 us -> 4.4 us  [up(): return lax.ppermute(a, axis, [(i, i + 1) for i in range(n - 1)])]
    slice x4 -> x0, local copies, waits for them, and re-layouts: 5.5 us -> none  [the longest x2 3.53 us: local(): a[:, j].reshape(nx * nz // 128, 128)]
    pallas_call x5 -> x6, Pallas kernels: 60.5 us -> 55.4 us  [the longest x1 14.7 us: sweep_second(): pl.pallas_call(second_kernel, out_shape=(shape(ROWS),) + (shape(PLANE),)...]
    all_to_all x1, starting transfers between devices: 4.35 us -> 8.91 us  [local(): lax.all_to_all(flux.reshape(devices, -1, 128), both, 0, 0, tiled=True)]
    all_to_all x1, waiting for transfers between devices: 0.01 us -> 2.94 us  [local(): lax.all_to_all(flux.reshape(devices, -1, 128), both, 0, 0, tiled=True)]
    broadcast_in_dim x5 -> x0, local copies, waits for them, and re-layouts: 2.54 us -> none  [local(): jnp.broadcast_to(v.reshape(-1, 8).T.reshape(slots, 1), (slots, 128))]
    unnamed x26 -> x34, local copies, waits for them, and re-layouts: 2.88 us -> 0.9 us
  transfers between devices with their start and end apart: 10 -> 10, of which waited for: 5 -> 4; matrix products, arithmetic and copies ran while one was open for 5% -> 0% of each run, Pallas kernels for 21% -> 28%
where the time goes in v2:
time: 110 us
  Pallas kernels  55.4 us (50%)
  starting transfers between devices  41.1 us (37%)
  waiting for transfers between devices  11.5 us (10%)
    pallas_call x1, Pallas kernels, sweep_second(): pl.pallas_call(second_kernel, out_shape=(shape(ROWS),) + (shape(PLANE),)...  14.7 us
    ppermute x4, starting transfers between devices, up(): return lax.ppermute(a, axis, [(i, i + 1) for i in range(n - 1)])  14.2 us
    pallas_call x1, Pallas kernels, sweep_first(): pl.pallas_call(first_kernel, out_shape=(shape(ROWS),) * 2 + (shape(2 * PL...  13.9 us
    all_to_all x1, starting transfers between devices, local(): lax.all_to_all(sent.reshape(devices, -1, 128), both, 0, 0, tiled=True)  11.5 us
    pallas_call x1, Pallas kernels, finish(): pl.pallas_call(finish_kernel, out_shape=shape(ROWS), in_specs=[SM, VM] +...  10.2 us
    all_to_all x1, starting transfers between devices, local(): lax.all_to_all(flux.reshape(devices, -1, 128), both, 0, 0, tiled=True)  8.91 us
    pallas_call x1, Pallas kernels, gather(): pl.pallas_call(gather_kernel, out_shape=(shape(n), pltpu.SMEM(rows.shape,...  8.81 us
    ppermute x4, starting transfers between devices, down(): return lax.ppermute(a, axis, [(i + 1, i) for i in range(n - 1)])  6.42 us
  transfers between devices with their start and end apart: 10, of which 4 were waited for; matrix products, arithmetic and copies ran while one was open for 0% of the time, Pallas kernels for 28%

profile of v2, /device:TPU:1, one launch (start us, length us, event | category | flops | bytes accessed | tf_op | source)
XLA Modules:
  0.0 109.8 jit_solution(8899299786199317897)
XLA Ops:
  0.6 8.8 %gather_rows.1 = (f32[4096,128]{1,0:T(8,128)}, s32[32,128]{1,0:T(8,128)S(4)}, f32[512,128]{1,0:T(8,128)}, f32[512,128]{1,0:T(8,128)}, f32[512,128]{1,0:T(8,128)}, /*index=5*/f32[512,128]{1,0:T(8,128)}) custom-call(s32[32,128]{1,0:T(8,128)} %bitcast.51, f32[8192,128]{1,0:T(8,128)} %bitcast.46, f32[32,256,128]{2,1,0:T(8,128)} %bitcast.41), custom_call_target="tpu_custom_call" | custom-call | tf_op jit(solution)/shard_map/gather_rows/pallas_call | solution.py:116
  9.4 0.0 copy-start.12
  9.5 11.5 %all-to-all-start = ((f32[128,32,128]{2,1,0:T(8,128)}), f32[128,32,128]{2,1,0:T(8,128)S(1)}, u32[]{:S(2)}, u32[]{:S(2)}) async-start(f32[128,32,128]{2,1,0:T(8,128)} %bitcast.48), calls=%async_computation | async-start | bytes 4194304 | tf_op jit(solution)/shard_map/all_to_all | solution.py:524
  21.0 3.4 %collective-permute-start = (f32[512,128]{1,0:T(8,128)}, f32[512,128]{1,0:T(8,128)S(1)}, u32[]{:S(2)}, u32[]{:S(2)}) collective-permute-start(f32[512,128]{1,0:T(8,128)} %get-tuple-element.27.sx1), channel_id=1, source_target_pairs={{0,32},{32,64},{64,96},{1,33},{33,65},{65,97},{2,34},{34,66},{66,9... | collective-permute-start | bytes 786440 | tf_op jit(solution)/shard_map/ppermute | solution.py:507
  24.4 0.0 copy-done.12
  24.4 1.3 %collective-permute-start.1 = (f32[512,128]{1,0:T(8,128)S(1)}, f32[512,128]{1,0:T(8,128)S(1)}, u32[]{:S(2)}, u32[]{:S(2)}) collective-permute-start(f32[512,128]{1,0:T(8,128)S(1)} %copy-done.12), channel_id=1, source_target_pairs={{32,0},{64,32},{96,64},{33,1},{65,33},{97,65},{34,2},{66,34},{98,6... | collective-permute-start | bytes 786440 | tf_op jit(solution)/shard_map/ppermute | solution.py:512
  25.7 3.7 %collective-permute-start.2 = (f32[512,128]{1,0:T(8,128)}, f32[512,128]{1,0:T(8,128)S(1)}, u32[]{:S(2)}, u32[]{:S(2)}) collective-permute-start(f32[512,128]{1,0:T(8,128)} %get-tuple-element.29.sy1), channel_id=1, source_target_pairs={{0,1},{1,2},{2,3},{3,4},{4,5},{5,6},{6,7},{7,8},{8,9},{9,10},{10,1... | collective-permute-start | bytes 786440 | tf_op jit(solution)/shard_map/ppermute | solution.py:507
  29.4 1.9 %collective-permute-start.3 = (f32[512,128]{1,0:T(8,128)}, f32[512,128]{1,0:T(8,128)S(1)}, u32[]{:S(2)}, u32[]{:S(2)}) collective-permute-start(f32[512,128]{1,0:T(8,128)} %get-tuple-element.28.sy0), channel_id=1, source_target_pairs={{1,0},{2,1},{3,2},{4,3},{5,4},{6,5},{7,6},{8,7},{9,8},{10,9},{11,1... | collective-permute-start | bytes 786440 | tf_op jit(solution)/shard_map/ppermute | solution.py:512
  31.3 0.0 copy-start
  31.3 0.0 copy-start.1
  31.4 0.0 copy-start.2
  31.4 0.0 copy-start.3
  31.4 13.9 %sweep_first.1 = (f32[8192,128]{1,0:T(8,128)}, f32[8192,128]{1,0:T(8,128)}, f32[512,128]{1,0:T(8,128)}, f32[512,128]{1,0:T(8,128)}, f32[512,128]{1,0:T(8,128)}, /*index=5*/f32[512,128]{1,0:T(8,128)}) custom-call(f32[4096,128]{1,0:T(8,128)} %get-tuple-element.30.after, f32[8192,128]{1,0:T(8,128)} %bitcast.47, f32[8192,128]{1,0:T(8,128)} %bitcast.42, ...), custom_call_target="tpu_custom_call" | custom-call | tf_op jit(solution)/shard_map/sweep_first/pallas_call | solution.py:289
  45.3 4.4 %collective-permute-done.xlo = f32[512,128]{1,0:T(8,128)S(1)} collective-permute-done((f32[512,128]{1,0:T(8,128)}, f32[512,128]{1,0:T(8,128)S(1)}, u32[]{:S(2)}, u32[]{:S(2)}) %collective-permute-start) | collective-permute-done | bytes 262176 | tf_op jit(solution)/shard_map/ppermute | solution.py:507
  49.7 2.0 %collective-permute-done.1.xhi = f32[512,128]{1,0:T(8,128)S(1)} collective-permute-done((f32[512,128]{1,0:T(8,128)S(1)}, f32[512,128]{1,0:T(8,128)S(1)}, u32[]{:S(2)}, u32[]{:S(2)}) %collective-permute-start.1) | collective-permute-done | bytes 262176 | tf_op jit(solution)/shard_map/ppermute | solution.py:512
  51.7 0.0 collective-permute-done.2.ylo
  51.7 0.0 collective-permute-done.3.yhi
  51.7 0.0 copy-start.7
  51.7 0.0 copy-done.4
  51.7 0.7 copy-done.5
  52.4 0.1 copy-done.6
  52.5 0.1 copy-done.7
  52.6 2.7 %sweep_first_sides.1 = (f32[256,128]{1,0:T(8,128)}, f32[256,128]{1,0:T(8,128)}, f32[256,128]{1,0:T(8,128)}, f32[256,128]{1,0:T(8,128)}) custom-call(f32[512,128]{1,0:T(8,128)} %get-tuple-element.26.sx0, f32[512,128]{1,0:T(8,128)} %get-tuple-element.27.sx1, f32[512,128]{1,0:T(8,128)} %get-tuple-element.28.sy0, f32[512,128]{1,0:T(8,128)} %get-tuple-element.29.sy1, ...), custom_call_target="tpu_custom_call" | custom-call | tf_op jit(solution)/shard_map/sweep_first_sides/pallas_call | solution.py:324
  55.2 0.0 copy-start.9
  55.2 0.0 copy-start.8
  55.2 0.0 all-to-all-done
  55.2 0.0 copy-done
  55.3 0.0 copy-done.1
  55.3 0.0 copy-done.2
  55.3 0.0 copy-done.3
  55.3 5.2 %channel_march.1 = (f32[32,128,128]{2,1,0:T(8,128)}, f32[8,512,128]{2,1,0:T(8,128)}) custom-call(f32[256,128]{1,0:T(8,128)} %get-tuple-element.35.refs_0_.fx0, f32[256,128]{1,0:T(8,128)} %get-tuple-element.36.refs_1_.fx1, f32[256,128]{1,0:T(8,128)} %get-tuple-element.37.refs_2_.fy0, f32[256,128]{1,0:T(8,128)} %get-tuple-element.38.refs_3_.fy1, ...), custom_call_target="tpu_custom_call" | custom-call | tf_op jit(solution)/shard_map/channel_march/pallas_call | solution.py:489
  60.5 8.9 %all-to-all-start.1 = ((f32[128,32,128]{2,1,0:T(8,128)}), f32[128,32,128]{2,1,0:T(8,128)S(1)}, u32[]{:S(2)}, u32[]{:S(2)}) async-start(f32[128,32,128]{2,1,0:T(8,128)} %bitcast.49), calls=%async_computation.1 | async-start | bytes 4194304 | tf_op jit(solution)/shard_map/all_to_all | solution.py:532
  69.4 0.0 copy-done.11
  69.4 3.4 %collective-permute-start.4 = (f32[256,128]{1,0:T(8,128)S(1)}, f32[256,128]{1,0:T(8,128)S(1)}, u32[]{:S(2)}, u32[]{:S(2)}) collective-permute-start(f32[256,128]{1,0:T(8,128)S(1)} %copy-done.11), channel_id=1, source_target_pairs={{0,32},{32,64},{64,96},{1,33},{33,65},{65,97},{2,34},{34,66},{66,9... | collective-permute-start | bytes 393224 | tf_op jit(solution)/shard_map/ppermute | solution.py:507
  72.8 0.0 copy-done.10
  72.9 1.3 %collective-permute-start.5 = (f32[256,128]{1,0:T(8,128)S(1)}, f32[256,128]{1,0:T(8,128)S(1)}, u32[]{:S(2)}, u32[]{:S(2)}) collective-permute-start(f32[256,128]{1,0:T(8,128)S(1)} %copy-done.10), channel_id=1, source_target_pairs={{32,0},{64,32},{96,64},{33,1},{65,33},{97,65},{34,2},{66,34},{98,6... | collective-permute-start | bytes 393224 | tf_op jit(solution)/shard_map/ppermute | solution.py:512
  74.2 0.0 copy-done.9
  74.2 3.7 %collective-permute-start.6 = (f32[256,128]{1,0:T(8,128)S(1)}, f32[256,128]{1,0:T(8,128)S(1)}, u32[]{:S(2)}, u32[]{:S(2)}) collective-permute-start(f32[256,128]{1,0:T(8,128)S(1)} %copy-done.9), channel_id=1, source_target_pairs={{0,1},{1,2},{2,3},{3,4},{4,5},{5,6},{6,7},{7,8},{8,9},{9,10},{10,1... | collective-permute-start | bytes 393224 | tf_op jit(solution)/shard_map/ppermute | solution.py:507
  77.9 0.0 copy-done.8
  77.9 1.9 %collective-permute-start.7 = (f32[256,128]{1,0:T(8,128)S(1)}, f32[256,128]{1,0:T(8,128)S(1)}, u32[]{:S(2)}, u32[]{:S(2)}) collective-permute-start(f32[256,128]{1,0:T(8,128)S(1)} %copy-done.8), channel_id=1, source_target_pairs={{1,0},{2,1},{3,2},{4,3},{5,4},{6,5},{7,6},{8,7},{9,8},{10,9},{11,1... | collective-permute-start | bytes 393224 | tf_op jit(solution)/shard_map/ppermute | solution.py:512
  79.8 14.7 %sweep_second.1 = (f32[8192,128]{1,0:T(8,128)}, f32[256,128]{1,0:T(8,128)}, f32[256,128]{1,0:T(8,128)}, f32[256,128]{1,0:T(8,128)}, f32[256,128]{1,0:T(8,128)}) custom-call(f32[8,512,128]{2,1,0:T(8,128)} %get-tuple-element.39.after, f32[8192,128]{1,0:T(8,128)} %get-tuple-element.40.u, f32[8192,128]{1,0:T(8,128)} %bitcast.43, f32[8192,128]{1,0:T(8,128)} %bitcast.45, ...), custom_call_target="tpu_custom_call" | custom-call | tf_op jit(solution)/shard_map/sweep_second/pallas_call | solution.py:405
  94.5 0.0 collective-permute-done.4.xlo
  94.5 2.1 %collective-permute-done.5.xhi = f32[256,128]{1,0:T(8,128)S(1)} collective-permute-done((f32[256,128]{1,0:T(8,128)S(1)}, f32[256,128]{1,0:T(8,128)S(1)}, u32[]{:S(2)}, u32[]{:S(2)}) %collective-permute-start.5) | collective-permute-done | bytes 131104 | tf_op jit(solution)/shard_map/ppermute | solution.py:512
  96.7 0.0 collective-permute-done.6.ylo
  96.7 0.0 collective-permute-done.7.yhi
  96.7 2.9 %all-to-all-done.1 = f32[128,32,128]{2,1,0:T(8,128)S(1)} async-done(((f32[128,32,128]{2,1,0:T(8,128)}), f32[128,32,128]{2,1,0:T(8,128)S(1)}, u32[]{:S(2)}, u32[]{:S(2)}) %all-to-all-start.1) | async-done | bytes 2097184 | tf_op jit(solution)/shard_map/all_to_all | solution.py:532
  99.6 0.0 copy-done.16
  99.7 10.2 %subtract_rows.1 = f32[8192,128]{1,0:T(8,128)} custom-call(s32[32,128]{1,0:T(8,128)S(4)} %get-tuple-element.25.at, f32[4096,128]{1,0:T(8,128)S(1)} %bitcast.37, f32[8192,128]{1,0:T(8,128)} %get-tuple-element.42.src, f32[256,128]{1,0:T(8,128)} %get-tuple-element.43.kx0, f32[256,128]{1,0:T(8,128)} %get-tuple-element.44.kx1, f32[256,128]{1,0:T(8,128)} %get-tuple-element.45.ky0, ...), custom_call_target="tpu_custom_call" | custom-call | tf_op jit(solution)/shard_map/subtract_rows/pallas_call | solution.py:160
  (12 shorter events, 0.0 us)
Async XLA Ops:
  9.4 15.0 %copy-start.12 = (f32[512,128]{1,0:T(8,128)S(1)}, f32[512,128]{1,0:T(8,128)}, u32[]{:S(2)}) copy-start(f32[512,128]{1,0:T(8,128)} %get-tuple-element.26.sx0) | copy-start | bytes 786436
  9.5 45.8 %all-to-all-start = ((f32[128,32,128]{2,1,0:T(8,128)}), f32[128,32,128]{2,1,0:T(8,128)S(1)}, u32[]{:S(2)}, u32[]{:S(2)}) async-start(f32[128,32,128]{2,1,0:T(8,128)} %bitcast.48), calls=%async_computation | async-start | bytes 4194304 | tf_op jit(solution)/shard_map/all_to_all | solution.py:524
  21.0 28.7 %collective-permute-start = (f32[512,128]{1,0:T(8,128)}, f32[512,128]{1,0:T(8,128)S(1)}, u32[]{:S(2)}, u32[]{:S(2)}) collective-permute-start(f32[512,128]{1,0:T(8,128)} %get-tuple-element.27.sx1), channel_id=1, source_target_pairs={{0,32},{32,64},{64,96},{1,33},{33,65},{65,97},{2,34},{34,66},{66,9... | collective-permute-start | bytes 786440 | tf_op jit(solution)/shard_map/ppermute | solution.py:507
  24.4 27.3 %collective-permute-start.1 = (f32[512,128]{1,0:T(8,128)S(1)}, f32[512,128]{1,0:T(8,128)S(1)}, u32[]{:S(2)}, u32[]{:S(2)}) collective-permute-start(f32[512,128]{1,0:T(8,128)S(1)} %copy-done.12), channel_id=1, source_target_pairs={{32,0},{64,32},{96,64},{33,1},{65,33},{97,65},{34,2},{66,34},{98,6... | collective-permute-start | bytes 786440 | tf_op jit(solution)/shard_map/ppermute | solution.py:512
  25.7 26.0 %collective-permute-start.2 = (f32[512,128]{1,0:T(8,128)}, f32[512,128]{1,0:T(8,128)S(1)}, u32[]{:S(2)}, u32[]{:S(2)}) collective-permute-start(f32[512,128]{1,0:T(8,128)} %get-tuple-element.29.sy1), channel_id=1, source_target_pairs={{0,1},{1,2},{2,3},{3,4},{4,5},{5,6},{6,7},{7,8},{8,9},{9,10},{10,1... | collective-permute-start | bytes 786440 | tf_op jit(solution)/shard_map/ppermute | solution.py:507
  29.4 22.3 %collective-permute-start.3 = (f32[512,128]{1,0:T(8,128)}, f32[512,128]{1,0:T(8,128)S(1)}, u32[]{:S(2)}, u32[]{:S(2)}) collective-permute-start(f32[512,128]{1,0:T(8,128)} %get-tuple-element.28.sy0), channel_id=1, source_target_pairs={{1,0},{2,1},{3,2},{4,3},{5,4},{6,5},{7,6},{8,7},{9,8},{10,9},{11,1... | collective-permute-start | bytes 786440 | tf_op jit(solution)/shard_map/ppermute | solution.py:512
  31.3 23.9 %copy-start = (s32[16384]{0:T(1024)S(1)}, s32[16384]{0:T(1024)}, u32[]{:S(2)}) copy-start(s32[16384]{0:T(1024)} %param.12) | copy-start | bytes 196612
  31.3 23.9 %copy-start.1 = (f32[16,128]{1,0:T(8,128)S(1)}, f32[16,128]{1,0:T(8,128)}, u32[]{:S(2)}) copy-start(f32[16,128]{1,0:T(8,128)} %refs_8_.1) | copy-start | bytes 24580
  31.4 23.9 %copy-start.2 = (f32[256]{0:T(256)S(1)}, f32[256]{0:T(256)}, u32[]{:S(2)}) copy-start(f32[256]{0:T(256)} %param.16) | copy-start | bytes 3076
  31.4 23.9 %copy-start.3 = (f32[256]{0:T(256)S(1)}, f32[256]{0:T(256)}, u32[]{:S(2)}) copy-start(f32[256]{0:T(256)} %param.17) | copy-start | bytes 3076
  49.7 2.1 %copy-start.4 = (f32[512,128]{1,0:T(8,128)}, f32[512,128]{1,0:T(8,128)S(1)}, u32[]{:S(2)}) copy-start(f32[512,128]{1,0:T(8,128)S(1)} %collective-permute-done.xlo) | copy-start | bytes 786436
  51.7 0.7 copy-start.5
  51.7 0.8 copy-start.6
  51.7 0.8 copy-start.7
  55.2 14.2 %copy-start.11 = (f32[256,128]{1,0:T(8,128)S(1)}, f32[256,128]{1,0:T(8,128)}, u32[]{:S(2)}) copy-start(f32[256,128]{1,0:T(8,128)} %get-tuple-element.36.refs_1_.fx1) | copy-start | bytes 393220
  55.2 17.6 %copy-start.10 = (f32[256,128]{1,0:T(8,128)S(1)}, f32[256,128]{1,0:T(8,128)}, u32[]{:S(2)}) copy-start(f32[256,128]{1,0:T(8,128)} %get-tuple-element.35.refs_0_.fx0) | copy-start | bytes 393220
  55.2 18.9 %copy-start.9 = (f32[256,128]{1,0:T(8,128)S(1)}, f32[256,128]{1,0:T(8,128)}, u32[]{:S(2)}) copy-start(f32[256,128]{1,0:T(8,128)} %get-tuple-element.38.refs_3_.fy1) | copy-start | bytes 393220
  55.2 22.6 %copy-start.8 = (f32[256,128]{1,0:T(8,128)S(1)}, f32[256,128]{1,0:T(8,128)}, u32[]{:S(2)}) copy-start(f32[256,128]{1,0:T(8,128)} %get-tuple-element.37.refs_2_.fy0) | copy-start | bytes 393220
  60.5 39.1 %all-to-all-start.1 = ((f32[128,32,128]{2,1,0:T(8,128)}), f32[128,32,128]{2,1,0:T(8,128)S(1)}, u32[]{:S(2)}, u32[]{:S(2)}) async-start(f32[128,32,128]{2,1,0:T(8,128)} %bitcast.49), calls=%async_computation.1 | async-start | bytes 4194304 | tf_op jit(solution)/shard_map/all_to_all | solution.py:532
  69.4 25.1 %collective-permute-start.4 = (f32[256,128]{1,0:T(8,128)S(1)}, f32[256,128]{1,0:T(8,128)S(1)}, u32[]{:S(2)}, u32[]{:S(2)}) collective-permute-start(f32[256,128]{1,0:T(8,128)S(1)} %copy-done.11), channel_id=1, source_target_pairs={{0,32},{32,64},{64,96},{1,33},{33,65},{65,97},{2,34},{34,66},{66,9... | collective-permute-start | bytes 393224 | tf_op jit(solution)/shard_map/ppermute | solution.py:507
  72.9 23.8 %collective-permute-start.5 = (f32[256,128]{1,0:T(8,128)S(1)}, f32[256,128]{1,0:T(8,128)S(1)}, u32[]{:S(2)}, u32[]{:S(2)}) collective-permute-start(f32[256,128]{1,0:T(8,128)S(1)} %copy-done.10), channel_id=1, source_target_pairs={{32,0},{64,32},{96,64},{33,1},{65,33},{97,65},{34,2},{66,34},{98,6... | collective-permute-start | bytes 393224 | tf_op jit(solution)/shard_map/ppermute | solution.py:512
  74.2 22.5 %collective-permute-start.6 = (f32[256,128]{1,0:T(8,128)S(1)}, f32[256,128]{1,0:T(8,128)S(1)}, u32[]{:S(2)}, u32[]{:S(2)}) collective-permute-start(f32[256,128]{1,0:T(8,128)S(1)} %copy-done.9), channel_id=1, source_target_pairs={{0,1},{1,2},{2,3},{3,4},{4,5},{5,6},{6,7},{7,8},{8,9},{9,10},{10,1... | collective-permute-start | bytes 393224 | tf_op jit(solution)/shard_map/ppermute | solution.py:507
  77.9 18.8 %collective-permute-start.7 = (f32[256,128]{1,0:T(8,128)S(1)}, f32[256,128]{1,0:T(8,128)S(1)}, u32[]{:S(2)}, u32[]{:S(2)}) collective-permute-start(f32[256,128]{1,0:T(8,128)S(1)} %copy-done.8), channel_id=1, source_target_pairs={{1,0},{2,1},{3,2},{4,3},{5,4},{6,5},{7,6},{8,7},{9,8},{10,9},{11,1... | collective-permute-start | bytes 393224 | tf_op jit(solution)/shard_map/ppermute | solution.py:512
  94.5 5.1 %copy-start.13 = (f32[256,128]{1,0:T(8,128)}, f32[256,128]{1,0:T(8,128)S(1)}, u32[]{:S(2)}) copy-start(f32[256,128]{1,0:T(8,128)S(1)} %collective-permute-done.4.xlo) | copy-start | bytes 393220
  96.7 3.0 %copy-start.14 = (f32[256,128]{1,0:T(8,128)}, f32[256,128]{1,0:T(8,128)S(1)}, u32[]{:S(2)}) copy-start(f32[256,128]{1,0:T(8,128)S(1)} %collective-permute-done.5.xhi) | copy-start | bytes 393220
  96.7 3.0 %copy-start.15 = (f32[256,128]{1,0:T(8,128)}, f32[256,128]{1,0:T(8,128)S(1)}, u32[]{:S(2)}) copy-start(f32[256,128]{1,0:T(8,128)S(1)} %collective-permute-done.6.ylo) | copy-start | bytes 393220
  96.7 3.0 %copy-start.16 = (f32[256,128]{1,0:T(8,128)}, f32[256,128]{1,0:T(8,128)S(1)}, u32[]{:S(2)}) copy-start(f32[256,128]{1,0:T(8,128)S(1)} %collective-permute-done.7.yhi) | copy-start | bytes 393220

commit v3 on v2

--- a/solution.py
+++ b/solution.py
@@ -62,14 +62,9 @@
     return ref.at[pl.ds(aligned(k * SPAN + shift, 8), SPAN)]
 
 
-def gather_kernel(rows, u, c, out, at, sx0, sx1, sy0, sy1, block, made, sides, at_v, sems, done, extra):
-    loads = [pltpu.make_async_copy(piece(u, k), piece(block, k), sems.at[k]) for k in range(PARTS)]
-    lines = [pltpu.make_async_copy(a, b, extra.at[n]) for n, (a, b) in enumerate((
-        (c.at[:, pl.ds(0, 64)], sides.at[:, pl.ds(0, 64)]),
-        (c.at[:, pl.ds(192, 64)], sides.at[:, pl.ds(192, 64)]),
-        (c.at[0, pl.ds(64, 128)], sides.at[0, pl.ds(64, 128)]),
-        (c.at[LINES - 1, pl.ds(64, 128)], sides.at[LINES - 1, pl.ds(64, 128)])))]
-    for load in loads + lines:
+def gather_kernel(rows, src, out, at, block, made, at_v, sems, done):
+    loads = [pltpu.make_async_copy(piece(src, k), piece(block, k), sems.at[k]) for k in range(PARTS)]
+    for load in loads:
         load.start()
     at_v[...] = place_in_tiles(rows[...])
     listed = pltpu.make_async_copy(at_v, at, sems.at[PARTS])
@@ -99,70 +94,90 @@
         return 0
 
     lax.fori_loop(0, PARTS, step, 0)
-    for load in lines:
-        load.wait()
-    for n in range(LINES):
-        row = pl.ds(n * LINE, LINE)
-        below = pl.ds(PLANE + n * LINE, LINE)
-        for ref, x, y in ((sx0, 0, n), (sx1, LINES - 1, n), (sy0, n, 0), (sy1, n, LINES - 1)):
-            ref[row, :] = block[tiled_line(x, y), :]
-            ref[below, :] = sides[x, pl.ds((y // 8) * 64 + y % 8, LINE, stride=8), :]
     for k in range(PARTS):
         save(k).wait()
 
 
-def gather(rows, u, c):
+def gather(rows, src):
     n = rows.shape[0] * 128
     return pl.pallas_call(
-        gather_kernel, out_shape=(shape(n), pltpu.SMEM(rows.shape, jnp.int32)) + (shape(2 * PLANE),) * 4,
-        in_specs=[VM, ANY, ANY], out_specs=(ANY, SM) + (VM,) * 4,
-        scratch_shapes=[pltpu.VMEM((ROWS, 128), F32), pltpu.VMEM((n, 128), F32), pltpu.VMEM((LINES, PLANE, 128), F32),
+        gather_kernel, out_shape=(shape(n), pltpu.SMEM(rows.shape, jnp.int32)),
+        in_specs=[VM, ANY], out_specs=(ANY, SM),
+        scratch_shapes=[pltpu.VMEM((ROWS, 128), F32), pltpu.VMEM((n, 128), F32),
                         pltpu.VMEM(rows.shape, jnp.int32), pltpu.SemaphoreType.DMA((PARTS + 1,)),
-                        pltpu.SemaphoreType.DMA((PARTS,)), pltpu.SemaphoreType.DMA((4,))],
+                        pltpu.SemaphoreType.DMA((PARTS,))],
         compiler_params=PARAMS, name="gather_rows",
-    )(rows, *in_hbm(u, c.reshape(LINES, PLANE, 128)))
-
-
-def finish_kernel(at, flux, src, kx0, kx1, ky0, ky1, xlo, xhi, ylo, yhi, out, block, sides, sems, beside):
+    )(rows, *in_hbm(src))
+
+
+def finish_kernel(at, flux, src, kx0, kx1, ky0, ky1, xlo, xhi, ylo, yhi, out, block, sink, sides, sems, beside):
     loads = [pltpu.make_async_copy(piece(src, k), piece(block, k), sems.at[k]) for k in range(PARTS)]
     extra = [pltpu.make_async_copy(a, sides.at[n], beside.at[n])
              for n, a in enumerate((kx0, kx1, ky0, ky1, xlo, xhi, ylo, yhi))]
     for load in loads + extra:
         load.start()
-    for load in loads:
-        load.wait()
+
+    def clear(n, _):
+        sink[pl.ds(aligned(n * PLANE, PLANE), PLANE), :] = jnp.zeros((PLANE, 128), F32)
+        return 0
+
+    lax.fori_loop(0, LINES, clear, 0)
 
     def group(g, _):
         base = aligned(g * 128, 128)
         for first in range(0, 128, 16):
             where = [at[g, first + n] for n in range(16)]
-            new = [block[pl.ds(t, 1), :] - flux[pl.ds(base + (first + n), 1), :] for n, t in enumerate(where)]
-            for t, v in zip(where, new):
-                block[pl.ds(t, 1), :] = v
+            rows = [flux[pl.ds(base + (first + n), 1), :] for n in range(16)]
+            for t, v in zip(where, rows):
+                sink[pl.ds(t, 1), :] = v
         return 0
 
     lax.fori_loop(0, at.shape[0], group, 0)
-    for load in extra:
+    for load in loads + extra:
         load.wait()
     for n in range(LINES):
         line = plain_line(0, n)
         for side, place in enumerate((tiled_line(0, n), tiled_line(LINES - 1, n),
                                       tiled_line(n, 0), tiled_line(n, LINES - 1))):
             block[place, :] = block[place, :] + sides[side, line, :] * sides[side + 4, line, :]
-    saves = [pltpu.make_async_copy(piece(block, k), piece(out, k), sems.at[k]) for k in range(PARTS)]
-    for save in saves:
-        save.start()
-    for save in saves:
-        save.wait()
+
+    def save(k):
+        return pltpu.make_async_copy(piece(block, k), piece(out, k), sems.at[k])
+
+    def step(k, _):
+        def plane(i, _):
+            part = pl.ds(aligned(k * SPAN + i * PLANE, PLANE), PLANE)
+            block[part, :] = block[part, :] - sink[part, :]
+            return 0
+
+        lax.fori_loop(0, SPAN // PLANE, plane, 0)
+        save(k).start()
+        return 0
+
+    lax.fori_loop(0, PARTS, step, 0)
+    for k in range(PARTS):
+        save(k).wait()
 
 
 def finish(at, flux, src, gains, halos):
     return pl.pallas_call(
         finish_kernel, out_shape=shape(ROWS), in_specs=[SM, VM] + [ANY] * 9, out_specs=ANY,
-        scratch_shapes=[pltpu.VMEM((ROWS, 128), F32), pltpu.VMEM((8, PLANE, 128), F32),
+        scratch_shapes=[pltpu.VMEM((ROWS, 128), F32), pltpu.VMEM((ROWS, 128), F32), pltpu.VMEM((8, PLANE, 128), F32),
                         pltpu.SemaphoreType.DMA((PARTS,)), pltpu.SemaphoreType.DMA((8,))],
         compiler_params=SMALL, name="subtract_rows",
     )(*in_smem(at), flux, *in_hbm(src, *gains, *halos))
+
+
+def tie_kernel(*refs):
+    pass
+
+
+def after_all(array, others):
+    n = len(others)
+    return pl.pallas_call(
+        tie_kernel, out_shape=pltpu.HBM(array.shape, array.dtype), in_specs=[ANY] * (n + 1), out_specs=ANY,
+        input_output_aliases={n: 0}, compiler_params=SMALL, name="tie",
+    )(*others, *in_hbm(array))
 
 
 def step_up(a, edge, corner, fill):
@@ -235,7 +250,7 @@
         ref[pl.ds(PLANE + ROWS, PLANE), :] = jnp.zeros((PLANE, 128), F32)
 
 
-def first_kernel(after, u, c, p, out, gain, nx0, nx1, ny0, ny1, us, cs, ps, vs, gs, nx, sems, done):
+def first_kernel(after, u, c, p, out, gain, sx0, sx1, sy0, sy1, nx0, nx1, ny0, ny1, us, cs, ps, vs, gs, nx, sems, done):
     del after
 
     def loads(k):
@@ -278,6 +293,11 @@
         put(nx, lax.div(x, LINES - 1) * (2 * PLANE) + y * LINE, numer, denom)
 
     both_sides(lambda x: relax_plane(x, load_u, load_c, load_p, store_x, True))
+    for n in range(LINES):
+        row, below = pl.ds(n * LINE, LINE), pl.ds(PLANE + n * LINE, LINE)
+        for ref, x, y in ((sx0, 0, n), (sx1, LINES - 1, n), (sy0, n, 0), (sy1, n, LINES - 1)):
+            ref[row, :] = load_u(x, y)
+            ref[below, :] = load_c(x, y)
     nx0[...] = nx[pl.ds(0, 2 * PLANE), :]
     nx1[...] = nx[pl.ds(2 * PLANE, 2 * PLANE), :]
     for k in range(PARTS):
@@ -287,8 +307,8 @@
 
 def sweep_first(after, u, c, p):
     return pl.pallas_call(
-        first_kernel, out_shape=(shape(ROWS),) * 2 + (shape(2 * PLANE),) * 4,
-        in_specs=[ANY] * 4, out_specs=(ANY,) * 2 + (VM,) * 4,
+        first_kernel, out_shape=(shape(ROWS),) * 2 + (shape(2 * PLANE),) * 8,
+        in_specs=[ANY] * 4, out_specs=(ANY,) * 2 + (VM,) * 8,
         scratch_shapes=[pltpu.VMEM((ROWS + 2 * PLANE, 128), F32), pltpu.VMEM((ROWS + 2 * PLANE, 128), F32),
                         pltpu.VMEM((ROWS, 128), F32), pltpu.VMEM((ROWS, 128), F32), pltpu.VMEM((ROWS, 128), F32),
                         pltpu.VMEM((4 * PLANE, 128), F32),
@@ -297,7 +317,9 @@
     )(*in_hbm(after, u, c, p))
 
 
-def sides_kernel(sx0, sx1, sy0, sy1, nx0, nx1, ny0, ny1, xlo, xhi, ylo, yhi, fx0, fx1, fy0, fy1):
+def sides_kernel(after, sx0, sx1, sy0, sy1, nx0, nx1, ny0, ny1, xlo, xhi, ylo, yhi, fx0, fx1, fy0, fy1):
+    del after
+
     def part(ref, start=0):
         return ref[pl.ds(start, PLANE), :]
 
@@ -320,11 +342,11 @@
             ref[pl.ds(rows, 8), :] = n / d
 
 
-def fix_sides(parts, halos):
+def fix_sides(after, parts, halos):
     return pl.pallas_call(
-        sides_kernel, out_shape=(shape(PLANE),) * 4, in_specs=[VM] * 12, out_specs=(VM,) * 4,
+        sides_kernel, out_shape=(shape(PLANE),) * 4, in_specs=[ANY] + [VM] * 12, out_specs=(VM,) * 4,
         compiler_params=PARAMS, name="sweep_first_sides",
-    )(*parts, *halos)
+    )(*in_hbm(after), *parts, *halos)
 
 
 def second_kernel(after, u, c, p, gain, fx0, fx1, fy0, fy1, xlo, xhi, ylo, yhi, out, kx0, kx1, ky0, ky1,
@@ -520,17 +542,18 @@
     slots = channel_coef.shape[0]
     u, c, p = tiles(solid_temp), tiles(conduct), tiles(power)
 
-    sent, at, *ends = gather(wall_rows.reshape(-1, 128), u, c)
+    sent, at = gather(wall_rows.reshape(-1, 128), u)
     arrived = lax.all_to_all(sent.reshape(devices, -1, 128), both, 0, 0, tiled=True)
 
-    halos = (up(ends[1], "gx"), down(ends[0], "gx"), up(ends[3], "gy"), down(ends[2], "gy"))
-    once, gain, *sums = sweep_first(sent, u, c, p)
-    faces = fix_sides((*ends, *sums), halos)
-
-    fluid, flux = channel(faces, me, channel_owner.reshape(-1, 128), arrived, span_prop, span_carry,
+    once, gain, *parts = sweep_first(sent, u, c, p)
+    halos = (up(parts[1], "gx"), down(parts[0], "gx"), up(parts[3], "gy"), down(parts[2], "gy"))
+
+    fluid, flux = channel((once,), me, channel_owner.reshape(-1, 128), arrived, span_prop, span_carry,
                           channel_coef, channel_inlet)
+    flux = after_all(flux, halos)
     returned = lax.all_to_all(flux.reshape(devices, -1, 128), both, 0, 0, tiled=True)
 
+    faces = fix_sides(flux, parts, halos)
     outer = (up(faces[1], "gx"), down(faces[0], "gx"), up(faces[3], "gy"), down(faces[2], "gy"))
     twice, *gains = sweep_second(flux, once, c, p, gain, faces, halos)
     solid_out = finish(at, returned.reshape(-1, 128), twice, gains, outer)

time: 110 us -> 99.2 us (0.902)
  Pallas kernels: 55.4 us -> 49.8 us
  waiting for transfers between devices: 11.5 us -> 7.39 us
  starting transfers between devices: 41.1 us -> 39.5 us
    all_to_all x1, waiting for transfers between devices: 0.01 us -> 5.93 us  [local(): lax.all_to_all(sent.reshape(devices, -1, 128), both, 0, 0, tiled=True)]
    ppermute x4, waiting for transfers between devices: 4.4 us -> 0.01 us  [up(): return lax.ppermute(a, axis, [(i, i + 1) for i in range(n - 1)])]
    ppermute x4, waiting for transfers between devices: 4.17 us -> 0.01 us  [down(): return lax.ppermute(a, axis, [(i + 1, i) for i in range(n - 1)])]
    pallas_call x1, Pallas kernels: 10.2 us -> 6.1 us  [finish(): pl.pallas_call(finish_kernel, out_shape=shape(ROWS), in_specs=[SM, VM] +...]
    all_to_all x1, starting transfers between devices: 8.91 us -> 6.37 us  [local(): lax.all_to_all(flux.reshape(devices, -1, 128), both, 0, 0, tiled=True)]
    pallas_call x1, Pallas kernels: 8.81 us -> 7.12 us  [gather(): pl.pallas_call(gather_kernel, out_shape=(shape(n), pltpu.SMEM(rows.shape,...]
    ppermute x4, starting transfers between devices: 6.42 us -> 7.97 us  [down(): return lax.ppermute(a, axis, [(i + 1, i) for i in range(n - 1)])]
    all_to_all x1, waiting for transfers between devices: 2.94 us -> 1.44 us  [local(): lax.all_to_all(flux.reshape(devices, -1, 128), both, 0, 0, tiled=True)]
  transfers between devices with their start and end apart: 10 -> 10, of which waited for: 4 -> 2; matrix products, arithmetic and copies ran while one was open for 0% -> 0% of each run, Pallas kernels for 28% -> 37%
where the time goes in v3:
time: 99.2 us; the launch traced here: 98.6 us
  Pallas kernels  49.8 us (50%)
  starting transfers between devices  39.5 us (40%)
  waiting for transfers between devices  7.39 us (7%)
    pallas_call x1, Pallas kernels, sweep_second(): pl.pallas_call(second_kernel, out_shape=(shape(ROWS),) + (shape(PLANE),)...  14.7 us
    pallas_call x1, Pallas kernels, sweep_first(): pl.pallas_call(first_kernel, out_shape=(shape(ROWS),) * 2 + (shape(2 * PL...  14.2 us
    ppermute x4, starting transfers between devices, up(): return lax.ppermute(a, axis, [(i, i + 1) for i in range(n - 1)])  13.6 us
    all_to_all x1, starting transfers between devices, local(): lax.all_to_all(sent.reshape(devices, -1, 128), both, 0, 0, tiled=True)  11.5 us
    ppermute x4, starting transfers between devices, down(): return lax.ppermute(a, axis, [(i + 1, i) for i in range(n - 1)])  7.97 us
    pallas_call x1, Pallas kernels, gather(): pl.pallas_call(gather_kernel, out_shape=(shape(n), pltpu.SMEM(rows.shape,...  7.12 us
    all_to_all x1, starting transfers between devices, local(): lax.all_to_all(flux.reshape(devices, -1, 128), both, 0, 0, tiled=True)  6.37 us
    pallas_call x1, Pallas kernels, finish(): pl.pallas_call(finish_kernel, out_shape=shape(ROWS), in_specs=[SM, VM] +...  6.1 us
  transfers between devices with their start and end apart: 10, of which 2 were waited for; matrix products, arithmetic and copies ran while one was open for 0% of the time, Pallas kernels for 37%

profile of v3, /device:TPU:1, one launch (start us, length us, event | category | flops | bytes accessed | tf_op | source)
XLA Modules:
  0.0 98.6 jit_solution(12081328755791215084)
XLA Ops:
  0.6 7.1 %gather_rows.1 = (f32[4096,128]{1,0:T(8,128)}, s32[32,128]{1,0:T(8,128)S(4)}) custom-call(s32[32,128]{1,0:T(8,128)} %bitcast.48, f32[8192,128]{1,0:T(8,128)} %bitcast.44), custom_call_target="tpu_custom_call" | custom-call | tf_op jit(solution)/shard_map/gather_rows/pallas_call | solution.py:103
  7.8 11.5 %all-to-all-start = ((f32[128,32,128]{2,1,0:T(8,128)}), f32[128,32,128]{2,1,0:T(8,128)S(1)}, u32[]{:S(2)}, u32[]{:S(2)}) async-start(f32[128,32,128]{2,1,0:T(8,128)} %bitcast.46), calls=%async_computation | async-start | bytes 4194304 | tf_op jit(solution)/shard_map/all_to_all | solution.py:546
  19.3 0.0 copy-start.4
  19.3 0.0 copy-start.5
  19.3 0.0 copy-start.6
  19.3 0.0 copy-start.7
  19.3 14.2 %sweep_first.1 = (f32[8192,128]{1,0:T(8,128)}, f32[8192,128]{1,0:T(8,128)}, f32[512,128]{1,0:T(8,128)}, f32[512,128]{1,0:T(8,128)}, f32[512,128]{1,0:T(8,128)}, ...) custom-call(f32[4096,128]{1,0:T(8,128)} %get-tuple-element.26.after,, ...), custom_call_target="tpu_custom_call" | custom-call | tf_op jit(solution)/shard_map/sweep_first/pallas_call | solution.py:309
  33.5 3.4 %collective-permute-start = (f32[512,128]{1,0:T(8,128)}, f32[512,128]{1,0:T(8,128)S(1)}, u32[]{:S(2)}, u32[]{:S(2)}) collective-permute-start(f32[512,128]{1,0:T(8,128)} %get-tuple-element.27.sx1), channel_id=1, source_target_pairs={{0,32},{32,64},{64,96},{1,33},{33,65},{65,97},{2,34},{34,66},{66,9... | collective-permute-start | bytes 786440 | tf_op jit(solution)/shard_map/ppermute | solution.py:529
  36.9 1.3 %collective-permute-start.1 = (f32[512,128]{1,0:T(8,128)}, f32[512,128]{1,0:T(8,128)S(1)}, u32[]{:S(2)}, u32[]{:S(2)}) collective-permute-start(f32[512,128]{1,0:T(8,128)} %get-tuple-element.28.sx0), channel_id=1, source_target_pairs={{32,0},{64,32},{96,64},{33,1},{65,33},{97,65},{34,2},{66,34},{98,6... | collective-permute-start | bytes 786440 | tf_op jit(solution)/shard_map/ppermute | solution.py:534
  38.2 3.7 %collective-permute-start.2 = (f32[512,128]{1,0:T(8,128)}, f32[512,128]{1,0:T(8,128)S(1)}, u32[]{:S(2)}, u32[]{:S(2)}) collective-permute-start(f32[512,128]{1,0:T(8,128)} %get-tuple-element.29.sy1), channel_id=1, source_target_pairs={{0,1},{1,2},{2,3},{3,4},{4,5},{5,6},{6,7},{7,8},{8,9},{9,10},{10,1... | collective-permute-start | bytes 786440 | tf_op jit(solution)/shard_map/ppermute | solution.py:529
  41.9 1.9 %collective-permute-start.3 = (f32[512,128]{1,0:T(8,128)}, f32[512,128]{1,0:T(8,128)S(1)}, u32[]{:S(2)}, u32[]{:S(2)}) collective-permute-start(f32[512,128]{1,0:T(8,128)} %get-tuple-element.30.sy0), channel_id=1, source_target_pairs={{1,0},{2,1},{3,2},{4,3},{5,4},{6,5},{7,6},{8,7},{9,8},{10,9},{11,1... | collective-permute-start | bytes 786440 | tf_op jit(solution)/shard_map/ppermute | solution.py:534
  43.9 5.9 %all-to-all-done = f32[128,32,128]{2,1,0:T(8,128)S(1)} async-done(((f32[128,32,128]{2,1,0:T(8,128)}), f32[128,32,128]{2,1,0:T(8,128)S(1)}, u32[]{:S(2)}, u32[]{:S(2)}) %all-to-all-start) | async-done | bytes 2097184 | tf_op jit(solution)/shard_map/all_to_all | solution.py:546
  49.8 0.0 copy-done.4
  49.8 0.0 copy-done.5
  49.8 0.0 copy-done.6
  49.8 0.0 copy-done.7
  49.8 5.1 %channel_march.1 = (f32[32,128,128]{2,1,0:T(8,128)}, f32[8,512,128]{2,1,0:T(8,128)}) custom-call(f32[8192,128]{1,0:T(8,128)} %get-tuple-element.31.refs_0_.u, s32[1]{0:T(128)} %bitcast.12.refs_1_, s32[128,128]{1,0:T(8,128)S(1)} %bitcast.36, f32[8,512,128]{2,1,0:T(8,128)S(1)} %bitcast.34, f32[16,128,128]{2,1,0:T(8,128)} %refs_4_.1, f32[16,128]{1,0:T(8,128)S(1)} %copy-done.5, ...), custom_call_target="tpu_custom_call" | custom-call | tf_op jit(solution)/shard_map/channel_march/pallas_call | solution.py:511
  54.9 0.0 collective-permute-done.refs_0_.xlo
  54.9 0.0 copy-start
  54.9 0.0 collective-permute-done.1.refs_1_.xhi
  54.9 0.0 copy-start.1
  54.9 0.0 collective-permute-done.2.refs_2_.ylo
  54.9 0.0 copy-start.2
  54.9 0.0 collective-permute-done.3.refs_3_.yhi
  54.9 0.0 copy-start.3
  55.0 0.6 copy-done
  55.6 0.1 copy-done.1
  55.7 0.1 copy-done.2
  55.8 0.1 copy-done.3
  55.9 6.4 %all-to-all-start.1 = ((f32[128,32,128]{2,1,0:T(8,128)}), f32[128,32,128]{2,1,0:T(8,128)S(1)}, u32[]{:S(2)}, u32[]{:S(2)}) async-start(f32[128,32,128]{2,1,0:T(8,128)} %bitcast.39), calls=%async_computation.1 | async-start | bytes 4194304 | tf_op jit(solution)/shard_map/all_to_all | solution.py:554
  62.2 2.7 %sweep_first_sides.1 = (f32[256,128]{1,0:T(8,128)}, f32[256,128]{1,0:T(8,128)}, f32[256,128]{1,0:T(8,128)}, f32[256,128]{1,0:T(8,128)}) custom-call(f32[8,512,128]{2,1,0:T(8,128)} %tie.1.after, f32[512,128]{1,0:T(8,128)} %get-tuple-element.28.sx0, f32[512,128]{1,0:T(8,128)} %get-tuple-element.27.sx1, f32[512,128]{1,0:T(8,128)} %get-tuple-element.30.sy0, ...), custom_call_target="tpu_custom_call" | custom-call | tf_op jit(solution)/shard_map/sweep_first_sides/pallas_call | solution.py:346
  64.9 1.3 %collective-permute-start.5 = (f32[256,128]{1,0:T(8,128)}, f32[256,128]{1,0:T(8,128)S(1)}, u32[]{:S(2)}, u32[]{:S(2)}) collective-permute-start(f32[256,128]{1,0:T(8,128)} %get-tuple-element.38.fx0), channel_id=1, source_target_pairs={{32,0},{64,32},{96,64},{33,1},{65,33},{97,65},{34,2},{66,34},{98,6... | collective-permute-start | bytes 393224 | tf_op jit(solution)/shard_map/ppermute | solution.py:534
  66.2 4.0 %collective-permute-start.4 = (f32[256,128]{1,0:T(8,128)}, f32[256,128]{1,0:T(8,128)S(1)}, u32[]{:S(2)}, u32[]{:S(2)}) collective-permute-start(f32[256,128]{1,0:T(8,128)} %get-tuple-element.39.fx1), channel_id=1, source_target_pairs={{0,32},{32,64},{64,96},{1,33},{33,65},{65,97},{2,34},{34,66},{66,9... | collective-permute-start | bytes 393224 | tf_op jit(solution)/shard_map/ppermute | solution.py:529
  70.2 3.5 %collective-permute-start.7 = (f32[256,128]{1,0:T(8,128)}, f32[256,128]{1,0:T(8,128)S(1)}, u32[]{:S(2)}, u32[]{:S(2)}) collective-permute-start(f32[256,128]{1,0:T(8,128)} %get-tuple-element.40.fy0), channel_id=1, source_target_pairs={{1,0},{2,1},{3,2},{4,3},{5,4},{6,5},{7,6},{8,7},{9,8},{10,9},{11,1... | collective-permute-start | bytes 393224 | tf_op jit(solution)/shard_map/ppermute | solution.py:534
  73.7 2.5 %collective-permute-start.6 = (f32[256,128]{1,0:T(8,128)}, f32[256,128]{1,0:T(8,128)S(1)}, u32[]{:S(2)}, u32[]{:S(2)}) collective-permute-start(f32[256,128]{1,0:T(8,128)} %get-tuple-element.41.fy1), channel_id=1, source_target_pairs={{0,1},{1,2},{2,3},{3,4},{4,5},{5,6},{6,7},{7,8},{8,9},{9,10},{10,1... | collective-permute-start | bytes 393224 | tf_op jit(solution)/shard_map/ppermute | solution.py:529
  76.2 14.7 %sweep_second.1 = (f32[8192,128]{1,0:T(8,128)}, f32[256,128]{1,0:T(8,128)}, f32[256,128]{1,0:T(8,128)}, f32[256,128]{1,0:T(8,128)}, f32[256,128]{1,0:T(8,128)}) custom-call(f32[8,512,128]{2,1,0:T(8,128)} %tie.1.after, f32[8192,128]{1,0:T(8,128)} %get-tuple-element.31.refs_0_.u, f32[8192,128]{1,0:T(8,128)} %bitcast.41, f32[8192,128]{1,0:T(8,128)} %bitcast.43, ...), custom_call_target="tpu_custom_call" | custom-call | tf_op jit(solution)/shard_map/sweep_second/pallas_call | solution.py:427
  90.9 0.0 collective-permute-done.5.xhi
  90.9 0.0 copy-start.8
  91.0 0.0 collective-permute-done.4.xlo
  91.0 0.0 copy-start.9
  91.0 0.0 collective-permute-done.7.yhi
  91.0 0.0 copy-start.10
  91.0 0.0 collective-permute-done.6.ylo
  91.0 0.0 copy-start.11
  91.0 1.4 %all-to-all-done.1 = f32[128,32,128]{2,1,0:T(8,128)S(1)} async-done(((f32[128,32,128]{2,1,0:T(8,128)}), f32[128,32,128]{2,1,0:T(8,128)S(1)}, u32[]{:S(2)}, u32[]{:S(2)}) %all-to-all-start.1) | async-done | bytes 2097184 | tf_op jit(solution)/shard_map/all_to_all | solution.py:554
  92.5 0.0 copy-done.8
  92.5 0.0 copy-done.9
  92.5 6.1 %subtract_rows.1 = f32[8192,128]{1,0:T(8,128)} custom-call(s32[32,128]{1,0:T(8,128)S(4)} %get-tuple-element.25.at, f32[4096,128]{1,0:T(8,128)S(1)} %bitcast.35, f32[8192,128]{1,0:T(8,128)} %get-tuple-element.42.src, f32[256,128]{1,0:T(8,128)} %get-tuple-element.43.kx0, f32[256,128]{1,0:T(8,128)} %get-tuple-element.44.kx1, f32[256,128]{1,0:T(8,128)} %get-tuple-element.45.ky0, ...), custom_call_target="tpu_custom_call" | custom-call | tf_op jit(solution)/shard_map/subtract_rows/pallas_call | solution.py:163
  (3 shorter events, 0.0 us)
Async XLA Ops:
  7.8 42.0 %all-to-all-start = ((f32[128,32,128]{2,1,0:T(8,128)}), f32[128,32,128]{2,1,0:T(8,128)S(1)}, u32[]{:S(2)}, u32[]{:S(2)}) async-start(f32[128,32,128]{2,1,0:T(8,128)} %bitcast.46), calls=%async_computation | async-start | bytes 4194304 | tf_op jit(solution)/shard_map/all_to_all | solution.py:546
  19.3 30.5 %copy-start.4 = (s32[16384]{0:T(1024)S(1)}, s32[16384]{0:T(1024)}, u32[]{:S(2)}) copy-start(s32[16384]{0:T(1024)} %param.12) | copy-start | bytes 196612
  19.3 30.5 %copy-start.5 = (f32[16,128]{1,0:T(8,128)S(1)}, f32[16,128]{1,0:T(8,128)}, u32[]{:S(2)}) copy-start(f32[16,128]{1,0:T(8,128)} %refs_5_.1) | copy-start | bytes 24580
  19.3 30.5 %copy-start.6 = (f32[256]{0:T(256)S(1)}, f32[256]{0:T(256)}, u32[]{:S(2)}) copy-start(f32[256]{0:T(256)} %param.16) | copy-start | bytes 3076
  19.3 30.5 %copy-start.7 = (f32[256]{0:T(256)S(1)}, f32[256]{0:T(256)}, u32[]{:S(2)}) copy-start(f32[256]{0:T(256)} %param.17) | copy-start | bytes 3076
  33.5 21.4 %collective-permute-start = (f32[512,128]{1,0:T(8,128)}, f32[512,128]{1,0:T(8,128)S(1)}, u32[]{:S(2)}, u32[]{:S(2)}) collective-permute-start(f32[512,128]{1,0:T(8,128)} %get-tuple-element.27.sx1), channel_id=1, source_target_pairs={{0,32},{32,64},{64,96},{1,33},{33,65},{65,97},{2,34},{34,66},{66,9... | collective-permute-start | bytes 786440 | tf_op jit(solution)/shard_map/ppermute | solution.py:529
  36.9 18.0 %collective-permute-start.1 = (f32[512,128]{1,0:T(8,128)}, f32[512,128]{1,0:T(8,128)S(1)}, u32[]{:S(2)}, u32[]{:S(2)}) collective-permute-start(f32[512,128]{1,0:T(8,128)} %get-tuple-element.28.sx0), channel_id=1, source_target_pairs={{32,0},{64,32},{96,64},{33,1},{65,33},{97,65},{34,2},{66,34},{98,6... | collective-permute-start | bytes 786440 | tf_op jit(solution)/shard_map/ppermute | solution.py:534
  38.2 16.7 %collective-permute-start.2 = (f32[512,128]{1,0:T(8,128)}, f32[512,128]{1,0:T(8,128)S(1)}, u32[]{:S(2)}, u32[]{:S(2)}) collective-permute-start(f32[512,128]{1,0:T(8,128)} %get-tuple-element.29.sy1), channel_id=1, source_target_pairs={{0,1},{1,2},{2,3},{3,4},{4,5},{5,6},{6,7},{7,8},{8,9},{9,10},{10,1... | collective-permute-start | bytes 786440 | tf_op jit(solution)/shard_map/ppermute | solution.py:529
  41.9 13.0 %collective-permute-start.3 = (f32[512,128]{1,0:T(8,128)}, f32[512,128]{1,0:T(8,128)S(1)}, u32[]{:S(2)}, u32[]{:S(2)}) collective-permute-start(f32[512,128]{1,0:T(8,128)} %get-tuple-element.30.sy0), channel_id=1, source_target_pairs={{1,0},{2,1},{3,2},{4,3},{5,4},{6,5},{7,6},{8,7},{9,8},{10,9},{11,1... | collective-permute-start | bytes 786440 | tf_op jit(solution)/shard_map/ppermute | solution.py:534
  54.9 0.7 copy-start
  54.9 0.8 copy-start.1
  54.9 0.9 copy-start.2
  54.9 0.9 copy-start.3
  55.9 36.6 %all-to-all-start.1 = ((f32[128,32,128]{2,1,0:T(8,128)}), f32[128,32,128]{2,1,0:T(8,128)S(1)}, u32[]{:S(2)}, u32[]{:S(2)}) async-start(f32[128,32,128]{2,1,0:T(8,128)} %bitcast.39), calls=%async_computation.1 | async-start | bytes 4194304 | tf_op jit(solution)/shard_map/all_to_all | solution.py:554
  64.9 26.0 %collective-permute-start.5 = (f32[256,128]{1,0:T(8,128)}, f32[256,128]{1,0:T(8,128)S(1)}, u32[]{:S(2)}, u32[]{:S(2)}) collective-permute-start(f32[256,128]{1,0:T(8,128)} %get-tuple-element.38.fx0), channel_id=1, source_target_pairs={{32,0},{64,32},{96,64},{33,1},{65,33},{97,65},{34,2},{66,34},{98,6... | collective-permute-start | bytes 393224 | tf_op jit(solution)/shard_map/ppermute | solution.py:534
  66.2 24.8 %collective-permute-start.4 = (f32[256,128]{1,0:T(8,128)}, f32[256,128]{1,0:T(8,128)S(1)}, u32[]{:S(2)}, u32[]{:S(2)}) collective-permute-start(f32[256,128]{1,0:T(8,128)} %get-tuple-element.39.fx1), channel_id=1, source_target_pairs={{0,32},{32,64},{64,96},{1,33},{33,65},{65,97},{2,34},{34,66},{66,9... | collective-permute-start | bytes 393224 | tf_op jit(solution)/shard_map/ppermute | solution.py:529
  70.2 20.7 %collective-permute-start.7 = (f32[256,128]{1,0:T(8,128)}, f32[256,128]{1,0:T(8,128)S(1)}, u32[]{:S(2)}, u32[]{:S(2)}) collective-permute-start(f32[256,128]{1,0:T(8,128)} %get-tuple-element.40.fy0), channel_id=1, source_target_pairs={{1,0},{2,1},{3,2},{4,3},{5,4},{6,5},{7,6},{8,7},{9,8},{10,9},{11,1... | collective-permute-start | bytes 393224 | tf_op jit(solution)/shard_map/ppermute | solution.py:534
  73.7 17.3 %collective-permute-start.6 = (f32[256,128]{1,0:T(8,128)}, f32[256,128]{1,0:T(8,128)S(1)}, u32[]{:S(2)}, u32[]{:S(2)}) collective-permute-start(f32[256,128]{1,0:T(8,128)} %get-tuple-element.41.fy1), channel_id=1, source_target_pairs={{0,1},{1,2},{2,3},{3,4},{4,5},{5,6},{6,7},{7,8},{8,9},{9,10},{10,1... | collective-permute-start | bytes 393224 | tf_op jit(solution)/shard_map/ppermute | solution.py:529
  90.9 1.5 %copy-start.8 = (f32[256,128]{1,0:T(8,128)}, f32[256,128]{1,0:T(8,128)S(1)}, u32[]{:S(2)}) copy-start(f32[256,128]{1,0:T(8,128)S(1)} %collective-permute-done.5.xhi) | copy-start | bytes 393220
  91.0 1.5 %copy-start.9 = (f32[256,128]{1,0:T(8,128)}, f32[256,128]{1,0:T(8,128)S(1)}, u32[]{:S(2)}) copy-start(f32[256,128]{1,0:T(8,128)S(1)} %collective-permute-done.4.xlo) | copy-start | bytes 393220
  91.0 1.5 %copy-start.10 = (f32[256,128]{1,0:T(8,128)}, f32[256,128]{1,0:T(8,128)S(1)}, u32[]{:S(2)}) copy-start(f32[256,128]{1,0:T(8,128)S(1)} %collective-permute-done.7.yhi) | copy-start | bytes 393220
  91.0 1.5 %copy-start.11 = (f32[256,128]{1,0:T(8,128)}, f32[256,128]{1,0:T(8,128)S(1)}, u32[]{:S(2)}) copy-start(f32[256,128]{1,0:T(8,128)S(1)} %collective-permute-done.6.ylo) | copy-start | bytes 393220

commit v4 on v3

--- a/solution.py
+++ b/solution.py
@@ -11,13 +11,14 @@
 VM = pl.BlockSpec(memory_space=pltpu.VMEM)
 SM = pl.BlockSpec(memory_space=pltpu.SMEM)
 ANY = pl.BlockSpec(memory_space=pl.ANY)
-PARAMS = pltpu.CompilerParams(vmem_limit_bytes=56 * 2**20)
+PARAMS = pltpu.CompilerParams(vmem_limit_bytes=44 * 2**20)
 SMALL = pltpu.CompilerParams(vmem_limit_bytes=16 * 2**20)
 LINES = 32
 LINE = 8
 PLANE = LINES * LINE
 ROWS = LINES * PLANE
 PARTS = 8
+FINE = 16
 SPAN = ROWS // PARTS
 
 
@@ -27,6 +28,10 @@
 
 def in_hbm(*arrays):
     return [pltpu.with_memory_space_constraint(a, pltpu.HBM) for a in arrays]
+
+
+def in_vmem(*arrays):
+    return [pltpu.with_memory_space_constraint(a, pltpu.VMEM) for a in arrays]
 
 
 def in_smem(*arrays):
@@ -58,15 +63,18 @@
     return (r & ~63) | ((r & 7) << 3) | ((r >> 3) & 7)
 
 
-def piece(ref, k, shift=0):
-    return ref.at[pl.ds(aligned(k * SPAN + shift, 8), SPAN)]
+def piece(ref, k, shift=0, parts=PARTS):
+    return ref.at[pl.ds(aligned(k * (ROWS // parts) + shift, 8), ROWS // parts)]
 
 
 def gather_kernel(rows, src, out, at, block, made, at_v, sems, done):
     loads = [pltpu.make_async_copy(piece(src, k), piece(block, k), sems.at[k]) for k in range(PARTS)]
+    asked = pltpu.make_async_copy(rows, at_v, sems.at[PARTS])
+    asked.start()
     for load in loads:
         load.start()
-    at_v[...] = place_in_tiles(rows[...])
+    asked.wait()
+    at_v[...] = place_in_tiles(at_v[...])
     listed = pltpu.make_async_copy(at_v, at, sems.at[PARTS])
     listed.start()
     listed.wait()
@@ -102,12 +110,12 @@
     n = rows.shape[0] * 128
     return pl.pallas_call(
         gather_kernel, out_shape=(shape(n), pltpu.SMEM(rows.shape, jnp.int32)),
-        in_specs=[VM, ANY], out_specs=(ANY, SM),
+        in_specs=[ANY, ANY], out_specs=(ANY, SM),
         scratch_shapes=[pltpu.VMEM((ROWS, 128), F32), pltpu.VMEM((n, 128), F32),
                         pltpu.VMEM(rows.shape, jnp.int32), pltpu.SemaphoreType.DMA((PARTS + 1,)),
                         pltpu.SemaphoreType.DMA((PARTS,))],
         compiler_params=PARAMS, name="gather_rows",
-    )(rows, *in_hbm(src))
+    )(*in_hbm(rows, src))
 
 
 def finish_kernel(at, flux, src, kx0, kx1, ky0, ky1, xlo, xhi, ylo, yhi, out, block, sink, sides, sems, beside):
@@ -175,9 +183,9 @@
 def after_all(array, others):
     n = len(others)
     return pl.pallas_call(
-        tie_kernel, out_shape=pltpu.HBM(array.shape, array.dtype), in_specs=[ANY] * (n + 1), out_specs=ANY,
+        tie_kernel, out_shape=pltpu.HBM(array.shape, array.dtype), in_specs=[VM] * n + [ANY], out_specs=ANY,
         input_output_aliases={n: 0}, compiler_params=SMALL, name="tie",
-    )(*others, *in_hbm(array))
+    )(*in_vmem(*others), *in_hbm(array))
 
 
 def step_up(a, edge, corner, fill):
@@ -223,25 +231,20 @@
         u, c, w = u_new, c_new, w_new
 
 
-def planes(ready, relax, save):
-    each = LINES // PARTS
+def planes(ready, relax, after):
+    each = LINES // FINE
     ready(0)
 
     def step(k, _):
-        @pl.when(k + 1 < PARTS)
+        @pl.when(k + 1 < FINE)
         def _():
             ready(k + 1)
 
         lax.fori_loop(0, each, lambda i, _: (relax(k * each + i), 0)[1], 0)
-        for copy in save(k):
-            copy.start()
+        after(k)
         return 0
 
-    lax.fori_loop(0, PARTS, step, 0)
-
-
-def both_sides(relax):
-    lax.fori_loop(0, 2, lambda i, _: (relax(i * (LINES - 1)), 0)[1], 0)
+    lax.fori_loop(0, FINE, step, 0)
 
 
 def clear_beyond(*refs):
@@ -250,117 +253,131 @@
         ref[pl.ds(PLANE + ROWS, PLANE), :] = jnp.zeros((PLANE, 128), F32)
 
 
-def first_kernel(after, u, c, p, out, gain, sx0, sx1, sy0, sy1, nx0, nx1, ny0, ny1, us, cs, ps, vs, gs, nx, sems, done):
+def first_kernel(after, u, c, p, out, gain, sx0, sx1, sy0, sy1, us, cs, ps, vs, gs, sides, sems, done, sent):
     del after
 
     def loads(k):
-        return [pltpu.make_async_copy(piece(a, k), piece(b, k, shift), sems.at[n, k])
+        return [pltpu.make_async_copy(piece(a, k, 0, FINE), piece(b, k, shift, FINE), sems.at[n, k])
                 for n, (a, b, shift) in enumerate(((u, us, PLANE), (c, cs, PLANE), (p, ps, 0)))]
 
-    def save(k):
-        return [pltpu.make_async_copy(piece(a, k), piece(b, k), done.at[n, k])
+    def saves(k):
+        return [pltpu.make_async_copy(piece(a, k, 0, FINE), piece(b, k, 0, FINE), done.at[n, k])
                 for n, (a, b) in enumerate(((vs, out), (gs, gain)))]
 
-    for k in range(PARTS):
+    for k in range(FINE):
         for load in loads(k):
             load.start()
     clear_beyond(us, cs)
 
+    load_u = lambda x, y: us[tiled_line(x + 1, y), :]
+    load_c = lambda x, y: cs[tiled_line(x + 1, y), :]
+    load_p = lambda x, y: ps[tiled_line(x, y), :]
+    sends = [pltpu.make_async_copy(sides.at[n], ref, sent.at[n]) for n, ref in enumerate((sx0, sx1, sy0, sy1))]
+
     def ready(k):
         for load in loads(k):
             load.wait()
 
-    load_u = lambda x, y: us[tiled_line(x + 1, y), :]
-    load_c = lambda x, y: cs[tiled_line(x + 1, y), :]
-    load_p = lambda x, y: ps[tiled_line(x, y), :]
-
-    def put(sums, start, numer, denom):
-        sums[pl.ds(aligned(start, 8), 8), :] = numer
-        sums[pl.ds(aligned(start + PLANE, 8), 8), :] = denom
+        @pl.when(k == FINE - 1)
+        def _():
+            for n in range(LINES):
+                row, below = pl.ds(n * LINE, LINE), pl.ds(PLANE + n * LINE, LINE)
+                for side, (x, y) in enumerate(((0, n), (LINES - 1, n), (n, 0), (n, LINES - 1))):
+                    sides[side, row, :] = load_u(x, y)
+                    sides[side, below, :] = load_c(x, y)
+            for send in sends:
+                send.start()
 
     def store(x, y, numer, denom, c):
         part = 1.0 / denom
         vs[plain_line(x, y), :] = numer * part
         gs[plain_line(x, y), :] = part
-        if y == 0:
-            put(ny0, x * LINE, numer, denom)
-        if y == LINES - 1:
-            put(ny1, x * LINE, numer, denom)
-
-    planes(ready, lambda x: relax_plane(x, load_u, load_c, load_p, store, True), save)
-
-    def store_x(x, y, numer, denom, c):
-        put(nx, lax.div(x, LINES - 1) * (2 * PLANE) + y * LINE, numer, denom)
-
-    both_sides(lambda x: relax_plane(x, load_u, load_c, load_p, store_x, True))
-    for n in range(LINES):
-        row, below = pl.ds(n * LINE, LINE), pl.ds(PLANE + n * LINE, LINE)
-        for ref, x, y in ((sx0, 0, n), (sx1, LINES - 1, n), (sy0, n, 0), (sy1, n, LINES - 1)):
-            ref[row, :] = load_u(x, y)
-            ref[below, :] = load_c(x, y)
-    nx0[...] = nx[pl.ds(0, 2 * PLANE), :]
-    nx1[...] = nx[pl.ds(2 * PLANE, 2 * PLANE), :]
-    for k in range(PARTS):
-        for copy in save(k):
-            copy.wait()
+
+    def after_piece(k):
+        for save in saves(k):
+            save.start()
+
+    planes(ready, lambda x: relax_plane(x, load_u, load_c, load_p, store, True), after_piece)
+    for send in sends:
+        send.wait()
+    for k in range(FINE):
+        for save in saves(k):
+            save.wait()
 
 
 def sweep_first(after, u, c, p):
     return pl.pallas_call(
-        first_kernel, out_shape=(shape(ROWS),) * 2 + (shape(2 * PLANE),) * 8,
-        in_specs=[ANY] * 4, out_specs=(ANY,) * 2 + (VM,) * 8,
+        first_kernel, out_shape=(shape(ROWS),) * 2 + (shape(2 * PLANE),) * 4,
+        in_specs=[ANY] * 4, out_specs=(ANY,) * 6,
         scratch_shapes=[pltpu.VMEM((ROWS + 2 * PLANE, 128), F32), pltpu.VMEM((ROWS + 2 * PLANE, 128), F32),
                         pltpu.VMEM((ROWS, 128), F32), pltpu.VMEM((ROWS, 128), F32), pltpu.VMEM((ROWS, 128), F32),
-                        pltpu.VMEM((4 * PLANE, 128), F32),
-                        pltpu.SemaphoreType.DMA((3, PARTS)), pltpu.SemaphoreType.DMA((2, PARTS))],
+                        pltpu.VMEM((4, 2 * PLANE, 128), F32), pltpu.SemaphoreType.DMA((3, FINE)),
+                        pltpu.SemaphoreType.DMA((2, FINE)), pltpu.SemaphoreType.DMA((4,))],
         compiler_params=PARAMS, name="sweep_first",
     )(*in_hbm(after, u, c, p))
 
 
-def sides_kernel(after, sx0, sx1, sy0, sy1, nx0, nx1, ny0, ny1, xlo, xhi, ylo, yhi, fx0, fx1, fy0, fy1):
+def sides_kernel(after, once, gain, sx0, sx1, sy0, sy1, xlo, xhi, ylo, yhi, fx0, fx1, fy0, fy1,
+                 bx0, bx1, by0, by1, on_x, on_y, cs, sems, passed):
     del after
-
-    def part(ref, start=0):
-        return ref[pl.ds(start, PLANE), :]
-
-    def add(numer, denom, c, u_side, c_side):
-        return numer + (c + c_side) * u_side, denom + c_side
-
-    for ref, sent, sums, halo, ends in (
-        (fx0, sx0, nx0, xlo, ((ylo, 0), (yhi, 0))),
-        (fx1, sx1, nx1, xhi, ((ylo, PLANE - 8), (yhi, PLANE - 8))),
-        (fy0, sy0, ny0, ylo, ((xlo, 0), (xhi, 0))),
-        (fy1, sy1, ny1, yhi, ((xlo, PLANE - 8), (xhi, PLANE - 8))),
-    ):
-        c = part(sent, PLANE)
-        numer, denom = add(part(sums), part(sums, PLANE), c, part(halo), part(halo, PLANE))
+    copies = []
+    for n, a in enumerate((once, gain)):
+        for side, x in enumerate((0, LINES - 1)):
+            copies.append((a.at[x], on_x.at[n, side]))
+            copies.append((a.at[:, pl.ds(x * LINE, LINE)], on_y.at[n, side]))
+    for side, a in enumerate((sx0, sx1, sy0, sy1)):
+        copies.append((a.at[pl.ds(PLANE, PLANE)], cs.at[side]))
+    copies = [pltpu.make_async_copy(a, b, sems.at[n]) for n, (a, b) in enumerate(copies)]
+    for copy in copies:
+        copy.start()
+    passing = [pltpu.make_async_copy(a.at[pl.ds(PLANE, PLANE)], b, passed.at[n])
+               for n, (a, b) in enumerate(((xlo, bx0), (xhi, bx1), (ylo, by0), (yhi, by1)))]
+    for copy in passing:
+        copy.start()
+    for copy in copies:
+        copy.wait()
+    end = PLANE - LINE
+    for side, (ref, halo, ends) in enumerate((
+        (fx0, xlo, ((ylo, 0), (yhi, 0))), (fx1, xhi, ((ylo, end), (yhi, end))),
+        (fy0, ylo, ((xlo, 0), (xhi, 0))), (fy1, yhi, ((xlo, end), (xhi, end))),
+    )):
+        c = cs[side]
+        v, g = [on_x[n, side] if side < 2 else on_y[n, side - 2].reshape(PLANE, 128) for n in range(2)]
+        c_out = halo[pl.ds(PLANE, PLANE), :]
+        numer = v + g * ((c + c_out) * halo[pl.ds(0, PLANE), :])
+        denom = 1.0 + g * c_out
         ref[...] = numer / denom
-        for rows, (other, line) in zip((0, PLANE - 8), ends):
-            at = slice(rows, rows + 8)
-            side = other[pl.ds(line, 8), :], other[pl.ds(PLANE + line, 8), :]
-            n, d = add(numer[at], denom[at], c[at], *side)
-            ref[pl.ds(rows, 8), :] = n / d
-
-
-def fix_sides(after, parts, halos):
+        for start, (other, line) in zip((0, end), ends):
+            at = slice(start, start + LINE)
+            c_out = other[pl.ds(PLANE + line, LINE), :]
+            more = numer[at] + g[at] * ((c[at] + c_out) * other[pl.ds(line, LINE), :])
+            ref[pl.ds(start, LINE), :] = more / (denom[at] + g[at] * c_out)
+    for copy in passing:
+        copy.wait()
+
+
+def fix_sides(after, once, gain, sides, halos):
+    by_plane = lambda a: a.reshape(LINES, PLANE, 128)
     return pl.pallas_call(
-        sides_kernel, out_shape=(shape(PLANE),) * 4, in_specs=[ANY] + [VM] * 12, out_specs=(VM,) * 4,
-        compiler_params=PARAMS, name="sweep_first_sides",
-    )(*in_hbm(after), *parts, *halos)
+        sides_kernel, out_shape=(shape(PLANE),) * 8, in_specs=[ANY] * 7 + [VM] * 4, out_specs=(VM,) * 4 + (ANY,) * 4,
+        scratch_shapes=[pltpu.VMEM((2, 2, PLANE, 128), F32), pltpu.VMEM((2, 2, LINES, LINE, 128), F32),
+                        pltpu.VMEM((4, PLANE, 128), F32), pltpu.SemaphoreType.DMA((12,)), pltpu.SemaphoreType.DMA((4,))],
+        compiler_params=SMALL, name="sweep_first_sides",
+    )(*in_hbm(after, by_plane(once), by_plane(gain), *sides), *in_vmem(*halos))
 
 
 def second_kernel(after, u, c, p, gain, fx0, fx1, fy0, fy1, xlo, xhi, ylo, yhi, out, kx0, kx1, ky0, ky1,
-                  us, cs, ps, gs, vs, kx, sems, done):
+                  us, cs, ps, gs, vs, sems, done):
     del after
 
     def loads(k):
-        return [pltpu.make_async_copy(piece(a, k), piece(b, k, shift), sems.at[n, k])
+        return [pltpu.make_async_copy(piece(a, k, 0, FINE), piece(b, k, shift, FINE), sems.at[n, k])
                 for n, (a, b, shift) in enumerate(((u, us, PLANE), (c, cs, PLANE), (p, ps, 0), (gain, gs, 0)))]
 
     def save(k):
-        return [pltpu.make_async_copy(piece(vs, k), piece(out, k), done.at[k])]
-
-    for k in range(PARTS):
+        return pltpu.make_async_copy(piece(vs, k, 0, FINE), piece(out, k, 0, FINE), done.at[k])
+
+    for k in range(FINE):
         for load in loads(k):
             load.start()
     clear_beyond(us, cs)
@@ -368,8 +385,8 @@
     def ready(k):
         for load in loads(k):
             load.wait()
-        for i in range(LINES // PARTS):
-            x = k * (LINES // PARTS) + i
+        for i in range(LINES // FINE):
+            x = k * (LINES // FINE) + i
             us[plain_line(x + 1, 0), :] = fy0[plain_line(0, x), :]
             us[plain_line(x + 1, LINES - 1), :] = fy1[plain_line(0, x), :]
 
@@ -377,7 +394,7 @@
         def _():
             us[pl.ds(PLANE, PLANE), :] = fx0[...]
 
-        @pl.when(k == PARTS - 1)
+        @pl.when(k == FINE - 1)
         def _():
             us[pl.ds(ROWS, PLANE), :] = fx1[...]
 
@@ -386,53 +403,56 @@
     load_p = lambda x, y: ps[tiled_line(x, y), :]
     y_sides = {0: (ylo, ky0), LINES - 1: (yhi, ky1)}
 
-    def put(x, y, numer, part, c, beside):
-        if y in y_sides or beside is not None:
-            denom = 1.0 / part
-            if beside is not None:
-                denom = denom + beside
+    def beyond_y(x, y, part):
+        outer = y_sides[y][0][plain_line(0, x), :]
+        return outer, part / (1.0 + part * outer)
+
+    def store(x, y, numer, _, c):
+        part = gs[plain_line(x, y), :]
+        if y in y_sides:
+            outer, part = beyond_y(x, y, part)
+            y_sides[y][1][plain_line(0, x), :] = (c + outer) * part
+        vs[tiled_line(x, y), :] = numer * part
+
+    def x_side(x, halo, k_side):
+        for y in range(LINES):
+            line = pl.ds(y * LINE, LINE)
+            outer = halo[pl.ds(y * LINE, LINE), :]
+            part = gs[plain_line(x, y), :]
             if y in y_sides:
-                halo, k_side = y_sides[y]
-                outer = halo[pl.ds(aligned(PLANE + x * LINE, 8), 8), :]
-                part = 1.0 / (denom + outer)
-                k_side[plain_line(0, x), :] = (c + outer) * part
-            else:
-                part = 1.0 / denom
-        vs[tiled_line(x, y), :] = numer * part
-        return part
-
-    def store(x, y, numer, _, c):
-        put(x, y, numer, gs[plain_line(x, y), :], c, None)
-
-    planes(ready, lambda x: relax_plane(x, load_u, load_c, load_p, store, False), lambda k: [])
-
-    def store_x(x, y, numer, _, c):
-        line = pl.ds(PLANE + y * LINE, LINE)
-        beside = jnp.where(x == 0, xlo[line, :], xhi[line, :])
-        part = put(x, y, numer, gs[plain_line(x, y), :], c, beside)
-        kx[pl.ds(aligned(lax.div(x, LINES - 1) * PLANE + y * LINE, 8), 8), :] = (c + beside) * part
-
-    both_sides(lambda x: relax_plane(x, load_u, load_c, load_p, store_x, False))
-    for k in range(PARTS):
-        for copy in save(k):
-            copy.start()
-    kx0[...] = kx[pl.ds(0, PLANE), :]
-    kx1[...] = kx[pl.ds(PLANE, PLANE), :]
-    for k in range(PARTS):
-        for copy in save(k):
-            copy.wait()
-
-
-def sweep_second(after, u, c, p, gain, faces, halos):
+                part = beyond_y(x, y, part)[1]
+            less = 1.0 / (1.0 + part * outer)
+            if y in y_sides:
+                k_y = y_sides[y][1]
+                k_y[plain_line(0, x), :] = k_y[plain_line(0, x), :] * less
+            vs[tiled_line(x, y), :] = vs[tiled_line(x, y), :] * less
+            k_side[line, :] = (load_c(x, y) + outer) * (part * less)
+
+    def after_piece(k):
+        @pl.when(k == 0)
+        def _():
+            x_side(0, xlo, kx0)
+
+        @pl.when(k == FINE - 1)
+        def _():
+            x_side(LINES - 1, xhi, kx1)
+
+        save(k).start()
+
+    planes(ready, lambda x: relax_plane(x, load_u, load_c, load_p, store, False), after_piece)
+    for k in range(FINE):
+        save(k).wait()
+
+
+def sweep_second(after, u, c, p, gain, faces, beyond):
     return pl.pallas_call(
         second_kernel, out_shape=(shape(ROWS),) + (shape(PLANE),) * 4,
         in_specs=[ANY] * 5 + [VM] * 8, out_specs=(ANY,) + (VM,) * 4,
         scratch_shapes=[pltpu.VMEM((ROWS + 2 * PLANE, 128), F32), pltpu.VMEM((ROWS + 2 * PLANE, 128), F32),
                         pltpu.VMEM((ROWS, 128), F32), pltpu.VMEM((ROWS, 128), F32), pltpu.VMEM((ROWS, 128), F32),
-                        pltpu.VMEM((2 * PLANE, 128), F32),
-                        pltpu.SemaphoreType.DMA((4, PARTS)), pltpu.SemaphoreType.DMA((PARTS,))],
+                        pltpu.SemaphoreType.DMA((4, FINE)), pltpu.SemaphoreType.DMA((FINE,))],
         compiler_params=PARAMS, name="sweep_second",
-    )(*in_hbm(after, u, c, p, gain), *faces, *halos)
+    )(*in_hbm(after, u, c, p, gain, *faces, *beyond))
 
 
 def channel_kernel(*refs):
@@ -513,7 +533,7 @@
         out_shape=(jax.ShapeDtypeStruct((size, spans * groups, 128), F32),
                    pltpu.HBM((groups, rows, 128), F32)),
         in_specs=[ANY] * len(after) + [SM] + [VM] * 2 + [ANY] + [VM] * 3, out_specs=(ANY, ANY),
-        scratch_shapes=[pltpu.VMEM((size, spans * groups, 128), F32), pltpu.VMEM((groups, rows, 128), F32),
+        scratch_shapes=[pltpu.VMEM((size, (spans + 1) * groups, 128), F32), pltpu.VMEM((groups, rows, 128), F32),
                         pltpu.VMEM(props.shape, F32)]
         + [pltpu.VMEM((groups * size, 128), F32)] * 3
         + [pltpu.SemaphoreType.DMA((spans,)), pltpu.SemaphoreType.DMA((spans // 4,)),
@@ -545,17 +565,18 @@
     sent, at = gather(wall_rows.reshape(-1, 128), u)
     arrived = lax.all_to_all(sent.reshape(devices, -1, 128), both, 0, 0, tiled=True)
 
-    once, gain, *parts = sweep_first(sent, u, c, p)
-    halos = (up(parts[1], "gx"), down(parts[0], "gx"), up(parts[3], "gy"), down(parts[2], "gy"))
+    once, gain, *sides = sweep_first(sent, u, c, p)
+    halos = (up(sides[1], "gx"), down(sides[0], "gx"), up(sides[3], "gy"), down(sides[2], "gy"))
 
     fluid, flux = channel((once,), me, channel_owner.reshape(-1, 128), arrived, span_prop, span_carry,
                           channel_coef, channel_inlet)
     flux = after_all(flux, halos)
     returned = lax.all_to_all(flux.reshape(devices, -1, 128), both, 0, 0, tiled=True)
 
-    faces = fix_sides(flux, parts, halos)
+    faces = fix_sides(flux, once, gain, sides, halos)
+    faces, beyond = faces[:4], faces[4:]
     outer = (up(faces[1], "gx"), down(faces[0], "gx"), up(faces[3], "gy"), down(faces[2], "gy"))
-    twice, *gains = sweep_second(flux, once, c, p, gain, faces, halos)
+    twice, *gains = sweep_second(flux, once, c, p, gain, faces, beyond)
     solid_out = finish(at, returned.reshape(-1, 128), twice, gains, outer)
     return untiles(solid_out, *solid_temp.shape), untiles(fluid, 1, slots, span_carry.shape[0] * 128)[0]
 

time: 99.2 us -> 96.5 us (0.973)
  Pallas kernels: 49.8 us -> 45.4 us
  waiting for transfers between devices: 7.39 us -> 10.5 us
    pallas_call x1, Pallas kernels: 14.7 us -> 12.8 us  [sweep_second(): pl.pallas_call(second_kernel, out_shape=(shape(ROWS),) + (shape(PLANE),)...]
    all_to_all x1, waiting for transfers between devices: 1.44 us -> 3.07 us  [local(): lax.all_to_all(flux.reshape(devices, -1, 128), both, 0, 0, tiled=True)]
    all_to_all x1, waiting for transfers between devices: 5.93 us -> 7.22 us  [local(): lax.all_to_all(sent.reshape(devices, -1, 128), both, 0, 0, tiled=True)]
    pallas_call x1, Pallas kernels: 14.2 us -> 12.9 us  [sweep_first(): pl.pallas_call(first_kernel, out_shape=(shape(ROWS),) * 2 + (shape(2 * PL...]
  transfers between devices with their start and end apart: 10 -> 10, of which waited for: 2 -> 3; matrix products, arithmetic and copies ran while one was open for 0% -> 0% of each run, Pallas kernels for 37% -> 34%
where the time goes in v4:
time: 96.5 us; the launch traced here: 95.9 us
  Pallas kernels  45.4 us (47%)
  starting transfers between devices  39 us (40%)
  waiting for transfers between devices  10.5 us (11%)
    ppermute x4, starting transfers between devices, up(): return lax.ppermute(a, axis, [(i, i + 1) for i in range(n - 1)])  13.6 us
    pallas_call x1, Pallas kernels, sweep_first(): pl.pallas_call(first_kernel, out_shape=(shape(ROWS),) * 2 + (shape(2 * PL...  12.9 us
    pallas_call x1, Pallas kernels, sweep_second(): pl.pallas_call(second_kernel, out_shape=(shape(ROWS),) + (shape(PLANE),)...  12.8 us
    all_to_all x1, starting transfers between devices, local(): lax.all_to_all(sent.reshape(devices, -1, 128), both, 0, 0, tiled=True)  11.5 us
    ppermute x4, starting transfers between devices, down(): return lax.ppermute(a, axis, [(i + 1, i) for i in range(n - 1)])  7.99 us
    all_to_all x1, waiting for transfers between devices, local(): lax.all_to_all(sent.reshape(devices, -1, 128), both, 0, 0, tiled=True)  7.22 us
    pallas_call x1, Pallas kernels, gather(): pl.pallas_call(gather_kernel, out_shape=(shape(n), pltpu.SMEM(rows.shape,...  6.42 us
    pallas_call x1, Pallas kernels, finish(): pl.pallas_call(finish_kernel, out_shape=shape(ROWS), in_specs=[SM, VM] +...  6.1 us
  transfers between devices with their start and end apart: 10, of which 3 were waited for; matrix products, arithmetic and copies ran while one was open for 0% of the time, Pallas kernels for 34%

profile of v4, /device:TPU:1, one launch (start us, length us, event | category | flops | bytes accessed | tf_op | source)
XLA Modules:
  0.0 95.9 jit_solution(8821341249224230571)
XLA Ops:
  0.6 6.4 %gather_rows.1 = (f32[4096,128]{1,0:T(8,128)}, s32[32,128]{1,0:T(8,128)S(4)}) custom-call(s32[32,128]{1,0:T(8,128)} %bitcast.52, f32[8192,128]{1,0:T(8,128)} %bitcast.48), custom_call_target="tpu_custom_call" | custom-call | tf_op jit(solution)/shard_map/gather_rows/pallas_call | solution.py:111
  7.1 11.5 %all-to-all-start = ((f32[128,32,128]{2,1,0:T(8,128)}), f32[128,32,128]{2,1,0:T(8,128)S(1)}, u32[]{:S(2)}, u32[]{:S(2)}) async-start(f32[128,32,128]{2,1,0:T(8,128)} %bitcast.50), calls=%async_computation | async-start | bytes 4194304 | tf_op jit(solution)/shard_map/all_to_all | solution.py:566
  18.6 0.0 copy-start
  18.6 0.0 copy-start.1
  18.6 0.0 copy-start.2
  18.6 0.0 copy-start.3
  18.6 12.9 %sweep_first.1 = (f32[8192,128]{1,0:T(8,128)}, f32[8192,128]{1,0:T(8,128)}, f32[512,128]{1,0:T(8,128)}, f32[512,128]{1,0:T(8,128)}, f32[512,128]{1,0:T(8,128)}, /*index=5*/f32[512,128]{1,0:T(8,128)}) custom-call(f32[4096,128]{1,0:T(8,128)} %get-tuple-element.26.after, f32[8192,128]{1,0:T(8,128)} %bitcast.49, f32[8192,128]{1,0:T(8,128)} %bitcast.43, ...), custom_call_target="tpu_custom_call" | custom-call | tf_op jit(solution)/shard_map/sweep_first/pallas_call | solution.py:309
  31.5 3.4 %collective-permute-start = (f32[512,128]{1,0:T(8,128)}, f32[512,128]{1,0:T(8,128)S(1)}, u32[]{:S(2)}, u32[]{:S(2)}) collective-permute-start(f32[512,128]{1,0:T(8,128)} %get-tuple-element.27.sx1), channel_id=1, source_target_pairs={{0,32},{32,64},{64,96},{1,33},{33,65},{65,97},{2,34},{34,66},{66,9... | collective-permute-start | bytes 786440 | tf_op jit(solution)/shard_map/ppermute | solution.py:549
  34.9 1.3 %collective-permute-start.1 = (f32[512,128]{1,0:T(8,128)}, f32[512,128]{1,0:T(8,128)S(1)}, u32[]{:S(2)}, u32[]{:S(2)}) collective-permute-start(f32[512,128]{1,0:T(8,128)} %get-tuple-element.28.sx0), channel_id=1, source_target_pairs={{32,0},{64,32},{96,64},{33,1},{65,33},{97,65},{34,2},{66,34},{98,6... | collective-permute-start | bytes 786440 | tf_op jit(solution)/shard_map/ppermute | solution.py:554
  36.2 3.7 %collective-permute-start.2 = (f32[512,128]{1,0:T(8,128)}, f32[512,128]{1,0:T(8,128)S(1)}, u32[]{:S(2)}, u32[]{:S(2)}) collective-permute-start(f32[512,128]{1,0:T(8,128)} %get-tuple-element.29.sy1), channel_id=1, source_target_pairs={{0,1},{1,2},{2,3},{3,4},{4,5},{5,6},{6,7},{7,8},{8,9},{9,10},{10,1... | collective-permute-start | bytes 786440 | tf_op jit(solution)/shard_map/ppermute | solution.py:549
  39.9 1.9 %collective-permute-start.3 = (f32[512,128]{1,0:T(8,128)}, f32[512,128]{1,0:T(8,128)S(1)}, u32[]{:S(2)}, u32[]{:S(2)}) collective-permute-start(f32[512,128]{1,0:T(8,128)} %get-tuple-element.30.sy0), channel_id=1, source_target_pairs={{1,0},{2,1},{3,2},{4,3},{5,4},{6,5},{7,6},{8,7},{9,8},{10,9},{11,1... | collective-permute-start | bytes 786440 | tf_op jit(solution)/shard_map/ppermute | solution.py:554
  41.9 7.2 %all-to-all-done = f32[128,32,128]{2,1,0:T(8,128)S(1)} async-done(((f32[128,32,128]{2,1,0:T(8,128)}), f32[128,32,128]{2,1,0:T(8,128)S(1)}, u32[]{:S(2)}, u32[]{:S(2)}) %all-to-all-start) | async-done | bytes 2097184 | tf_op jit(solution)/shard_map/all_to_all | solution.py:566
  49.1 0.0 copy-done
  49.1 0.0 copy-done.1
  49.1 0.0 copy-done.2
  49.1 0.0 copy-done.3
  49.1 4.4 %channel_march.1 = (f32[32,128,128]{2,1,0:T(8,128)}, f32[8,512,128]{2,1,0:T(8,128)}) custom-call(f32[8192,128]{1,0:T(8,128)} %get-tuple-element.31.refs_0_.u, s32[1]{0:T(128)} %bitcast.12.refs_1_, s32[128,128]{1,0:T(8,128)S(1)} %bitcast.38, f32[8,512,128]{2,1,0:T(8,128)S(1)} %bitcast.36, f32[16,128,128]{2,1,0:T(8,128)} %refs_4_.1, f32[16,128]{1,0:T(8,128)S(1)} %copy-done.1, ...), custom_call_target="tpu_custom_call" | custom-call | tf_op jit(solution)/shard_map/channel_march/pallas_call | solution.py:531
  53.6 0.0 collective-permute-done.refs_0_.xlo
  53.6 0.0 collective-permute-done.1.refs_1_.xhi
  53.6 0.0 collective-permute-done.2.refs_2_.ylo
  53.6 0.0 collective-permute-done.3.refs_3_.yhi
  53.6 5.9 %all-to-all-start.1 = ((f32[128,32,128]{2,1,0:T(8,128)}), f32[128,32,128]{2,1,0:T(8,128)S(1)}, u32[]{:S(2)}, u32[]{:S(2)}) async-start(f32[128,32,128]{2,1,0:T(8,128)} %bitcast.42), calls=%async_computation.1 | async-start | bytes 4194304 | tf_op jit(solution)/shard_map/all_to_all | solution.py:574
  59.5 2.7 %sweep_first_sides.1 = (f32[256,128]{1,0:T(8,128)}, f32[256,128]{1,0:T(8,128)}, f32[256,128]{1,0:T(8,128)}, f32[256,128]{1,0:T(8,128)}, f32[256,128]{1,0:T(8,128...) custom-call(f32[8,512,128]{2,1,0:T(8,128)} %tie.1.after, f32[32,256,128]{2,1,0:T(8,128)} %bitcast.41, ...), custom_call_target="tpu_custom_call" | custom-call | tf_op jit(solution)/shard_map/sweep_first_sides/pallas_call | solution.py:361
  62.3 1.3 %collective-permute-start.5 = (f32[256,128]{1,0:T(8,128)}, f32[256,128]{1,0:T(8,128)S(1)}, u32[]{:S(2)}, u32[]{:S(2)}) collective-permute-start(f32[256,128]{1,0:T(8,128)} %get-tuple-element.34.fx0), channel_id=1, source_target_pairs={{32,0},{64,32},{96,64},{33,1},{65,33},{97,65},{34,2},{66,34},{98,6... | collective-permute-start | bytes 393224 | tf_op jit(solution)/shard_map/ppermute | solution.py:554
  63.6 4.0 %collective-permute-start.4 = (f32[256,128]{1,0:T(8,128)}, f32[256,128]{1,0:T(8,128)S(1)}, u32[]{:S(2)}, u32[]{:S(2)}) collective-permute-start(f32[256,128]{1,0:T(8,128)} %get-tuple-element.35.fx1), channel_id=1, source_target_pairs={{0,32},{32,64},{64,96},{1,33},{33,65},{65,97},{2,34},{34,66},{66,9... | collective-permute-start | bytes 393224 | tf_op jit(solution)/shard_map/ppermute | solution.py:549
  67.6 3.5 %collective-permute-start.7 = (f32[256,128]{1,0:T(8,128)}, f32[256,128]{1,0:T(8,128)S(1)}, u32[]{:S(2)}, u32[]{:S(2)}) collective-permute-start(f32[256,128]{1,0:T(8,128)} %get-tuple-element.36.fy0), channel_id=1, source_target_pairs={{1,0},{2,1},{3,2},{4,3},{5,4},{6,5},{7,6},{8,7},{9,8},{10,9},{11,1... | collective-permute-start | bytes 393224 | tf_op jit(solution)/shard_map/ppermute | solution.py:554
  71.1 2.5 %collective-permute-start.6 = (f32[256,128]{1,0:T(8,128)}, f32[256,128]{1,0:T(8,128)S(1)}, u32[]{:S(2)}, u32[]{:S(2)}) collective-permute-start(f32[256,128]{1,0:T(8,128)} %get-tuple-element.37.fy1), channel_id=1, source_target_pairs={{0,1},{1,2},{2,3},{3,4},{4,5},{5,6},{6,7},{7,8},{8,9},{9,10},{10,1... | collective-permute-start | bytes 393224 | tf_op jit(solution)/shard_map/ppermute | solution.py:549
  73.6 12.8 %sweep_second.1 = (f32[8192,128]{1,0:T(8,128)}, f32[256,128]{1,0:T(8,128)}, f32[256,128]{1,0:T(8,128)}, f32[256,128]{1,0:T(8,128)}, f32[256,128]{1,0:T(8,128)}) custom-call(f32[8,512,128]{2,1,0:T(8,128)} %tie.1.after, f32[8192,128]{1,0:T(8,128)} %get-tuple-element.31.refs_0_.u, f32[8192,128]{1,0:T(8,128)} %bitcast.44, f32[8192,128]{1,0:T(8,128)} %bitcast.46, ...), custom_call_target="tpu_custom_call" | custom-call | tf_op jit(solution)/shard_map/sweep_second/pallas_call | solution.py:448
  86.5 0.2 collective-permute-done.5.xhi
  86.6 0.0 copy-start.4
  86.7 0.0 collective-permute-done.4.xlo
  86.7 0.0 copy-start.5
  86.7 0.0 collective-permute-done.7.yhi
  86.7 0.0 copy-start.6
  86.7 0.0 collective-permute-done.6.ylo
  86.7 0.0 copy-start.7
  86.7 3.1 %all-to-all-done.1 = f32[128,32,128]{2,1,0:T(8,128)S(1)} async-done(((f32[128,32,128]{2,1,0:T(8,128)}), f32[128,32,128]{2,1,0:T(8,128)S(1)}, u32[]{:S(2)}, u32[]{:S(2)}) %all-to-all-start.1) | async-done | bytes 2097184 | tf_op jit(solution)/shard_map/all_to_all | solution.py:574
  89.8 0.0 copy-done.4
  89.8 0.0 copy-done.5
  89.8 0.0 copy-done.6
  89.8 0.0 copy-done.7
  89.8 6.1 %subtract_rows.1 = f32[8192,128]{1,0:T(8,128)} custom-call(s32[32,128]{1,0:T(8,128)S(4)} %get-tuple-element.25.at, f32[4096,128]{1,0:T(8,128)S(1)} %bitcast.37, f32[8192,128]{1,0:T(8,128)} %get-tuple-element.42.src, f32[256,128]{1,0:T(8,128)} %get-tuple-element.43.kx0, f32[256,128]{1,0:T(8,128)} %get-tuple-element.44.kx1, f32[256,128]{1,0:T(8,128)} %get-tuple-element.45.ky0, ...), custom_call_target="tpu_custom_call" | custom-call | tf_op jit(solution)/shard_map/subtract_rows/pallas_call | solution.py:171
  (1 shorter events, 0.0 us)
Async XLA Ops:
  7.1 42.0 %all-to-all-start = ((f32[128,32,128]{2,1,0:T(8,128)}), f32[128,32,128]{2,1,0:T(8,128)S(1)}, u32[]{:S(2)}, u32[]{:S(2)}) async-start(f32[128,32,128]{2,1,0:T(8,128)} %bitcast.50), calls=%async_computation | async-start | bytes 4194304 | tf_op jit(solution)/shard_map/all_to_all | solution.py:566
  18.6 30.5 %copy-start = (s32[16384]{0:T(1024)S(1)}, s32[16384]{0:T(1024)}, u32[]{:S(2)}) copy-start(s32[16384]{0:T(1024)} %param.12) | copy-start | bytes 196612
  18.6 30.5 %copy-start.1 = (f32[16,128]{1,0:T(8,128)S(1)}, f32[16,128]{1,0:T(8,128)}, u32[]{:S(2)}) copy-start(f32[16,128]{1,0:T(8,128)} %refs_5_.1) | copy-start | bytes 24580
  18.6 30.5 %copy-start.2 = (f32[256]{0:T(256)S(1)}, f32[256]{0:T(256)}, u32[]{:S(2)}) copy-start(f32[256]{0:T(256)} %param.16) | copy-start | bytes 3076
  18.6 30.5 %copy-start.3 = (f32[256]{0:T(256)S(1)}, f32[256]{0:T(256)}, u32[]{:S(2)}) copy-start(f32[256]{0:T(256)} %param.17) | copy-start | bytes 3076
  31.5 22.1 %collective-permute-start = (f32[512,128]{1,0:T(8,128)}, f32[512,128]{1,0:T(8,128)S(1)}, u32[]{:S(2)}, u32[]{:S(2)}) collective-permute-start(f32[512,128]{1,0:T(8,128)} %get-tuple-element.27.sx1), channel_id=1, source_target_pairs={{0,32},{32,64},{64,96},{1,33},{33,65},{65,97},{2,34},{34,66},{66,9... | collective-permute-start | bytes 786440 | tf_op jit(solution)/shard_map/ppermute | solution.py:549
  34.9 18.6 %collective-permute-start.1 = (f32[512,128]{1,0:T(8,128)}, f32[512,128]{1,0:T(8,128)S(1)}, u32[]{:S(2)}, u32[]{:S(2)}) collective-permute-start(f32[512,128]{1,0:T(8,128)} %get-tuple-element.28.sx0), channel_id=1, source_target_pairs={{32,0},{64,32},{96,64},{33,1},{65,33},{97,65},{34,2},{66,34},{98,6... | collective-permute-start | bytes 786440 | tf_op jit(solution)/shard_map/ppermute | solution.py:554
  36.2 17.3 %collective-permute-start.2 = (f32[512,128]{1,0:T(8,128)}, f32[512,128]{1,0:T(8,128)S(1)}, u32[]{:S(2)}, u32[]{:S(2)}) collective-permute-start(f32[512,128]{1,0:T(8,128)} %get-tuple-element.29.sy1), channel_id=1, source_target_pairs={{0,1},{1,2},{2,3},{3,4},{4,5},{5,6},{6,7},{7,8},{8,9},{9,10},{10,1... | collective-permute-start | bytes 786440 | tf_op jit(solution)/shard_map/ppermute | solution.py:549
  39.9 13.7 %collective-permute-start.3 = (f32[512,128]{1,0:T(8,128)}, f32[512,128]{1,0:T(8,128)S(1)}, u32[]{:S(2)}, u32[]{:S(2)}) collective-permute-start(f32[512,128]{1,0:T(8,128)} %get-tuple-element.30.sy0), channel_id=1, source_target_pairs={{1,0},{2,1},{3,2},{4,3},{5,4},{6,5},{7,6},{8,7},{9,8},{10,9},{11,1... | collective-permute-start | bytes 786440 | tf_op jit(solution)/shard_map/ppermute | solution.py:554
  53.6 36.1 %all-to-all-start.1 = ((f32[128,32,128]{2,1,0:T(8,128)}), f32[128,32,128]{2,1,0:T(8,128)S(1)}, u32[]{:S(2)}, u32[]{:S(2)}) async-start(f32[128,32,128]{2,1,0:T(8,128)} %bitcast.42), calls=%async_computation.1 | async-start | bytes 4194304 | tf_op jit(solution)/shard_map/all_to_all | solution.py:574
  62.3 24.4 %collective-permute-start.5 = (f32[256,128]{1,0:T(8,128)}, f32[256,128]{1,0:T(8,128)S(1)}, u32[]{:S(2)}, u32[]{:S(2)}) collective-permute-start(f32[256,128]{1,0:T(8,128)} %get-tuple-element.34.fx0), channel_id=1, source_target_pairs={{32,0},{64,32},{96,64},{33,1},{65,33},{97,65},{34,2},{66,34},{98,6... | collective-permute-start | bytes 393224 | tf_op jit(solution)/shard_map/ppermute | solution.py:554
  63.6 23.1 %collective-permute-start.4 = (f32[256,128]{1,0:T(8,128)}, f32[256,128]{1,0:T(8,128)S(1)}, u32[]{:S(2)}, u32[]{:S(2)}) collective-permute-start(f32[256,128]{1,0:T(8,128)} %get-tuple-element.35.fx1), channel_id=1, source_target_pairs={{0,32},{32,64},{64,96},{1,33},{33,65},{65,97},{2,34},{34,66},{66,9... | collective-permute-start | bytes 393224 | tf_op jit(solution)/shard_map/ppermute | solution.py:549
  67.6 19.0 %collective-permute-start.7 = (f32[256,128]{1,0:T(8,128)}, f32[256,128]{1,0:T(8,128)S(1)}, u32[]{:S(2)}, u32[]{:S(2)}) collective-permute-start(f32[256,128]{1,0:T(8,128)} %get-tuple-element.36.fy0), channel_id=1, source_target_pairs={{1,0},{2,1},{3,2},{4,3},{5,4},{6,5},{7,6},{8,7},{9,8},{10,9},{11,1... | collective-permute-start | bytes 393224 | tf_op jit(solution)/shard_map/ppermute | solution.py:554
  71.1 15.6 %collective-permute-start.6 = (f32[256,128]{1,0:T(8,128)}, f32[256,128]{1,0:T(8,128)S(1)}, u32[]{:S(2)}, u32[]{:S(2)}) collective-permute-start(f32[256,128]{1,0:T(8,128)} %get-tuple-element.37.fy1), channel_id=1, source_target_pairs={{0,1},{1,2},{2,3},{3,4},{4,5},{5,6},{6,7},{7,8},{8,9},{9,10},{10,1... | collective-permute-start | bytes 393224 | tf_op jit(solution)/shard_map/ppermute | solution.py:549
  86.6 3.1 %copy-start.4 = (f32[256,128]{1,0:T(8,128)}, f32[256,128]{1,0:T(8,128)S(1)}, u32[]{:S(2)}) copy-start(f32[256,128]{1,0:T(8,128)S(1)} %collective-permute-done.5.xhi) | copy-start | bytes 393220
  86.7 3.1 %copy-start.5 = (f32[256,128]{1,0:T(8,128)}, f32[256,128]{1,0:T(8,128)S(1)}, u32[]{:S(2)}) copy-start(f32[256,128]{1,0:T(8,128)S(1)} %collective-permute-done.4.xlo) | copy-start | bytes 393220
  86.7 3.1 %copy-start.6 = (f32[256,128]{1,0:T(8,128)}, f32[256,128]{1,0:T(8,128)S(1)}, u32[]{:S(2)}) copy-start(f32[256,128]{1,0:T(8,128)S(1)} %collective-permute-done.7.yhi) | copy-start | bytes 393220
  86.7 3.1 %copy-start.7 = (f32[256,128]{1,0:T(8,128)}, f32[256,128]{1,0:T(8,128)S(1)}, u32[]{:S(2)}) copy-start(f32[256,128]{1,0:T(8,128)S(1)} %collective-permute-done.6.ylo) | copy-start | bytes 393220

commit v5 on v4

--- a/solution.py
+++ b/solution.py
@@ -17,8 +17,10 @@
 LINE = 8
 PLANE = LINES * LINE
 ROWS = LINES * PLANE
+SPARE = 8
 PARTS = 8
 FINE = 16
+AHEAD = 4
 SPAN = ROWS // PARTS
 
 
@@ -170,7 +172,8 @@
 def finish(at, flux, src, gains, halos):
     return pl.pallas_call(
         finish_kernel, out_shape=shape(ROWS), in_specs=[SM, VM] + [ANY] * 9, out_specs=ANY,
-        scratch_shapes=[pltpu.VMEM((ROWS, 128), F32), pltpu.VMEM((ROWS, 128), F32), pltpu.VMEM((8, PLANE, 128), F32),
+        scratch_shapes=[pltpu.VMEM((ROWS + SPARE, 128), F32), pltpu.VMEM((ROWS, 128), F32),
+                        pltpu.VMEM((8, PLANE, 128), F32),
                         pltpu.SemaphoreType.DMA((PARTS,)), pltpu.SemaphoreType.DMA((8,))],
         compiler_params=SMALL, name="subtract_rows",
     )(*in_smem(at), flux, *in_hbm(src, *gains, *halos))
@@ -231,11 +234,15 @@
         u, c, w = u_new, c_new, w_new
 
 
-def planes(ready, relax, after):
+def planes(start, ready, relax, after):
     each = LINES // FINE
     ready(0)
 
     def step(k, _):
+        @pl.when(k + AHEAD < FINE)
+        def _():
+            start(k + AHEAD)
+
         @pl.when(k + 1 < FINE)
         def _():
             ready(k + 1)
@@ -264,10 +271,14 @@
         return [pltpu.make_async_copy(piece(a, k, 0, FINE), piece(b, k, 0, FINE), done.at[n, k])
                 for n, (a, b) in enumerate(((vs, out), (gs, gain)))]
 
-    for k in range(FINE):
+    for k in range(AHEAD):
         for load in loads(k):
             load.start()
     clear_beyond(us, cs)
+
+    def start(k):
+        for load in loads(k):
+            load.start()
 
     load_u = lambda x, y: us[tiled_line(x + 1, y), :]
     load_c = lambda x, y: cs[tiled_line(x + 1, y), :]
@@ -297,7 +308,7 @@
         for save in saves(k):
             save.start()
 
-    planes(ready, lambda x: relax_plane(x, load_u, load_c, load_p, store, True), after_piece)
+    planes(start, ready, lambda x: relax_plane(x, load_u, load_c, load_p, store, True), after_piece)
     for send in sends:
         send.wait()
     for k in range(FINE):
@@ -309,8 +320,9 @@
     return pl.pallas_call(
         first_kernel, out_shape=(shape(ROWS),) * 2 + (shape(2 * PLANE),) * 4,
         in_specs=[ANY] * 4, out_specs=(ANY,) * 6,
-        scratch_shapes=[pltpu.VMEM((ROWS + 2 * PLANE, 128), F32), pltpu.VMEM((ROWS + 2 * PLANE, 128), F32),
-                        pltpu.VMEM((ROWS, 128), F32), pltpu.VMEM((ROWS, 128), F32), pltpu.VMEM((ROWS, 128), F32),
+        scratch_shapes=[pltpu.VMEM((ROWS + 2 * PLANE + SPARE, 128), F32), pltpu.VMEM((ROWS + 2 * PLANE + SPARE, 128), F32),
+                        pltpu.VMEM((ROWS + SPARE, 128), F32), pltpu.VMEM((ROWS + SPARE, 128), F32),
+                        pltpu.VMEM((ROWS + SPARE, 128), F32),
                         pltpu.VMEM((4, 2 * PLANE, 128), F32), pltpu.SemaphoreType.DMA((3, FINE)),
                         pltpu.SemaphoreType.DMA((2, FINE)), pltpu.SemaphoreType.DMA((4,))],
         compiler_params=PARAMS, name="sweep_first",
@@ -377,10 +389,14 @@
     def save(k):
         return pltpu.make_async_copy(piece(vs, k, 0, FINE), piece(out, k, 0, FINE), done.at[k])
 
-    for k in range(FINE):
+    for k in range(AHEAD):
         for load in loads(k):
             load.start()
     clear_beyond(us, cs)
+
+    def start(k):
+        for load in loads(k):
+            load.start()
 
     def ready(k):
         for load in loads(k):
@@ -439,7 +455,7 @@
 
         save(k).start()
 
-    planes(ready, lambda x: relax_plane(x, load_u, load_c, load_p, store, False), after_piece)
+    planes(start, ready, lambda x: relax_plane(x, load_u, load_c, load_p, store, False), after_piece)
     for k in range(FINE):
         save(k).wait()
 
@@ -448,8 +464,9 @@
     return pl.pallas_call(
         second_kernel, out_shape=(shape(ROWS),) + (shape(PLANE),) * 4,
         in_specs=[ANY] * 5 + [VM] * 8, out_specs=(ANY,) + (VM,) * 4,
-        scratch_shapes=[pltpu.VMEM((ROWS + 2 * PLANE, 128), F32), pltpu.VMEM((ROWS + 2 * PLANE, 128), F32),
-                        pltpu.VMEM((ROWS, 128), F32), pltpu.VMEM((ROWS, 128), F32), pltpu.VMEM((ROWS, 128), F32),
+        scratch_shapes=[pltpu.VMEM((ROWS + 2 * PLANE + SPARE, 128), F32), pltpu.VMEM((ROWS + 2 * PLANE + SPARE, 128), F32),
+                        pltpu.VMEM((ROWS + SPARE, 128), F32), pltpu.VMEM((ROWS + SPARE, 128), F32),
+                        pltpu.VMEM((ROWS + SPARE, 128), F32),
                         pltpu.SemaphoreType.DMA((4, FINE)), pltpu.SemaphoreType.DMA((FINE,))],
         compiler_params=PARAMS, name="sweep_second",
     )(*in_hbm(after, u, c, p, gain, *faces, *beyond))

time: 96.5 us -> 96.6 us (level)
  transfers between devices with their start and end apart: 10 -> 10, of which waited for: 3 -> 2; matrix products, arithmetic and copies ran while one was open for 0% -> 0% of each run, Pallas kernels for 34% -> 35%
where the time goes in v5:
time: 96.6 us; the launch traced here: 96 us
  Pallas kernels  45.9 us (48%)
  starting transfers between devices  39.2 us (41%)
  waiting for transfers between devices  9.98 us (10%)
    ppermute x4, starting transfers between devices, up(): return lax.ppermute(a, axis, [(i, i + 1) for i in range(n - 1)])  13.6 us
    pallas_call x1, Pallas kernels, sweep_second(): pl.pallas_call(second_kernel, out_shape=(shape(ROWS),) + (shape(PLANE),)...  13.2 us
    pallas_call x1, Pallas kernels, sweep_first(): pl.pallas_call(first_kernel, out_shape=(shape(ROWS),) * 2 + (shape(2 * PL...  13 us
    all_to_all x1, starting transfers between devices, local(): lax.all_to_all(sent.reshape(devices, -1, 128), both, 0, 0, tiled=True)  11.5 us
    ppermute x4, starting transfers between devices, down(): return lax.ppermute(a, axis, [(i + 1, i) for i in range(n - 1)])  7.99 us
    all_to_all x1, waiting for transfers between devices, local(): lax.all_to_all(sent.reshape(devices, -1, 128), both, 0, 0, tiled=True)  7.12 us
    pallas_call x1, Pallas kernels, gather(): pl.pallas_call(gather_kernel, out_shape=(shape(n), pltpu.SMEM(rows.shape,...  6.42 us
    pallas_call x1, Pallas kernels, finish(): pl.pallas_call(finish_kernel, out_shape=shape(ROWS), in_specs=[SM, VM] +...  6.13 us
  transfers between devices with their start and end apart: 10, of which 2 were waited for; matrix products, arithmetic and copies ran while one was open for 0% of the time, Pallas kernels for 35%

profile of v5, /device:TPU:1, one launch (start us, length us, event | category | flops | bytes accessed | tf_op | source)
XLA Modules:
  0.0 96.0 jit_solution(592784003796568067)
XLA Ops:
  0.6 6.4 %gather_rows.1 = (f32[4096,128]{1,0:T(8,128)}, s32[32,128]{1,0:T(8,128)S(4)}) custom-call(s32[32,128]{1,0:T(8,128)} %bitcast.52, f32[8192,128]{1,0:T(8,128)} %bitcast.48), custom_call_target="tpu_custom_call" | custom-call | tf_op jit(solution)/shard_map/gather_rows/pallas_call | solution.py:113
  7.1 11.5 %all-to-all-start = ((f32[128,32,128]{2,1,0:T(8,128)}), f32[128,32,128]{2,1,0:T(8,128)S(1)}, u32[]{:S(2)}, u32[]{:S(2)}) async-start(f32[128,32,128]{2,1,0:T(8,128)} %bitcast.50), calls=%async_computation | async-start | bytes 4194304 | tf_op jit(solution)/shard_map/all_to_all | solution.py:583
  18.6 0.0 copy-start
  18.6 0.0 copy-start.1
  18.6 0.0 copy-start.2
  18.6 0.0 copy-start.3
  18.6 13.0 %sweep_first.1 = (f32[8192,128]{1,0:T(8,128)}, f32[8192,128]{1,0:T(8,128)}, f32[512,128]{1,0:T(8,128)}, f32[512,128]{1,0:T(8,128)}, f32[512,128]{1,0:T(8,128)}, /*index=5*/f32[512,128]{1,0:T(8,128)}) custom-call(f32[4096,128]{1,0:T(8,128)} %get-tuple-element.26.after, f32[8192,128]{1,0:T(8,128)} %bitcast.49, f32[8192,128]{1,0:T(8,128)} %bitcast.43, ...), custom_call_target="tpu_custom_call" | custom-call | tf_op jit(solution)/shard_map/sweep_first/pallas_call | solution.py:320
  31.6 3.4 %collective-permute-start = (f32[512,128]{1,0:T(8,128)}, f32[512,128]{1,0:T(8,128)S(1)}, u32[]{:S(2)}, u32[]{:S(2)}) collective-permute-start(f32[512,128]{1,0:T(8,128)} %get-tuple-element.27.sx1), channel_id=1, source_target_pairs={{0,32},{32,64},{64,96},{1,33},{33,65},{65,97},{2,34},{34,66},{66,9... | collective-permute-start | bytes 786440 | tf_op jit(solution)/shard_map/ppermute | solution.py:566
  35.0 1.3 %collective-permute-start.1 = (f32[512,128]{1,0:T(8,128)}, f32[512,128]{1,0:T(8,128)S(1)}, u32[]{:S(2)}, u32[]{:S(2)}) collective-permute-start(f32[512,128]{1,0:T(8,128)} %get-tuple-element.28.sx0), channel_id=1, source_target_pairs={{32,0},{64,32},{96,64},{33,1},{65,33},{97,65},{34,2},{66,34},{98,6... | collective-permute-start | bytes 786440 | tf_op jit(solution)/shard_map/ppermute | solution.py:571
  36.3 3.7 %collective-permute-start.2 = (f32[512,128]{1,0:T(8,128)}, f32[512,128]{1,0:T(8,128)S(1)}, u32[]{:S(2)}, u32[]{:S(2)}) collective-permute-start(f32[512,128]{1,0:T(8,128)} %get-tuple-element.29.sy1), channel_id=1, source_target_pairs={{0,1},{1,2},{2,3},{3,4},{4,5},{5,6},{6,7},{7,8},{8,9},{9,10},{10,1... | collective-permute-start | bytes 786440 | tf_op jit(solution)/shard_map/ppermute | solution.py:566
  40.0 1.9 %collective-permute-start.3 = (f32[512,128]{1,0:T(8,128)}, f32[512,128]{1,0:T(8,128)S(1)}, u32[]{:S(2)}, u32[]{:S(2)}) collective-permute-start(f32[512,128]{1,0:T(8,128)} %get-tuple-element.30.sy0), channel_id=1, source_target_pairs={{1,0},{2,1},{3,2},{4,3},{5,4},{6,5},{7,6},{8,7},{9,8},{10,9},{11,1... | collective-permute-start | bytes 786440 | tf_op jit(solution)/shard_map/ppermute | solution.py:571
  42.0 7.1 %all-to-all-done = f32[128,32,128]{2,1,0:T(8,128)S(1)} async-done(((f32[128,32,128]{2,1,0:T(8,128)}), f32[128,32,128]{2,1,0:T(8,128)S(1)}, u32[]{:S(2)}, u32[]{:S(2)}) %all-to-all-start) | async-done | bytes 2097184 | tf_op jit(solution)/shard_map/all_to_all | solution.py:583
  49.1 0.0 copy-done
  49.1 0.0 copy-done.1
  49.1 0.0 copy-done.2
  49.1 0.0 copy-done.3
  49.1 4.4 %channel_march.1 = (f32[32,128,128]{2,1,0:T(8,128)}, f32[8,512,128]{2,1,0:T(8,128)}) custom-call(f32[8192,128]{1,0:T(8,128)} %get-tuple-element.31.refs_0_.u, s32[1]{0:T(128)} %bitcast.12.refs_1_, s32[128,128]{1,0:T(8,128)S(1)} %bitcast.38, f32[8,512,128]{2,1,0:T(8,128)S(1)} %bitcast.36, f32[16,128,128]{2,1,0:T(8,128)} %refs_4_.1, f32[16,128]{1,0:T(8,128)S(1)} %copy-done.1, ...), custom_call_target="tpu_custom_call" | custom-call | tf_op jit(solution)/shard_map/channel_march/pallas_call | solution.py:548
  53.6 0.0 collective-permute-done.refs_0_.xlo
  53.6 0.0 collective-permute-done.1.refs_1_.xhi
  53.6 0.0 collective-permute-done.2.refs_2_.ylo
  53.6 0.0 collective-permute-done.3.refs_3_.yhi
  53.6 6.0 %all-to-all-start.1 = ((f32[128,32,128]{2,1,0:T(8,128)}), f32[128,32,128]{2,1,0:T(8,128)S(1)}, u32[]{:S(2)}, u32[]{:S(2)}) async-start(f32[128,32,128]{2,1,0:T(8,128)} %bitcast.42), calls=%async_computation.1 | async-start | bytes 4194304 | tf_op jit(solution)/shard_map/all_to_all | solution.py:591
  59.6 2.7 %sweep_first_sides.1 = (f32[256,128]{1,0:T(8,128)}, f32[256,128]{1,0:T(8,128)}, f32[256,128]{1,0:T(8,128)}, f32[256,128]{1,0:T(8,128)}, f32[256,128]{1,0:T(8,128...) custom-call(f32[8,512,128]{2,1,0:T(8,128)} %tie.1.after, f32[32,256,128]{2,1,0:T(8,128)} %bitcast.41, ...), custom_call_target="tpu_custom_call" | custom-call | tf_op jit(solution)/shard_map/sweep_first_sides/pallas_call | solution.py:373
  62.4 1.3 %collective-permute-start.5 = (f32[256,128]{1,0:T(8,128)}, f32[256,128]{1,0:T(8,128)S(1)}, u32[]{:S(2)}, u32[]{:S(2)}) collective-permute-start(f32[256,128]{1,0:T(8,128)} %get-tuple-element.34.fx0), channel_id=1, source_target_pairs={{32,0},{64,32},{96,64},{33,1},{65,33},{97,65},{34,2},{66,34},{98,6... | collective-permute-start | bytes 393224 | tf_op jit(solution)/shard_map/ppermute | solution.py:571
  63.7 4.0 %collective-permute-start.4 = (f32[256,128]{1,0:T(8,128)}, f32[256,128]{1,0:T(8,128)S(1)}, u32[]{:S(2)}, u32[]{:S(2)}) collective-permute-start(f32[256,128]{1,0:T(8,128)} %get-tuple-element.35.fx1), channel_id=1, source_target_pairs={{0,32},{32,64},{64,96},{1,33},{33,65},{65,97},{2,34},{34,66},{66,9... | collective-permute-start | bytes 393224 | tf_op jit(solution)/shard_map/ppermute | solution.py:566
  67.7 3.5 %collective-permute-start.7 = (f32[256,128]{1,0:T(8,128)}, f32[256,128]{1,0:T(8,128)S(1)}, u32[]{:S(2)}, u32[]{:S(2)}) collective-permute-start(f32[256,128]{1,0:T(8,128)} %get-tuple-element.36.fy0), channel_id=1, source_target_pairs={{1,0},{2,1},{3,2},{4,3},{5,4},{6,5},{7,6},{8,7},{9,8},{10,9},{11,1... | collective-permute-start | bytes 393224 | tf_op jit(solution)/shard_map/ppermute | solution.py:571
  71.2 2.5 %collective-permute-start.6 = (f32[256,128]{1,0:T(8,128)}, f32[256,128]{1,0:T(8,128)S(1)}, u32[]{:S(2)}, u32[]{:S(2)}) collective-permute-start(f32[256,128]{1,0:T(8,128)} %get-tuple-element.37.fy1), channel_id=1, source_target_pairs={{0,1},{1,2},{2,3},{3,4},{4,5},{5,6},{6,7},{7,8},{8,9},{9,10},{10,1... | collective-permute-start | bytes 393224 | tf_op jit(solution)/shard_map/ppermute | solution.py:566
  73.7 13.2 %sweep_second.1 = (f32[8192,128]{1,0:T(8,128)}, f32[256,128]{1,0:T(8,128)}, f32[256,128]{1,0:T(8,128)}, f32[256,128]{1,0:T(8,128)}, f32[256,128]{1,0:T(8,128)}) custom-call(f32[8,512,128]{2,1,0:T(8,128)} %tie.1.after, f32[8192,128]{1,0:T(8,128)} %get-tuple-element.31.refs_0_.u, f32[8192,128]{1,0:T(8,128)} %bitcast.44, f32[8192,128]{1,0:T(8,128)} %bitcast.46, ...), custom_call_target="tpu_custom_call" | custom-call | tf_op jit(solution)/shard_map/sweep_second/pallas_call | solution.py:464
  86.9 0.0 collective-permute-done.5.xhi
  87.0 0.0 copy-start.4
  87.0 0.0 collective-permute-done.4.xlo
  87.0 0.0 copy-start.5
  87.0 0.0 collective-permute-done.7.yhi
  87.0 0.0 copy-start.6
  87.0 0.0 collective-permute-done.6.ylo
  87.0 0.0 copy-start.7
  87.0 2.8 %all-to-all-done.1 = f32[128,32,128]{2,1,0:T(8,128)S(1)} async-done(((f32[128,32,128]{2,1,0:T(8,128)}), f32[128,32,128]{2,1,0:T(8,128)S(1)}, u32[]{:S(2)}, u32[]{:S(2)}) %all-to-all-start.1) | async-done | bytes 2097184 | tf_op jit(solution)/shard_map/all_to_all | solution.py:591
  89.9 0.0 copy-done.4
  89.9 0.0 copy-done.5
  89.9 0.0 copy-done.6
  89.9 0.0 copy-done.7
  89.9 6.1 %subtract_rows.1 = f32[8192,128]{1,0:T(8,128)} custom-call(s32[32,128]{1,0:T(8,128)S(4)} %get-tuple-element.25.at, f32[4096,128]{1,0:T(8,128)S(1)} %bitcast.37, f32[8192,128]{1,0:T(8,128)} %get-tuple-element.42.src, f32[256,128]{1,0:T(8,128)} %get-tuple-element.43.kx0, f32[256,128]{1,0:T(8,128)} %get-tuple-element.44.kx1, f32[256,128]{1,0:T(8,128)} %get-tuple-element.45.ky0, ...), custom_call_target="tpu_custom_call" | custom-call | tf_op jit(solution)/shard_map/subtract_rows/pallas_call | solution.py:173
  (1 shorter events, 0.0 us)
Async XLA Ops:
  7.1 42.0 %all-to-all-start = ((f32[128,32,128]{2,1,0:T(8,128)}), f32[128,32,128]{2,1,0:T(8,128)S(1)}, u32[]{:S(2)}, u32[]{:S(2)}) async-start(f32[128,32,128]{2,1,0:T(8,128)} %bitcast.50), calls=%async_computation | async-start | bytes 4194304 | tf_op jit(solution)/shard_map/all_to_all | solution.py:583
  18.6 30.5 %copy-start = (s32[16384]{0:T(1024)S(1)}, s32[16384]{0:T(1024)}, u32[]{:S(2)}) copy-start(s32[16384]{0:T(1024)} %param.12) | copy-start | bytes 196612
  18.6 30.5 %copy-start.1 = (f32[16,128]{1,0:T(8,128)S(1)}, f32[16,128]{1,0:T(8,128)}, u32[]{:S(2)}) copy-start(f32[16,128]{1,0:T(8,128)} %refs_5_.1) | copy-start | bytes 24580
  18.6 30.5 %copy-start.2 = (f32[256]{0:T(256)S(1)}, f32[256]{0:T(256)}, u32[]{:S(2)}) copy-start(f32[256]{0:T(256)} %param.16) | copy-start | bytes 3076
  18.6 30.5 %copy-start.3 = (f32[256]{0:T(256)S(1)}, f32[256]{0:T(256)}, u32[]{:S(2)}) copy-start(f32[256]{0:T(256)} %param.17) | copy-start | bytes 3076
  31.6 22.0 %collective-permute-start = (f32[512,128]{1,0:T(8,128)}, f32[512,128]{1,0:T(8,128)S(1)}, u32[]{:S(2)}, u32[]{:S(2)}) collective-permute-start(f32[512,128]{1,0:T(8,128)} %get-tuple-element.27.sx1), channel_id=1, source_target_pairs={{0,32},{32,64},{64,96},{1,33},{33,65},{65,97},{2,34},{34,66},{66,9... | collective-permute-start | bytes 786440 | tf_op jit(solution)/shard_map/ppermute | solution.py:566
  35.0 18.5 %collective-permute-start.1 = (f32[512,128]{1,0:T(8,128)}, f32[512,128]{1,0:T(8,128)S(1)}, u32[]{:S(2)}, u32[]{:S(2)}) collective-permute-start(f32[512,128]{1,0:T(8,128)} %get-tuple-element.28.sx0), channel_id=1, source_target_pairs={{32,0},{64,32},{96,64},{33,1},{65,33},{97,65},{34,2},{66,34},{98,6... | collective-permute-start | bytes 786440 | tf_op jit(solution)/shard_map/ppermute | solution.py:571
  36.3 17.2 %collective-permute-start.2 = (f32[512,128]{1,0:T(8,128)}, f32[512,128]{1,0:T(8,128)S(1)}, u32[]{:S(2)}, u32[]{:S(2)}) collective-permute-start(f32[512,128]{1,0:T(8,128)} %get-tuple-element.29.sy1), channel_id=1, source_target_pairs={{0,1},{1,2},{2,3},{3,4},{4,5},{5,6},{6,7},{7,8},{8,9},{9,10},{10,1... | collective-permute-start | bytes 786440 | tf_op jit(solution)/shard_map/ppermute | solution.py:566
  40.0 13.6 %collective-permute-start.3 = (f32[512,128]{1,0:T(8,128)}, f32[512,128]{1,0:T(8,128)S(1)}, u32[]{:S(2)}, u32[]{:S(2)}) collective-permute-start(f32[512,128]{1,0:T(8,128)} %get-tuple-element.30.sy0), channel_id=1, source_target_pairs={{1,0},{2,1},{3,2},{4,3},{5,4},{6,5},{7,6},{8,7},{9,8},{10,9},{11,1... | collective-permute-start | bytes 786440 | tf_op jit(solution)/shard_map/ppermute | solution.py:571
  53.6 36.3 %all-to-all-start.1 = ((f32[128,32,128]{2,1,0:T(8,128)}), f32[128,32,128]{2,1,0:T(8,128)S(1)}, u32[]{:S(2)}, u32[]{:S(2)}) async-start(f32[128,32,128]{2,1,0:T(8,128)} %bitcast.42), calls=%async_computation.1 | async-start | bytes 4194304 | tf_op jit(solution)/shard_map/all_to_all | solution.py:591
  62.4 24.6 %collective-permute-start.5 = (f32[256,128]{1,0:T(8,128)}, f32[256,128]{1,0:T(8,128)S(1)}, u32[]{:S(2)}, u32[]{:S(2)}) collective-permute-start(f32[256,128]{1,0:T(8,128)} %get-tuple-element.34.fx0), channel_id=1, source_target_pairs={{32,0},{64,32},{96,64},{33,1},{65,33},{97,65},{34,2},{66,34},{98,6... | collective-permute-start | bytes 393224 | tf_op jit(solution)/shard_map/ppermute | solution.py:571
  63.7 23.3 %collective-permute-start.4 = (f32[256,128]{1,0:T(8,128)}, f32[256,128]{1,0:T(8,128)S(1)}, u32[]{:S(2)}, u32[]{:S(2)}) collective-permute-start(f32[256,128]{1,0:T(8,128)} %get-tuple-element.35.fx1), channel_id=1, source_target_pairs={{0,32},{32,64},{64,96},{1,33},{33,65},{65,97},{2,34},{34,66},{66,9... | collective-permute-start | bytes 393224 | tf_op jit(solution)/shard_map/ppermute | solution.py:566
  67.7 19.3 %collective-permute-start.7 = (f32[256,128]{1,0:T(8,128)}, f32[256,128]{1,0:T(8,128)S(1)}, u32[]{:S(2)}, u32[]{:S(2)}) collective-permute-start(f32[256,128]{1,0:T(8,128)} %get-tuple-element.36.fy0), channel_id=1, source_target_pairs={{1,0},{2,1},{3,2},{4,3},{5,4},{6,5},{7,6},{8,7},{9,8},{10,9},{11,1... | collective-permute-start | bytes 393224 | tf_op jit(solution)/shard_map/ppermute | solution.py:571
  71.2 15.8 %collective-permute-start.6 = (f32[256,128]{1,0:T(8,128)}, f32[256,128]{1,0:T(8,128)S(1)}, u32[]{:S(2)}, u32[]{:S(2)}) collective-permute-start(f32[256,128]{1,0:T(8,128)} %get-tuple-element.37.fy1), channel_id=1, source_target_pairs={{0,1},{1,2},{2,3},{3,4},{4,5},{5,6},{6,7},{7,8},{8,9},{9,10},{10,1... | collective-permute-start | bytes 393224 | tf_op jit(solution)/shard_map/ppermute | solution.py:566
  87.0 2.9 %copy-start.4 = (f32[256,128]{1,0:T(8,128)}, f32[256,128]{1,0:T(8,128)S(1)}, u32[]{:S(2)}) copy-start(f32[256,128]{1,0:T(8,128)S(1)} %collective-permute-done.5.xhi) | copy-start | bytes 393220
  87.0 2.9 %copy-start.5 = (f32[256,128]{1,0:T(8,128)}, f32[256,128]{1,0:T(8,128)S(1)}, u32[]{:S(2)}) copy-start(f32[256,128]{1,0:T(8,128)S(1)} %collective-permute-done.4.xlo) | copy-start | bytes 393220
  87.0 2.9 %copy-start.6 = (f32[256,128]{1,0:T(8,128)}, f32[256,128]{1,0:T(8,128)S(1)}, u32[]{:S(2)}) copy-start(f32[256,128]{1,0:T(8,128)S(1)} %collective-permute-done.7.yhi) | copy-start | bytes 393220
  87.0 2.9 %copy-start.7 = (f32[256,128]{1,0:T(8,128)}, f32[256,128]{1,0:T(8,128)S(1)}, u32[]{:S(2)}) copy-start(f32[256,128]{1,0:T(8,128)S(1)} %collective-permute-done.6.ylo) | copy-start | bytes 393220

commit v6 on v5

--- a/solution.py
+++ b/solution.py
@@ -8,6 +8,7 @@
 from jax.sharding import PartitionSpec as P
 
 F32 = jnp.float32
+GY = ("pair", "core")
 VM = pl.BlockSpec(memory_space=pltpu.VMEM)
 SM = pl.BlockSpec(memory_space=pltpu.SMEM)
 ANY = pl.BlockSpec(memory_space=pl.ANY)
@@ -69,6 +70,19 @@
     return ref.at[pl.ds(aligned(k * (ROWS // parts) + shift, 8), ROWS // parts)]
 
 
+def order_by_core(lists):
+    half = lists.shape[0] // 2
+    even, odd = lists[pl.ds(0, half, stride=2), :], lists[pl.ds(1, half, stride=2), :]
+    lane = lax.broadcasted_iota(jnp.int32, (half, 128), 1)
+
+    def four(*parts):
+        return jnp.where(lane < 32, parts[0], jnp.where(lane < 64, parts[1], jnp.where(lane < 96, parts[2], parts[3])))
+
+    turned = lambda a, n: pltpu.roll(a, n, 1)
+    lists[pl.ds(0, half), :] = four(even, turned(even, 96), turned(odd, 64), turned(odd, 32))
+    lists[pl.ds(half, half), :] = four(turned(even, 96), turned(even, 64), turned(odd, 32), odd)
+
+
 def gather_kernel(rows, src, out, at, block, made, at_v, sems, done):
     loads = [pltpu.make_async_copy(piece(src, k), piece(block, k), sems.at[k]) for k in range(PARTS)]
     asked = pltpu.make_async_copy(rows, at_v, sems.at[PARTS])
@@ -77,6 +91,7 @@
         load.start()
     asked.wait()
     at_v[...] = place_in_tiles(at_v[...])
+    order_by_core(at_v)
     listed = pltpu.make_async_copy(at_v, at, sems.at[PARTS])
     listed.start()
     listed.wait()
@@ -475,8 +490,8 @@
 def channel_kernel(*refs):
     (me, owners, arrived, props, carry, coef_at, inlet_at, fluid_out, flux_out,
      fluids, fluxes, weights, prev, coef, live, done_x, done_f, here_p) = refs[-18:]
-    spans, groups = props.shape[0], arrived.shape[0]
-    size = arrived.shape[1] // spans
+    spans, groups = props.shape[0], arrived.shape[0] // 2
+    size = arrived.shape[1] // groups
     here = me[0]
     halves = [pltpu.make_async_copy(props.at[part], weights.at[part], here_p.at[n])
               for n, part in enumerate((pl.ds(0, spans // 2), pl.ds(spans // 2, spans // 2)))]
@@ -488,10 +503,13 @@
     dot = functools.partial(jnp.dot, preferred_element_type=F32)
 
     def block(s):
-        return pl.ds(aligned(lax.rem(here + s, spans) * size, size), size)
+        return pl.ds(aligned(lax.rem(lax.div(here + s, 2), groups) * size, size), size)
+
+    def core(s):
+        return lax.rem(here + s, 2) * groups
 
     def save_flux(s):
-        return pltpu.make_async_copy(fluxes.at[:, block(s), :], flux_out.at[:, block(s), :], done_x.at[s])
+        return pltpu.make_async_copy(fluxes.at[pl.ds(core(s), groups), block(s), :], flux_out.at[pl.ds(core(s), groups), block(s), :], done_x.at[s])
 
     def save_fluid(n):
         part = pl.ds(n * 4 * groups, 4 * groups)
@@ -513,7 +531,7 @@
         if s % (spans // 2) == 0:
             halves[s // (spans // 2)].wait()
         turn = lax.div(here + s, spans)
-        at = [(lax.rem(turn + q, groups), block(s)) for q in range(groups)]
+        at = [(core(s) + lax.rem(turn + q, groups), block(s)) for q in range(groups)]
         wall = jnp.concatenate([arrived[g, r, :] for g, r in at], axis=0)
         scale = coef[...]
         x = scale * wall
@@ -544,19 +562,19 @@
     spans = props.shape[0]
     groups = 8
     size = coef.shape[0] // groups
-    rows = spans * size
+    rows = groups * size
     fluid, flux = pl.pallas_call(
         channel_kernel,
         out_shape=(jax.ShapeDtypeStruct((size, spans * groups, 128), F32),
-                   pltpu.HBM((groups, rows, 128), F32)),
+                   pltpu.HBM((2 * groups, rows, 128), F32)),
         in_specs=[ANY] * len(after) + [SM] + [VM] * 2 + [ANY] + [VM] * 3, out_specs=(ANY, ANY),
-        scratch_shapes=[pltpu.VMEM((size, (spans + 1) * groups, 128), F32), pltpu.VMEM((groups, rows, 128), F32),
+        scratch_shapes=[pltpu.VMEM((size, (spans + 1) * groups, 128), F32), pltpu.VMEM((2 * groups, rows, 128), F32),
                         pltpu.VMEM(props.shape, F32)]
         + [pltpu.VMEM((groups * size, 128), F32)] * 3
         + [pltpu.SemaphoreType.DMA((spans,)), pltpu.SemaphoreType.DMA((spans // 4,)),
            pltpu.SemaphoreType.DMA((2,))],
         compiler_params=SMALL, name="channel_march",
-    )(*in_hbm(*after), me, owners, arrived.reshape(groups, rows, 128), *in_hbm(props), carry,
+    )(*in_hbm(*after), me, owners, arrived.reshape(2 * groups, rows, 128), *in_hbm(props), carry,
       coef.reshape(2, 128), inlet.reshape(2, 128))
     return fluid.reshape(-1, 128), flux
 
@@ -573,34 +591,36 @@
 
 def local(solid_temp, conduct, power, channel_owner, wall_rows, span_prop, span_carry,
           channel_coef, channel_inlet):
-    both = ("gx", "gy")
+    both = ("gx", *GY)
+    by_core = ("core", "gx", "pair")
     devices = lax.axis_size(both)
     me = lax.axis_index(both).astype(jnp.int32).reshape(1)
     slots = channel_coef.shape[0]
     u, c, p = tiles(solid_temp), tiles(conduct), tiles(power)
 
     sent, at = gather(wall_rows.reshape(-1, 128), u)
-    arrived = lax.all_to_all(sent.reshape(devices, -1, 128), both, 0, 0, tiled=True)
+    arrived = lax.all_to_all(sent.reshape(devices, -1, 128), by_core, 0, 0, tiled=True)
 
     once, gain, *sides = sweep_first(sent, u, c, p)
-    halos = (up(sides[1], "gx"), down(sides[0], "gx"), up(sides[3], "gy"), down(sides[2], "gy"))
+    halos = (up(sides[1], "gx"), down(sides[0], "gx"), up(sides[3], GY), down(sides[2], GY))
 
     fluid, flux = channel((once,), me, channel_owner.reshape(-1, 128), arrived, span_prop, span_carry,
                           channel_coef, channel_inlet)
     flux = after_all(flux, halos)
-    returned = lax.all_to_all(flux.reshape(devices, -1, 128), both, 0, 0, tiled=True)
+    returned = lax.all_to_all(flux.reshape(devices, -1, 128), by_core, 0, 0, tiled=True)
 
     faces = fix_sides(flux, once, gain, sides, halos)
     faces, beyond = faces[:4], faces[4:]
-    outer = (up(faces[1], "gx"), down(faces[0], "gx"), up(faces[3], "gy"), down(faces[2], "gy"))
+    outer = (up(faces[1], "gx"), down(faces[0], "gx"), up(faces[3], GY), down(faces[2], GY))
     twice, *gains = sweep_second(flux, once, c, p, gain, faces, beyond)
     solid_out = finish(at, returned.reshape(-1, 128), twice, gains, outer)
     return untiles(solid_out, *solid_temp.shape), untiles(fluid, 1, slots, span_carry.shape[0] * 128)[0]
 
 
 def solution(mesh):
-    both = ("gx", "gy")
-    placed = (P("gx", "gy", None),) * 3 + (P(),) + (P(both),) + (
+    split = jax.sharding.Mesh(mesh.devices.reshape(mesh.shape["gx"], -1, 2), ("gx", *GY))
+    both = ("gx", *GY)
+    placed = (P("gx", GY, None),) * 3 + (P(),) + (P(both),) + (
         P(both, None, None), P(both, None), P(both), P(both))
-    return jax.shard_map(local, mesh=mesh, in_specs=placed,
-                         out_specs=(P("gx", "gy", None), P(both, None)), check_vma=False)
+    return jax.shard_map(local, mesh=split, in_specs=placed,
+                         out_specs=(P("gx", GY, None), P(both, None)), check_vma=False)

time: 96.6 us -> 96.2 us (level); the launches traced: 96 us -> 94.4 us
  waiting for transfers between devices: 9.98 us -> 6.35 us
  starting transfers between devices: 39.2 us -> 41.1 us
    all_to_all x2, waiting for transfers between devices: 9.95 us -> 6.33 us  [the longest x1 5.15 us: local(): lax.all_to_all(sent.reshape(devices, -1, 128), by_core, 0, 0, tiled=True)]
    all_to_all x2, starting transfers between devices: 17.5 us -> 19.5 us  [the longest x1 11.5 us: local(): lax.all_to_all(sent.reshape(devices, -1, 128), by_core, 0, 0, tiled=True)]
where the time goes in v6:
time: 96.2 us; the launch traced here: 94.4 us
  Pallas kernels  45.9 us (48%)
  starting transfers between devices  41.1 us (43%)
  waiting for transfers between devices  6.35 us (7%)
    ppermute x4, starting transfers between devices, up(): return lax.ppermute(a, axis, [(i, i + 1) for i in range(n - 1)])  13.6 us
    pallas_call x1, Pallas kernels, sweep_second(): pl.pallas_call(second_kernel, out_shape=(shape(ROWS),) + (shape(PLANE),)...  13.2 us
    pallas_call x1, Pallas kernels, sweep_first(): pl.pallas_call(first_kernel, out_shape=(shape(ROWS),) * 2 + (shape(2 * PL...  13 us
    all_to_all x1, starting transfers between devices, local(): lax.all_to_all(sent.reshape(devices, -1, 128), by_core, 0, 0, tiled=True)  11.5 us
    all_to_all x1, starting transfers between devices, local(): lax.all_to_all(flux.reshape(devices, -1, 128), by_core, 0, 0, tiled=True)  8 us
    ppermute x4, starting transfers between devices, down(): return lax.ppermute(a, axis, [(i + 1, i) for i in range(n - 1)])  7.99 us
    pallas_call x1, Pallas kernels, gather(): pl.pallas_call(gather_kernel, out_shape=(shape(n), pltpu.SMEM(rows.shape,...  6.42 us
    pallas_call x1, Pallas kernels, finish(): pl.pallas_call(finish_kernel, out_shape=shape(ROWS), in_specs=[SM, VM] +...  6.13 us
  transfers between devices with their start and end apart: 10, of which 2 were waited for; matrix products, arithmetic and copies ran while one was open for 0% of the time, Pallas kernels for 35%

profile of v6, /device:TPU:1, one launch (start us, length us, event | category | flops | bytes accessed | tf_op | source)
XLA Modules:
  0.0 94.4 jit_solution(9315326550885360215)
XLA Ops:
  0.6 6.4 %gather_rows.1 = (f32[4096,128]{1,0:T(8,128)}, s32[32,128]{1,0:T(8,128)S(4)}) custom-call(s32[32,128]{1,0:T(8,128)} %bitcast.52, f32[8192,128]{1,0:T(8,128)} %bitcast.48), custom_call_target="tpu_custom_call" | custom-call | tf_op jit(solution)/shard_map/gather_rows/pallas_call | solution.py:128
  7.1 11.5 %all-to-all-start = ((f32[128,32,128]{2,1,0:T(8,128)}), f32[128,32,128]{2,1,0:T(8,128)S(1)}, u32[]{:S(2)}, u32[]{:S(2)}) async-start(f32[128,32,128]{2,1,0:T(8,128)} %bitcast.50), calls=%async_computation | async-start | bytes 4194304 | tf_op jit(solution)/shard_map/all_to_all | solution.py:602
  18.6 0.0 copy-start
  18.6 0.0 copy-start.1
  18.6 0.0 copy-start.2
  18.6 0.0 copy-start.3
  18.6 13.0 %sweep_first.1 = (f32[8192,128]{1,0:T(8,128)}, f32[8192,128]{1,0:T(8,128)}, f32[512,128]{1,0:T(8,128)}, f32[512,128]{1,0:T(8,128)}, f32[512,128]{1,0:T(8,128)}, /*index=5*/f32[512,128]{1,0:T(8,128)}) custom-call(f32[4096,128]{1,0:T(8,128)} %get-tuple-element.26.after, f32[8192,128]{1,0:T(8,128)} %bitcast.49, f32[8192,128]{1,0:T(8,128)} %bitcast.43, ...), custom_call_target="tpu_custom_call" | custom-call | tf_op jit(solution)/shard_map/sweep_first/pallas_call | solution.py:335
  31.6 3.4 %collective-permute-start = (f32[512,128]{1,0:T(8,128)}, f32[512,128]{1,0:T(8,128)S(1)}, u32[]{:S(2)}, u32[]{:S(2)}) collective-permute-start(f32[512,128]{1,0:T(8,128)} %get-tuple-element.27.sx1), channel_id=1, source_target_pairs={{0,32},{32,64},{64,96},{1,33},{33,65},{65,97},{2,34},{34,66},{66,9... | collective-permute-start | bytes 786440 | tf_op jit(solution)/shard_map/ppermute | solution.py:584
  35.0 1.3 %collective-permute-start.1 = (f32[512,128]{1,0:T(8,128)}, f32[512,128]{1,0:T(8,128)S(1)}, u32[]{:S(2)}, u32[]{:S(2)}) collective-permute-start(f32[512,128]{1,0:T(8,128)} %get-tuple-element.28.sx0), channel_id=1, source_target_pairs={{32,0},{64,32},{96,64},{33,1},{65,33},{97,65},{34,2},{66,34},{98,6... | collective-permute-start | bytes 786440 | tf_op jit(solution)/shard_map/ppermute | solution.py:589
  36.3 3.7 %collective-permute-start.2 = (f32[512,128]{1,0:T(8,128)}, f32[512,128]{1,0:T(8,128)S(1)}, u32[]{:S(2)}, u32[]{:S(2)}) collective-permute-start(f32[512,128]{1,0:T(8,128)} %get-tuple-element.29.sy1), channel_id=1, source_target_pairs={{0,1},{1,2},{2,3},{3,4},{4,5},{5,6},{6,7},{7,8},{8,9},{9,10},{10,1... | collective-permute-start | bytes 786440 | tf_op jit(solution)/shard_map/ppermute | solution.py:584
  40.0 1.9 %collective-permute-start.3 = (f32[512,128]{1,0:T(8,128)}, f32[512,128]{1,0:T(8,128)S(1)}, u32[]{:S(2)}, u32[]{:S(2)}) collective-permute-start(f32[512,128]{1,0:T(8,128)} %get-tuple-element.30.sy0), channel_id=1, source_target_pairs={{1,0},{2,1},{3,2},{4,3},{5,4},{6,5},{7,6},{8,7},{9,8},{10,9},{11,1... | collective-permute-start | bytes 786440 | tf_op jit(solution)/shard_map/ppermute | solution.py:589
  42.0 5.2 %all-to-all-done = f32[128,32,128]{2,1,0:T(8,128)S(1)} async-done(((f32[128,32,128]{2,1,0:T(8,128)}), f32[128,32,128]{2,1,0:T(8,128)S(1)}, u32[]{:S(2)}, u32[]{:S(2)}) %all-to-all-start) | async-done | bytes 2097184 | tf_op jit(solution)/shard_map/all_to_all | solution.py:602
  47.1 0.0 copy-done
  47.1 0.0 copy-done.1
  47.1 0.0 copy-done.2
  47.1 0.0 copy-done.3
  47.1 4.4 %channel_march.1 = (f32[32,128,128]{2,1,0:T(8,128)}, f32[16,256,128]{2,1,0:T(8,128)}) custom-call(f32[8192,128]{1,0:T(8,128)} %get-tuple-element.31.refs_0_.u, s32[1]{0:T(128)} %bitcast.12.refs_1_, s32[128,128]{1,0:T(8,128)S(1)} %bitcast.38, f32[16,256,128]{2,1,0:T(8,128)S(1)} %bitcast.36, f32[16,128,128]{2,1,0:T(8,128)} %refs_4_.1, ...), custom_call_target="tpu_custom_call" | custom-call | tf_op jit(solution)/shard_map/channel_march/pallas_call | solution.py:566
  51.6 0.0 collective-permute-done.refs_0_.xlo
  51.6 0.0 collective-permute-done.1.refs_1_.xhi
  51.6 0.0 collective-permute-done.2.refs_2_.ylo
  51.6 0.0 collective-permute-done.3.refs_3_.yhi
  51.6 8.0 %all-to-all-start.1 = ((f32[128,32,128]{2,1,0:T(8,128)}), f32[128,32,128]{2,1,0:T(8,128)S(1)}, u32[]{:S(2)}, u32[]{:S(2)}) async-start(f32[128,32,128]{2,1,0:T(8,128)} %bitcast.42), calls=%async_computation.1 | async-start | bytes 4194304 | tf_op jit(solution)/shard_map/all_to_all | solution.py:610
  59.6 2.7 %sweep_first_sides.1 = (f32[256,128]{1,0:T(8,128)}, f32[256,128]{1,0:T(8,128)}, f32[256,128]{1,0:T(8,128)}, f32[256,128]{1,0:T(8,128)}, f32[256,128]{1,0:T(8,128...) custom-call(f32[16,256,128]{2,1,0:T(8,128)} %tie.1.after, f32[32,256,128]{2,1,0:T(8,128)} %bitcast.41, ...), custom_call_target="tpu_custom_call" | custom-call | tf_op jit(solution)/shard_map/sweep_first_sides/pallas_call | solution.py:388
  62.4 1.3 %collective-permute-start.5 = (f32[256,128]{1,0:T(8,128)}, f32[256,128]{1,0:T(8,128)S(1)}, u32[]{:S(2)}, u32[]{:S(2)}) collective-permute-start(f32[256,128]{1,0:T(8,128)} %get-tuple-element.34.fx0), channel_id=1, source_target_pairs={{32,0},{64,32},{96,64},{33,1},{65,33},{97,65},{34,2},{66,34},{98,6... | collective-permute-start | bytes 393224 | tf_op jit(solution)/shard_map/ppermute | solution.py:589
  63.7 4.0 %collective-permute-start.4 = (f32[256,128]{1,0:T(8,128)}, f32[256,128]{1,0:T(8,128)S(1)}, u32[]{:S(2)}, u32[]{:S(2)}) collective-permute-start(f32[256,128]{1,0:T(8,128)} %get-tuple-element.35.fx1), channel_id=1, source_target_pairs={{0,32},{32,64},{64,96},{1,33},{33,65},{65,97},{2,34},{34,66},{66,9... | collective-permute-start | bytes 393224 | tf_op jit(solution)/shard_map/ppermute | solution.py:584
  67.7 3.5 %collective-permute-start.7 = (f32[256,128]{1,0:T(8,128)}, f32[256,128]{1,0:T(8,128)S(1)}, u32[]{:S(2)}, u32[]{:S(2)}) collective-permute-start(f32[256,128]{1,0:T(8,128)} %get-tuple-element.36.fy0), channel_id=1, source_target_pairs={{1,0},{2,1},{3,2},{4,3},{5,4},{6,5},{7,6},{8,7},{9,8},{10,9},{11,1... | collective-permute-start | bytes 393224 | tf_op jit(solution)/shard_map/ppermute | solution.py:589
  71.2 2.5 %collective-permute-start.6 = (f32[256,128]{1,0:T(8,128)}, f32[256,128]{1,0:T(8,128)S(1)}, u32[]{:S(2)}, u32[]{:S(2)}) collective-permute-start(f32[256,128]{1,0:T(8,128)} %get-tuple-element.37.fy1), channel_id=1, source_target_pairs={{0,1},{1,2},{2,3},{3,4},{4,5},{5,6},{6,7},{7,8},{8,9},{9,10},{10,1... | collective-permute-start | bytes 393224 | tf_op jit(solution)/shard_map/ppermute | solution.py:584
  73.7 13.2 %sweep_second.1 = (f32[8192,128]{1,0:T(8,128)}, f32[256,128]{1,0:T(8,128)}, f32[256,128]{1,0:T(8,128)}, f32[256,128]{1,0:T(8,128)}, f32[256,128]{1,0:T(8,128)}) custom-call(f32[16,256,128]{2,1,0:T(8,128)} %tie.1.after, f32[8192,128]{1,0:T(8,128)} %get-tuple-element.31.refs_0_.u, f32[8192,128]{1,0:T(8,128)} %bitcast.44, f32[8192,128]{1,0:T(8,128)} %bitcast.46, ...), custom_call_target="tpu_custom_call" | custom-call | tf_op jit(solution)/shard_map/sweep_second/pallas_call | solution.py:479
  86.9 0.0 collective-permute-done.5.xhi
  87.0 0.0 copy-start.4
  87.0 0.0 collective-permute-done.4.xlo
  87.0 0.0 copy-start.5
  87.0 0.0 collective-permute-done.7.yhi
  87.0 0.0 copy-start.6
  87.0 0.0 collective-permute-done.6.ylo
  87.0 0.0 copy-start.7
  87.0 1.2 %all-to-all-done.1 = f32[128,32,128]{2,1,0:T(8,128)S(1)} async-done(((f32[128,32,128]{2,1,0:T(8,128)}), f32[128,32,128]{2,1,0:T(8,128)S(1)}, u32[]{:S(2)}, u32[]{:S(2)}) %all-to-all-start.1) | async-done | bytes 2097184 | tf_op jit(solution)/shard_map/all_to_all | solution.py:610
  88.2 0.0 copy-done.4
  88.2 0.0 copy-done.5
  88.2 0.0 copy-done.6
  88.2 0.0 copy-done.7
  88.2 6.1 %subtract_rows.1 = f32[8192,128]{1,0:T(8,128)} custom-call(s32[32,128]{1,0:T(8,128)S(4)} %get-tuple-element.25.at, f32[4096,128]{1,0:T(8,128)S(1)} %bitcast.37, f32[8192,128]{1,0:T(8,128)} %get-tuple-element.42.src, f32[256,128]{1,0:T(8,128)} %get-tuple-element.43.kx0, f32[256,128]{1,0:T(8,128)} %get-tuple-element.44.kx1, f32[256,128]{1,0:T(8,128)} %get-tuple-element.45.ky0, ...), custom_call_target="tpu_custom_call" | custom-call | tf_op jit(solution)/shard_map/subtract_rows/pallas_call | solution.py:188
  (1 shorter events, 0.0 us)
Async XLA Ops:
  7.1 40.1 %all-to-all-start = ((f32[128,32,128]{2,1,0:T(8,128)}), f32[128,32,128]{2,1,0:T(8,128)S(1)}, u32[]{:S(2)}, u32[]{:S(2)}) async-start(f32[128,32,128]{2,1,0:T(8,128)} %bitcast.50), calls=%async_computation | async-start | bytes 4194304 | tf_op jit(solution)/shard_map/all_to_all | solution.py:602
  18.6 28.6 %copy-start = (s32[16384]{0:T(1024)S(1)}, s32[16384]{0:T(1024)}, u32[]{:S(2)}) copy-start(s32[16384]{0:T(1024)} %param.12) | copy-start | bytes 196612
  18.6 28.6 %copy-start.1 = (f32[16,128]{1,0:T(8,128)S(1)}, f32[16,128]{1,0:T(8,128)}, u32[]{:S(2)}) copy-start(f32[16,128]{1,0:T(8,128)} %refs_5_.1) | copy-start | bytes 24580
  18.6 28.5 %copy-start.2 = (f32[256]{0:T(256)S(1)}, f32[256]{0:T(256)}, u32[]{:S(2)}) copy-start(f32[256]{0:T(256)} %param.16) | copy-start | bytes 3076
  18.6 28.5 %copy-start.3 = (f32[256]{0:T(256)S(1)}, f32[256]{0:T(256)}, u32[]{:S(2)}) copy-start(f32[256]{0:T(256)} %param.17) | copy-start | bytes 3076
  31.6 20.0 %collective-permute-start = (f32[512,128]{1,0:T(8,128)}, f32[512,128]{1,0:T(8,128)S(1)}, u32[]{:S(2)}, u32[]{:S(2)}) collective-permute-start(f32[512,128]{1,0:T(8,128)} %get-tuple-element.27.sx1), channel_id=1, source_target_pairs={{0,32},{32,64},{64,96},{1,33},{33,65},{65,97},{2,34},{34,66},{66,9... | collective-permute-start | bytes 786440 | tf_op jit(solution)/shard_map/ppermute | solution.py:584
  35.0 16.6 %collective-permute-start.1 = (f32[512,128]{1,0:T(8,128)}, f32[512,128]{1,0:T(8,128)S(1)}, u32[]{:S(2)}, u32[]{:S(2)}) collective-permute-start(f32[512,128]{1,0:T(8,128)} %get-tuple-element.28.sx0), channel_id=1, source_target_pairs={{32,0},{64,32},{96,64},{33,1},{65,33},{97,65},{34,2},{66,34},{98,6... | collective-permute-start | bytes 786440 | tf_op jit(solution)/shard_map/ppermute | solution.py:589
  36.3 15.3 %collective-permute-start.2 = (f32[512,128]{1,0:T(8,128)}, f32[512,128]{1,0:T(8,128)S(1)}, u32[]{:S(2)}, u32[]{:S(2)}) collective-permute-start(f32[512,128]{1,0:T(8,128)} %get-tuple-element.29.sy1), channel_id=1, source_target_pairs={{0,1},{1,2},{2,3},{3,4},{4,5},{5,6},{6,7},{7,8},{8,9},{9,10},{10,1... | collective-permute-start | bytes 786440 | tf_op jit(solution)/shard_map/ppermute | solution.py:584
  40.0 11.6 %collective-permute-start.3 = (f32[512,128]{1,0:T(8,128)}, f32[512,128]{1,0:T(8,128)S(1)}, u32[]{:S(2)}, u32[]{:S(2)}) collective-permute-start(f32[512,128]{1,0:T(8,128)} %get-tuple-element.30.sy0), channel_id=1, source_target_pairs={{1,0},{2,1},{3,2},{4,3},{5,4},{6,5},{7,6},{8,7},{9,8},{10,9},{11,1... | collective-permute-start | bytes 786440 | tf_op jit(solution)/shard_map/ppermute | solution.py:589
  51.6 36.6 %all-to-all-start.1 = ((f32[128,32,128]{2,1,0:T(8,128)}), f32[128,32,128]{2,1,0:T(8,128)S(1)}, u32[]{:S(2)}, u32[]{:S(2)}) async-start(f32[128,32,128]{2,1,0:T(8,128)} %bitcast.42), calls=%async_computation.1 | async-start | bytes 4194304 | tf_op jit(solution)/shard_map/all_to_all | solution.py:610
  62.4 24.6 %collective-permute-start.5 = (f32[256,128]{1,0:T(8,128)}, f32[256,128]{1,0:T(8,128)S(1)}, u32[]{:S(2)}, u32[]{:S(2)}) collective-permute-start(f32[256,128]{1,0:T(8,128)} %get-tuple-element.34.fx0), channel_id=1, source_target_pairs={{32,0},{64,32},{96,64},{33,1},{65,33},{97,65},{34,2},{66,34},{98,6... | collective-permute-start | bytes 393224 | tf_op jit(solution)/shard_map/ppermute | solution.py:589
  63.7 23.3 %collective-permute-start.4 = (f32[256,128]{1,0:T(8,128)}, f32[256,128]{1,0:T(8,128)S(1)}, u32[]{:S(2)}, u32[]{:S(2)}) collective-permute-start(f32[256,128]{1,0:T(8,128)} %get-tuple-element.35.fx1), channel_id=1, source_target_pairs={{0,32},{32,64},{64,96},{1,33},{33,65},{65,97},{2,34},{34,66},{66,9... | collective-permute-start | bytes 393224 | tf_op jit(solution)/shard_map/ppermute | solution.py:584
  67.7 19.3 %collective-permute-start.7 = (f32[256,128]{1,0:T(8,128)}, f32[256,128]{1,0:T(8,128)S(1)}, u32[]{:S(2)}, u32[]{:S(2)}) collective-permute-start(f32[256,128]{1,0:T(8,128)} %get-tuple-element.36.fy0), channel_id=1, source_target_pairs={{1,0},{2,1},{3,2},{4,3},{5,4},{6,5},{7,6},{8,7},{9,8},{10,9},{11,1... | collective-permute-start | bytes 393224 | tf_op jit(solution)/shard_map/ppermute | solution.py:589
  71.2 15.8 %collective-permute-start.6 = (f32[256,128]{1,0:T(8,128)}, f32[256,128]{1,0:T(8,128)S(1)}, u32[]{:S(2)}, u32[]{:S(2)}) collective-permute-start(f32[256,128]{1,0:T(8,128)} %get-tuple-element.37.fy1), channel_id=1, source_target_pairs={{0,1},{1,2},{2,3},{3,4},{4,5},{5,6},{6,7},{7,8},{8,9},{9,10},{10,1... | collective-permute-start | bytes 393224 | tf_op jit(solution)/shard_map/ppermute | solution.py:584
  87.0 1.3 %copy-start.4 = (f32[256,128]{1,0:T(8,128)}, f32[256,128]{1,0:T(8,128)S(1)}, u32[]{:S(2)}) copy-start(f32[256,128]{1,0:T(8,128)S(1)} %collective-permute-done.5.xhi) | copy-start | bytes 393220
  87.0 1.2 %copy-start.5 = (f32[256,128]{1,0:T(8,128)}, f32[256,128]{1,0:T(8,128)S(1)}, u32[]{:S(2)}) copy-start(f32[256,128]{1,0:T(8,128)S(1)} %collective-permute-done.4.xlo) | copy-start | bytes 393220
  87.0 1.2 %copy-start.6 = (f32[256,128]{1,0:T(8,128)}, f32[256,128]{1,0:T(8,128)S(1)}, u32[]{:S(2)}) copy-start(f32[256,128]{1,0:T(8,128)S(1)} %collective-permute-done.7.yhi) | copy-start | bytes 393220
  87.0 1.2 %copy-start.7 = (f32[256,128]{1,0:T(8,128)}, f32[256,128]{1,0:T(8,128)S(1)}, u32[]{:S(2)}) copy-start(f32[256,128]{1,0:T(8,128)S(1)} %collective-permute-done.6.ylo) | copy-start | bytes 393220
